TPU v7x, 512 devices: a whole 4x8x8 slice. The times are simulated.
512 devices in a mesh: row: 32 (over z_hi, x, core), col: 16 (over z_lo, y).
Axes of the slice: x: 4, y: 8, z: 8 (z_hi: 4, z_lo: 2; z = z_hi * 2 + z_lo), core: 2. Of those that a mesh axis runs over, the one named last changes fastest.
Arguments:
- noise: bfloat16 [16384, 2048], P('row', 'col'), may hold values from -10 to 10, as said below
- data: bfloat16 [2048, 16384], P('row', 'col'), may hold values from -10 to 10, as said below
Outputs:
- targets: bfloat16 [2048, 16384], P('col', 'row')
- row_potential: float32 [16384], P('row')
- col_potential: float32 [16384], P('col')
Inputs may be any that keep to these rules, and one draw needn't show every extreme that they name: `noise`: entries of order one. `data`: entries of order one.
All inputs are finite; a program needn't handle non-finite values.
Results may differ from a plain program's by a relative error of at most 0.0049.
Values may be sent and summed in bfloat16 or wider, within the bound.
No kernel may reach another device: no remote copies, remote signals or barrier semaphores. Data moves between devices by JAX's collectives and lax.ppermute only.
A program may use at most 64 MiB of HBM per device.

v0:
```python
import jax
import jax.numpy as jnp
from jax import lax
from jax.sharding import PartitionSpec as P

ITERS = 4


EPS = 0.01


def local(noise, data):
    rows_all = noise.shape[0] * lax.axis_size("row")
    cols_all = data.shape[1] * lax.axis_size("col")
    noise_full = lax.all_gather(noise, "col", axis=1, tiled=True)
    noise_sq = jnp.sum(noise_full.astype(jnp.float32) ** 2, axis=1)
    data_full = lax.all_gather(data, "row", axis=0, tiled=True)
    data_sq = jnp.sum(data_full.astype(jnp.float32) ** 2, axis=0)
    cross = jnp.dot(noise_full, data_full, preferred_element_type=jnp.float32)
    cost = (noise_sq[:, None] + data_sq[None, :] - 2.0 * cross) / noise_full.shape[1]
    col_potential = jnp.zeros((data.shape[1],), jnp.float32)
    row_potential = jnp.zeros((noise.shape[0],), jnp.float32)
    for step in range(ITERS):
        scores = (col_potential[None, :] - cost) / EPS
        peak = lax.pmax(jnp.max(scores, axis=1), "col")
        total = lax.psum(jnp.sum(jnp.exp(scores - peak[:, None]), axis=1), "col")
        row_potential = -EPS * jnp.log(float(rows_all)) - EPS * (peak + jnp.log(total))
        scores = (row_potential[:, None] - cost) / EPS
        peak = lax.pmax(jnp.max(scores, axis=0), "row")
        total = lax.psum(jnp.sum(jnp.exp(scores - peak[None, :]), axis=0), "row")
        col_potential = -EPS * jnp.log(float(cols_all)) - EPS * (peak + jnp.log(total))
    weights = (
        rows_all * jnp.exp((row_potential[:, None] + col_potential[None, :] - cost) / EPS)
    ).astype(jnp.bfloat16)
    contract = (((1,), (1,)), ((), ()))
    terms = lax.dot_general(data_full, weights, contract, preferred_element_type=jnp.float32)
    targets = lax.psum_scatter(terms, "col", scatter_dimension=0, tiled=True).astype(jnp.bfloat16)
    return (targets, row_potential, col_potential)


def solution(mesh):
    placed = (P("row", "col"), P("row", "col"))
    return jax.shard_map(
        local,
        mesh=mesh,
        in_specs=placed,
        out_specs=(P("col", "row"), P("row"), P("col")),
        check_vma=False,
    )
```

profile of v0, /device:TPU:6, one launch (start us, length us, event | category | flops | bytes accessed | tf_op | source)
XLA Modules:
  0.0 1075.7 jit_solution(8993773488837862262)
XLA Ops:
  7.2 0.7 all-gather.3.cloned.1.call-update
  7.9 0.7 all-gather.5.cloned.1.call-update
  8.7 80.5 %all-gather.3.cloned.1.call-done = bf16[512,2048]{1,0:T(8,128)(2,1)} async-done(((bf16[512,128]{1,0:T(8,128)(2,1)}), bf16[512,2048]{1,0:T(8,128)(2,1)}) %all-gather.3.cloned.1.call-update) | async-done | bytes 2097168 | tf_op jit(solution)/shard_map/all_gather | solution.py:15
  89.2 2.1 multiply_reduce_fusion.1
  91.2 65.8 %all-gather.5.cloned.1.call-done = bf16[2048,1024]{1,0:T(8,128)(2,1)} async-done(((bf16[64,1024]{1,0:T(8,128)(2,1)}), bf16[2048,1024]{1,0:T(8,128)(2,1)}) %all-gather.5.cloned.1.call-update) | async-done | bytes 4194320 | tf_op jit(solution)/shard_map/all_gather | solution.py:17
  157.0 3.3 multiply_reduce_fusion
  160.4 4.2 fusion
  164.6 34.7 %pmax.56 = f32[512]{0:T(512)S(1)} all-reduce(f32[512]{0:T(512)S(1)} %get-tuple-element.6), channel_id=1, replica_groups=mesh['row'=32,'col'=16] {'col'}, use_global_device_ids=true, to_apply=%region_3.0 | all-reduce | flops 512 | bytes 4096 | tf_op jit(solution)/shard_map/pmax | solution.py:25
  199.3 0.6 exponential_reduce_fusion.7
  199.9 30.6 %psum.56 = f32[512]{0:T(512)S(1)} all-reduce(f32[512]{0:T(512)S(1)} %exponential_reduce_fusion.7), channel_id=1, replica_groups=mesh['row'=32,'col'=16] {'col'}, use_global_device_ids=true, to_apply=%region_5.0 | all-reduce | flops 512 | bytes 4096 | tf_op jit(solution)/shard_map/psum | solution.py:26
  230.8 56.1 %pmax.57 = f32[1024]{0:T(1024)S(1)} all-reduce(f32[1024]{0:T(1024)S(1)} %fusion.1), channel_id=1, replica_groups=mesh['row'=32,'col'=16] {'row'}, use_global_device_ids=true, to_apply=%region_7.0 | all-reduce | flops 1024 | bytes 8192 | tf_op jit(solution)/shard_map/pmax | solution.py:29
  287.4 66.2 %psum.57 = f32[1024]{0:T(1024)S(1)} all-reduce(f32[1024]{0:T(1024)S(1)} %exponential_reduce_fusion.6), channel_id=1, replica_groups=mesh['row'=32,'col'=16] {'row'}, use_global_device_ids=true, to_apply=%region_9.0 | all-reduce | flops 1024 | bytes 8192 | tf_op jit(solution)/shard_map/psum | solution.py:30
  353.9 32.6 %pmax.58 = f32[512]{0:T(512)S(1)} all-reduce(f32[512]{0:T(512)S(1)} %fusion.2), channel_id=1, replica_groups=mesh['row'=32,'col'=16] {'col'}, use_global_device_ids=true, to_apply=%region_11.0 | all-reduce | flops 512 | bytes 4096 | tf_op jit(solution)/shard_map/pmax | solution.py:25
  386.5 0.6 exponential_reduce_fusion.5
  387.1 30.6 %psum.58 = f32[512]{0:T(512)S(1)} all-reduce(f32[512]{0:T(512)S(1)} %exponential_reduce_fusion.5), channel_id=1, replica_groups=mesh['row'=32,'col'=16] {'col'}, use_global_device_ids=true, to_apply=%region_13.0 | all-reduce | flops 512 | bytes 4096 | tf_op jit(solution)/shard_map/psum | solution.py:26
  418.0 69.9 %pmax.59 = f32[1024]{0:T(1024)S(1)} all-reduce(f32[1024]{0:T(1024)S(1)} %fusion.3), channel_id=1, replica_groups=mesh['row'=32,'col'=16] {'row'}, use_global_device_ids=true, to_apply=%region_15.0 | all-reduce | flops 1024 | bytes 8192 | tf_op jit(solution)/shard_map/pmax | solution.py:29
  487.9 0.5 exponential_reduce_fusion.4
  488.4 69.9 %psum.59 = f32[1024]{0:T(1024)S(1)} all-reduce(f32[1024]{0:T(1024)S(1)} %exponential_reduce_fusion.4), channel_id=1, replica_groups=mesh['row'=32,'col'=16] {'row'}, use_global_device_ids=true, to_apply=%region_17.0 | all-reduce | flops 1024 | bytes 8192 | tf_op jit(solution)/shard_map/psum | solution.py:30
  558.6 32.6 %pmax.60 = f32[512]{0:T(512)S(1)} all-reduce(f32[512]{0:T(512)S(1)} %fusion.4), channel_id=1, replica_groups=mesh['row'=32,'col'=16] {'col'}, use_global_device_ids=true, to_apply=%region_19.0 | all-reduce | flops 512 | bytes 4096 | tf_op jit(solution)/shard_map/pmax | solution.py:25
  591.2 0.6 exponential_reduce_fusion.3
  591.8 30.6 %psum.60 = f32[512]{0:T(512)S(1)} all-reduce(f32[512]{0:T(512)S(1)} %exponential_reduce_fusion.3), channel_id=1, replica_groups=mesh['row'=32,'col'=16] {'col'}, use_global_device_ids=true, to_apply=%region_21.0 | all-reduce | flops 512 | bytes 4096 | tf_op jit(solution)/shard_map/psum | solution.py:26
  622.7 69.9 %pmax.61 = f32[1024]{0:T(1024)S(1)} all-reduce(f32[1024]{0:T(1024)S(1)} %fusion.5), channel_id=1, replica_groups=mesh['row'=32,'col'=16] {'row'}, use_global_device_ids=true, to_apply=%region_23.0 | all-reduce | flops 1024 | bytes 8192 | tf_op jit(solution)/shard_map/pmax | solution.py:29
  693.1 69.9 %psum.61 = f32[1024]{0:T(1024)S(1)} all-reduce(f32[1024]{0:T(1024)S(1)} %exponential_reduce_fusion.2), channel_id=1, replica_groups=mesh['row'=32,'col'=16] {'row'}, use_global_device_ids=true, to_apply=%region_25.0 | all-reduce | flops 1024 | bytes 8192 | tf_op jit(solution)/shard_map/psum | solution.py:30
  763.2 32.6 %pmax.62 = f32[512]{0:T(512)S(1)} all-reduce(f32[512]{0:T(512)S(1)} %fusion.6), channel_id=1, replica_groups=mesh['row'=32,'col'=16] {'col'}, use_global_device_ids=true, to_apply=%region_27.0 | all-reduce | flops 512 | bytes 4096 | tf_op jit(solution)/shard_map/pmax | solution.py:25
  795.9 0.6 exponential_reduce_fusion.1
  796.5 30.6 %psum.62 = f32[512]{0:T(512)S(1)} all-reduce(f32[512]{0:T(512)S(1)} %exponential_reduce_fusion.1), channel_id=1, replica_groups=mesh['row'=32,'col'=16] {'col'}, use_global_device_ids=true, to_apply=%region_29.0 | all-reduce | flops 512 | bytes 4096 | tf_op jit(solution)/shard_map/psum | solution.py:26
  827.4 69.9 %pmax.63 = f32[1024]{0:T(1024)S(1)} all-reduce(f32[1024]{0:T(1024)S(1)} %fusion.7), channel_id=1, replica_groups=mesh['row'=32,'col'=16] {'row'}, use_global_device_ids=true, to_apply=%region_31.0 | all-reduce | flops 1024 | bytes 8192 | tf_op jit(solution)/shard_map/pmax | solution.py:29
  897.7 69.9 %psum.63 = f32[1024]{0:T(1024)S(1)} all-reduce(f32[1024]{0:T(1024)S(1)} %exponential_reduce_fusion), channel_id=1, replica_groups=mesh['row'=32,'col'=16] {'row'}, use_global_device_ids=true, to_apply=%region_33.0 | all-reduce | flops 1024 | bytes 8192 | tf_op jit(solution)/shard_map/psum | solution.py:30
  967.6 6.7 convolution_bitcast_fusion
  974.4 93.0 %reduce-scatter.2.cloned.1.call-done = f32[128,512]{0,1:T(8,128)} async-done(((f32[2048,512]{0,1:T(8,128)}), f32[128,512]{0,1:T(8,128)}) %reduce-scatter.2.cloned.1.call-update) | async-done | bytes 262160 | tf_op jit(solution)/shard_map/reduce_scatter | solution.py:37
  1067.4 1.0 convert_element_type.15
  1068.4 0.8 copy.5
  (28 shorter events, 3.9 us)
Async XLA Ops:
  7.2 82.0 %all-gather.3.cloned.1.call-start = ((), (), s32[]{:S(2)}) async-start(), calls=%async_computation.1 | async-start | bytes 2228224 | tf_op jit(solution)/shard_map/all_gather | solution.py:15
  7.9 149.1 %all-gather.5.cloned.1.call-start = ((), (), s32[]{:S(2)}) async-start(), calls=%async_computation.2 | async-start | bytes 4325376 | tf_op jit(solution)/shard_map/all_gather | solution.py:17
  8.6 1058.8 %reduce-scatter.2.cloned.1.call-start = ((), (), s32[]{:S(2)}) async-start(), calls=%async_computation.3 | async-start | bytes 4456448 | tf_op jit(solution)/shard_map/reduce_scatter | solution.py:37
  157.0 3.4 copy-start
  827.1 140.5 %copy-start.1 = (f32[512]{0:T(512)}, f32[512]{0:T(512)S(1)}, u32[]{:S(2)}) copy-start(f32[512]{0:T(512)S(1)} %multiply_subtract_fusion.4) | copy-start | bytes 6148
  967.6 6.7 copy-start.2
Sparse Core Ops, SparseCore 0:
  10.0 79.1 all-gather.2
  92.3 64.6 all-gather.4
  974.5 92.8 reduce-scatter.1
where the time goes:
time: 1080 us
  blocking collectives  797 us (74%)
  waiting for transfers between devices  241 us (22%)
  between operations  13.8 us (1%)
  other arithmetic  12.6 us (1%)
  matrix products  10.9 us (1%)
    psum x4, blocking collectives, local(): total = lax.psum(jnp.sum(jnp.exp(scores - peak[None, :]), axis=0), 'row')  276 us
    pmax x4, blocking collectives, local(): peak = lax.pmax(jnp.max(scores, axis=0), 'row')  266 us
    pmax x4, blocking collectives, local(): peak = lax.pmax(jnp.max(scores, axis=1), 'col')  133 us
    psum x4, blocking collectives, local(): total = lax.psum(jnp.sum(jnp.exp(scores - peak[:, None]), axis=1), 'col')  122 us
    reduce_scatter x1, waiting for transfers between devices, local(): lax.psum_scatter(terms, 'col', scatter_dimension=0, tiled=True)  93 us
    all_gather x1, waiting for transfers between devices, local(): noise_full = lax.all_gather(noise, 'col', axis=1, tiled=True)  80.5 us
    all_gather x1, waiting for transfers between devices, local(): data_full = lax.all_gather(data, 'row', axis=0, tiled=True)  65.8 us
  transfers between devices with their start and end apart: 3, of which 3 were waited for; matrix products, arithmetic and copies ran while one was open for 0% of the time, Pallas kernels for 0%

commit v1 on v0

v1 whole, which is shorter than its diff:
```python
import jax
import jax.numpy as jnp
from jax import lax
from jax.sharding import PartitionSpec as P

ITERS = 4

EPS = 0.01
LIFT = 64


def share(part, axis):
    copies = jnp.broadcast_to(part[None], (lax.axis_size(axis),) + part.shape)
    return lax.all_to_all(copies, axis, 0, 0)


def log_total(scores, dim, axis):
    peak = jnp.max(scores, axis=dim)
    total = jnp.sum(jnp.exp(scores - jnp.expand_dims(peak, dim)), axis=dim)
    both = share(jnp.stack([peak, total]), axis)
    peaks, totals = both[:, 0], both[:, 1]
    whole = jnp.max(peaks, axis=0)
    return whole + jnp.log(jnp.sum(totals * jnp.exp(peaks - whole[None]), axis=0))


def local(noise, data):
    width = noise.shape[1] * lax.axis_size("col")
    rows_all = noise.shape[0] * lax.axis_size("row")
    cols_all = data.shape[1] * lax.axis_size("col")
    data_full = lax.all_gather(data, "row", axis=0, tiled=True)
    noise_full = share(noise, "col").transpose(1, 0, 2).reshape(noise.shape[0], width)
    noise_sq = jnp.sum(noise_full.astype(jnp.float32) ** 2, axis=1)
    data_sq = jnp.sum(data_full.astype(jnp.float32) ** 2, axis=0)
    cross = jnp.dot(noise_full, data_full, preferred_element_type=jnp.float32)
    cost = (noise_sq[:, None] + data_sq[None, :] - 2.0 * cross) / width

    row_first = -EPS * jnp.log(float(rows_all)) - EPS * log_total(-cost / EPS, 1, "col")
    scores = (row_first[:, None] - cost) / EPS
    col_first = -EPS * jnp.log(float(cols_all)) - EPS * log_total(scores, 0, "row")

    lift = 2.0**LIFT
    plan = lift * jnp.exp((row_first[:, None] + col_first[None, :] - cost) / EPS)
    by_col = jnp.ones((data.shape[1],), jnp.float32)
    for step in range(1, ITERS):
        part = jnp.sum(plan * by_col[None, :], axis=1)
        by_row = (lift / rows_all) / jnp.sum(share(part, "col"), axis=0)
        part = jnp.sum(plan * by_row[:, None], axis=0)
        by_col = (lift / cols_all) / jnp.sum(share(part, "row"), axis=0)
    row_potential = row_first + EPS * jnp.log(by_row)
    col_potential = col_first + EPS * jnp.log(by_col)

    weights = (plan * ((rows_all / lift) * by_row)[:, None] * by_col[None, :]).astype(
        jnp.bfloat16
    )
    contract = (((1,), (1,)), ((), ()))
    terms = lax.dot_general(data_full, weights, contract, preferred_element_type=jnp.float32)
    n = lax.axis_size("col")
    terms = terms.astype(jnp.bfloat16).reshape(n, width // n, noise.shape[0])
    parts = lax.all_to_all(terms, "col", 0, 0)
    targets = jnp.sum(parts.astype(jnp.float32), axis=0).astype(jnp.bfloat16)
    return (targets, row_potential, col_potential)


def solution(mesh):
    placed = (P("row", "col"), P("row", "col"))
    return jax.shard_map(
        local,
        mesh=mesh,
        in_specs=placed,
        out_specs=(P("col", "row"), P("row"), P("col")),
        check_vma=False,
    )
```

time: 1080 us -> 281 us (0.26)
  blocking collectives: 797 us -> 220 us
  waiting for transfers between devices: 241 us -> 21.1 us
    pmax x8 -> x0, blocking collectives: 398 us -> none  [the longest x4 266 us: local(): peak = lax.pmax(jnp.max(scores, axis=0), 'row')]
    psum x8 -> x0, blocking collectives: 398 us -> none  [the longest x4 276 us: local(): total = lax.psum(jnp.sum(jnp.exp(scores - peak[None, :]), axis=0), 'row')]
    all_to_all x0 -> x10, blocking collectives: none -> 220 us  [the longest x9 168 us: share(): return lax.all_to_all(copies, axis, 0, 0)]
    reduce_scatter x1 -> x0, waiting for transfers between devices: 93 us -> none  [local(): lax.psum_scatter(terms, 'col', scatter_dimension=0, tiled=True)]
    all_gather x1 -> x0, waiting for transfers between devices: 80.5 us -> none  [local(): noise_full = lax.all_gather(noise, 'col', axis=1, tiled=True)]
    all_gather x1, waiting for transfers between devices: 65.8 us -> 20.4 us  [local(): data_full = lax.all_gather(data, 'row', axis=0, tiled=True)]
  transfers between devices with their start and end apart: 3 -> 1, of which waited for: 3 -> 1; matrix products, arithmetic and copies ran while one was open for 0% -> 1% of each run, Pallas kernels for 0% -> 0%
where the time goes in v1:
time: 281 us; the launch traced here: 279 us
  blocking collectives  220 us (78%)
  waiting for transfers between devices  21.1 us (8%)
  between operations  14.2 us (5%)
  other arithmetic  11.3 us (4%)
  matrix products  8.97 us (3%)
  local copies, waits for them, and re-layouts  3.05 us (1%)
    all_to_all x9, blocking collectives, share(): return lax.all_to_all(copies, axis, 0, 0)  168 us
    all_to_all x1, blocking collectives, local(): parts = lax.all_to_all(terms, 'col', 0, 0)  52.5 us
    all_gather x1, waiting for transfers between devices, local(): data_full = lax.all_gather(data, 'row', axis=0, tiled=True)  20.4 us
  transfers between devices with their start and end apart: 1, of which 1 were waited for; matrix products, arithmetic and copies ran while one was open for 1% of the time, Pallas kernels for 0%

profile of v1, /device:TPU:6, one launch (start us, length us, event | category | flops | bytes accessed | tf_op | source)
XLA Modules:
  0.0 279.0 jit_solution(5100181825993817144)
XLA Ops:
  7.2 0.7 all-gather.2.cloned.1.call-update
  7.9 1.0 copy.20
  9.1 58.3 %all_to_all.56 = bf16[16,512,128]{1,2,0:T(8,128)(2,1)S(1)} all-to-all(bf16[16,512,128]{1,2,0:T(8,128)(2,1)S(1)} %broadcast_in_dim.18), channel_id=1, replica_groups=mesh['row'=32,'col'=16] {'col'}, dimensions={0} | all-to-all | bytes 4194304 | tf_op jit(solution)/shard_map/all_to_all | solution.py:14
  67.4 0.5 multiply_reduce_fusion.1
  67.9 20.4 %all-gather.2.cloned.1.call-done = bf16[2048,1024]{1,0:T(8,128)(2,1)} async-done(((bf16[64,1024]{1,0:T(8,128)(2,1)}), bf16[2048,1024]{1,0:T(8,128)(2,1)}) %all-gather.2.cloned.1.call-update) | async-done | bytes 4194320 | tf_op jit(solution)/shard_map/all_gather | solution.py:30
  88.3 3.3 %multiply_reduce_fusion = f32[1024]{0:T(1024)S(1)} fusion(bf16[2048,1024]{1,0:T(8,128)(2,1)} %all-gather.2.cloned.1.call-done), kind=kLoop, calls=%fused_computation | loop fusion | flops 6290432 | bytes 4198400 | tf_op jit(solution)/shard_map/reduce_sum | solution.py:33
  91.8 4.2 %fusion = (f32[512]{0:T(512)S(1)}, f32[512,1024]{1,0:T(8,128)S(1)}) fusion(bf16[512,2048]{0,1:T(8,128)(2,1)} %bitcast.41, bf16[2048,1024]{1,0:T(8,128)(2,1)S(1)} %copy-done.1, f32[1024]{0:T(1024)S(1)} %multiply_reduce_fusion, f32[512]{0:T(512)S(1)} %multiply_reduce_fusion.1), kind=kOutput, calls=%fused_computation.17 | convolution fusion | flops 2151153152 | bytes 8396800 | tf_op jit(solution)/shard_map/dot_general | solution.py:34
  96.0 0.5 exponential_reduce_fusion.1
  96.5 14.4 %all_to_all.57 = f32[16,2,512]{2,1,0:T(2,128)S(1)} all-to-all(f32[16,2,512]{2,1,0:T(2,128)S(1)} %broadcast_in_dim.19), channel_id=1, replica_groups=mesh['row'=32,'col'=16] {'col'}, dimensions={0} | all-to-all | bytes 131072 | tf_op jit(solution)/shard_map/all_to_all | solution.py:14
  111.0 0.3 fusion.1
  111.3 0.5 exponential_reduce_fusion
  111.9 19.1 %all_to_all.58 = f32[32,2,1024]{2,1,0:T(2,128)S(1)} all-to-all(f32[32,2,1024]{2,1,0:T(2,128)S(1)} %broadcast_in_dim.20), channel_id=1, replica_groups=mesh['row'=32,'col'=16] {'row'}, dimensions={0} | all-to-all | bytes 524288 | tf_op jit(solution)/shard_map/all_to_all | solution.py:14
  131.0 0.2 fusion.13
  131.3 0.7 multiply_reduce_fusion.7
  132.0 11.6 %all_to_all.59 = f32[16,1,512]{2,1,0:T(1,128)S(1)} all-to-all(f32[16,1,512]{2,1,0:T(1,128)S(1)} %broadcast_in_dim.21), channel_id=1, replica_groups=mesh['row'=32,'col'=16] {'col'}, dimensions={0} | all-to-all | bytes 65536 | tf_op jit(solution)/shard_map/all_to_all | solution.py:14
  143.6 0.6 multiply_reduce_fusion.6
  144.3 14.3 %all_to_all.60 = f32[32,1,1024]{2,1,0:T(1,128)S(1)} all-to-all(f32[32,1,1024]{2,1,0:T(1,128)S(1)} %broadcast_in_dim.22), channel_id=1, replica_groups=mesh['row'=32,'col'=16] {'row'}, dimensions={0} | all-to-all | bytes 262144 | tf_op jit(solution)/shard_map/all_to_all | solution.py:14
  158.7 0.7 multiply_reduce_fusion.5
  159.5 11.1 %all_to_all.61 = f32[16,1,512]{2,1,0:T(1,128)S(1)} all-to-all(f32[16,1,512]{2,1,0:T(1,128)S(1)} %broadcast_in_dim.23), channel_id=1, replica_groups=mesh['row'=32,'col'=16] {'col'}, dimensions={0} | all-to-all | bytes 65536 | tf_op jit(solution)/shard_map/all_to_all | solution.py:14
  170.6 0.6 multiply_reduce_fusion.4
  171.3 14.1 %all_to_all.62 = f32[32,1,1024]{2,1,0:T(1,128)S(1)} all-to-all(f32[32,1,1024]{2,1,0:T(1,128)S(1)} %broadcast_in_dim.24), channel_id=1, replica_groups=mesh['row'=32,'col'=16] {'row'}, dimensions={0} | all-to-all | bytes 262144 | tf_op jit(solution)/shard_map/all_to_all | solution.py:14
  185.4 0.7 multiply_reduce_fusion.3
  186.2 11.1 %all_to_all.63 = f32[16,1,512]{2,1,0:T(1,128)S(1)} all-to-all(f32[16,1,512]{2,1,0:T(1,128)S(1)} %broadcast_in_dim.25), channel_id=1, replica_groups=mesh['row'=32,'col'=16] {'col'}, dimensions={0} | all-to-all | bytes 65536 | tf_op jit(solution)/shard_map/all_to_all | solution.py:14
  197.3 0.6 multiply_add_fusion.1
  197.9 0.6 multiply_reduce_fusion.2
  198.6 14.1 %all_to_all.64 = f32[32,1,1024]{2,1,0:T(1,128)S(1)} all-to-all(f32[32,1,1024]{2,1,0:T(1,128)S(1)} %broadcast_in_dim.26), channel_id=1, replica_groups=mesh['row'=32,'col'=16] {'row'}, dimensions={0} | all-to-all | bytes 262144 | tf_op jit(solution)/shard_map/all_to_all | solution.py:14
  212.7 0.6 multiply_add_fusion
  213.3 4.8 %fusion.2 = bf16[64,16,8,128]{3,2,1,0:T(8,128)(2,1)S(1)} fusion(bf16[2048,1024]{1,0:T(8,128)(2,1)} %all-gather.2.cloned.1.call-done, f32[1024]{0:T(1024)S(1)} %get-tuple-element.19, f32[512]{0:T(512)S(1)} %get-tuple-element.22, f32[512,1024]{1,0:T(8,128)S(1)} %get-tuple-element.24, f32[1024]{0:T(1024)S(1)} %multiply_subtract_fusion, ...), kind=kOutput, calls=%fused_computation.19 | convolution fusion | flops 2151677952 | bytes 8400896 | tf_op jit(solution)/shard_map/dot_general | solution.py:56
  218.1 0.5 copy.67
  218.7 52.5 %all_to_all.65 = bf16[16,128,512]{1,2,0:T(8,128)(2,1)S(1)} all-to-all(bf16[16,128,512]{1,2,0:T(8,128)(2,1)S(1)} %bitcast.42), channel_id=1, replica_groups=mesh['row'=32,'col'=16] {'col'}, dimensions={0} | all-to-all | bytes 4194304 | tf_op jit(solution)/shard_map/all_to_all | solution.py:59
  271.1 0.3 reduce_sum.192
  271.4 0.8 copy.31
  (31 shorter events, 1.4 us)
Async XLA Ops:
  7.2 81.1 %all-gather.2.cloned.1.call-start = ((), (), s32[]{:S(2)}) async-start(), calls=%async_computation.10 | async-start | bytes 4325376 | tf_op jit(solution)/shard_map/all_gather | solution.py:30
  67.4 24.2 %copy-start = (bf16[16,512,128]{1,2,0:T(8,128)(2,1)}, bf16[16,512,128]{1,2,0:T(8,128)(2,1)S(1)}, u32[]{:S(2)}) copy-start(bf16[16,512,128]{1,2,0:T(8,128)(2,1)S(1)} %all_to_all.56) | copy-start | bytes 6291460
  88.3 3.4 %copy-start.1 = (bf16[2048,1024]{1,0:T(8,128)(2,1)S(1)}, bf16[2048,1024]{1,0:T(8,128)(2,1)}, u32[]{:S(2)}) copy-start(bf16[2048,1024]{1,0:T(8,128)(2,1)} %all-gather.2.cloned.1.call-done) | copy-start | bytes 12582916
Sparse Core Ops, SparseCore 0:
  11.1 77.1 all-gather.1

commit v2 on v1

v2 whole, which is shorter than its diff:
```python
import jax
import jax.numpy as jnp
from jax import lax
from jax.sharding import PartitionSpec as P

ITERS = 4

EPS = 0.01
LIFT = 64

Z_HI, X, CORE = 4, 4, 2
Z_LO, Y = 2, 8
Y_GROUPS = [[z * Y + y for y in range(Y)] for z in range(Z_LO)]
OWNERS = [[z * Y + y for y in range(Y) for z in range(Z_LO)]]


def along_z(array, by):
    step = X * CORE
    pairs = [(i, (i + by * step) % (Z_HI * step)) for i in range(Z_HI * step)]
    return lax.ppermute(array, "row", pairs)


def along_x(array, by):
    step = X * CORE
    pairs = [(i, i // step * step + (i + by * CORE) % step) for i in range(Z_HI * step)]
    return lax.ppermute(array, "row", pairs)


def other_core(array):
    return lax.ppermute(array, "row", [(i, i ^ 1) for i in range(Z_HI * X * CORE)])


def other_z(array):
    return lax.ppermute(array, "col", [(i, (i + Y) % (Z_LO * Y)) for i in range(Z_LO * Y)])


def share(part, axis, groups=None):
    count = len(groups[0]) if groups else lax.axis_size(axis)
    copies = jnp.broadcast_to(part[None], (count,) + part.shape)
    return lax.all_to_all(copies, axis, 0, 0, axis_index_groups=groups)


def gather_noise(noise):
    there = other_z(noise)
    first = lax.axis_index("col") < Y
    low, high = jnp.where(first, noise, there), jnp.where(first, there, noise)
    half = noise.shape[1] // 2
    halves = [
        jnp.concatenate([low[:, k : k + half], high[:, k : k + half]], axis=1)
        for k in (0, half)
    ]
    return share(jnp.stack(halves), "col", Y_GROUPS)


def gather_data(data):
    row = lax.axis_index("row")
    z, x = row // (X * CORE), row // CORE % X
    up, down = along_z(data, 1), along_z(data, -1)
    far = along_z(up, 1)
    plane = jnp.zeros((2, Z_LO) + data.shape, data.dtype)
    for piece, by in ((data, 0), (up, 3), (down, 1), (far, 2)):
        at = (z + by) % Z_HI
        plane = lax.dynamic_update_slice(plane, piece[None, None], (at % 2, at // 2, 0, 0))
    up, down = along_x(plane, 1), along_x(plane, -1)
    far = along_x(up, 1)
    whole = jnp.zeros((2, X, Z_LO) + data.shape, data.dtype)
    for piece, by in ((plane, 0), (up, 3), (down, 1), (far, 2)):
        whole = lax.dynamic_update_slice(whole, piece[:, None], (0, (x + by) % X, 0, 0, 0))
    return whole.reshape(-1, data.shape[1])


def log_total(scores, dim, axis):
    peak = jnp.max(scores, axis=dim)
    total = jnp.sum(jnp.exp(scores - jnp.expand_dims(peak, dim)), axis=dim)
    logs = share(peak + jnp.log(total), axis)
    whole = jnp.max(logs, axis=0)
    return whole + jnp.log(jnp.sum(jnp.exp(logs - whole[None]), axis=0))


def local(noise, data):
    rows, cols = noise.shape[0], data.shape[1]
    width = noise.shape[1] * lax.axis_size("col")
    rows_all = rows * lax.axis_size("row")
    cols_all = cols * lax.axis_size("col")
    core = lax.axis_index("row") % CORE

    noise_all = gather_noise(noise)
    here = gather_data(data)
    there = other_core(here)
    sq = jnp.sum(here.astype(jnp.float32) ** 2, axis=0)
    data_sq = sq + other_core(sq)
    noise_sq = jnp.sum(noise_all.astype(jnp.float32) ** 2, axis=(0, 1, 3))

    def half(which):
        part = lax.dynamic_index_in_dim(noise_all, which, 1, keepdims=False)
        return part.transpose(1, 0, 2).reshape(rows, -1)

    cross = jnp.dot(half(core), here, preferred_element_type=jnp.float32)
    cross += jnp.dot(half(1 - core), there, preferred_element_type=jnp.float32)

    unit = 1.0 / (width * EPS)
    logits = cross * (2.0 * unit)
    row_first = -jnp.log(float(rows_all)) - log_total(
        logits - (data_sq * unit)[None, :], 1, "col"
    )
    col_first = -jnp.log(float(cols_all)) - log_total(logits + row_first[:, None], 0, "row")

    lift = 2.0**LIFT
    plan = lift * jnp.exp(logits + row_first[:, None] + col_first[None, :])
    by_col = jnp.ones((cols,), jnp.float32)
    for step in range(1, ITERS):
        part = jnp.sum(plan * by_col[None, :], axis=1)
        by_row = (lift / rows_all) / jnp.sum(share(part, "col"), axis=0)
        part = jnp.sum(plan * by_row[:, None], axis=0)
        by_col = (lift / cols_all) / jnp.sum(share(part, "row"), axis=0)
    row_potential = noise_sq / width + EPS * (row_first + jnp.log(by_row))
    col_potential = data_sq / width + EPS * (col_first + jnp.log(by_col))

    weights = (plan * ((rows_all / lift) * by_row)[:, None] * by_col[None, :]).astype(
        jnp.bfloat16
    )
    contract = (((1,), (1,)), ((), ()))
    terms = [
        lax.dot_general(part, weights, contract, preferred_element_type=jnp.float32)
        .astype(jnp.bfloat16)
        .reshape(Z_LO * Y, -1, rows)
        for part in (here, there)
    ]
    parts = lax.all_to_all(jnp.stack(terms, axis=1), "col", 0, 0, axis_index_groups=OWNERS)
    targets = jnp.sum(parts.astype(jnp.float32), axis=0).astype(jnp.bfloat16)
    targets = jnp.where(core == 0, targets, targets[::-1]).reshape(-1, rows)
    return (targets, row_potential, col_potential)


def solution(mesh):
    placed = (P("row", "col"), P("row", "col"))
    return jax.shard_map(
        local,
        mesh=mesh,
        in_specs=placed,
        out_specs=(P("col", "row"), P("row"), P("col")),
        check_vma=False,
    )
```

time: 281 us -> 269 us (0.957)
  blocking collectives: 220 us -> 95.9 us
  waiting for transfers between devices: 21.1 us -> 85.5 us
  starting transfers between devices: 0.04 us -> 46.7 us
  between operations: 14.2 us -> 1.31 us
  local copies, waits for them, and re-layouts: 3.05 us -> 11.2 us
  matrix products: 8.97 us -> 12 us
  other arithmetic: 11.3 us -> 14.2 us
    all_to_all x10 -> x7, blocking collectives: 220 us -> 95.9 us  [share(): return lax.all_to_all(copies, axis, 0, 0, axis_index_groups=groups)]
    all_to_all x0 -> x3, waiting for transfers between devices: none -> 64 us  [the longest x1 51.3 us: local(): lax.all_to_all(jnp.stack(terms, axis=1), 'col', 0, 0, axis_index_groups=O...]
    ppermute x0 -> x9, starting transfers between devices: none -> 32.2 us  [the longest x3 15.2 us: along_z(): return lax.ppermute(array, 'row', pairs)]
    ppermute x0 -> x9, waiting for transfers between devices: none -> 21.4 us  [the longest x3 8.65 us: along_x(): return lax.ppermute(array, 'row', pairs)]
    all_gather x1 -> x0, waiting for transfers between devices: 20.4 us -> none  [local(): data_full = lax.all_gather(data, 'row', axis=0, tiled=True)]
    all_to_all x0 -> x3, starting transfers between devices: none -> 14.5 us  [the longest x2 10.8 us: share(): return lax.all_to_all(copies, axis, 0, 0, axis_index_groups=groups)]
    dynamic_update_slice x0 -> x8, local copies, waits for them, and re-layouts: none -> 5.36 us  [the longest x4 4.39 us: gather_data(): lax.dynamic_update_slice(whole, piece[:, None], (0, (x + by) % X, 0, 0, 0))]
    broadcast_in_dim x9 -> x11, local copies, waits for them, and re-layouts: 0.56 us -> 4.19 us  [the longest x9 2.55 us: share(): copies = jnp.broadcast_to(part[None], (count,) + part.shape)]
  transfers between devices with their start and end apart: 1 -> 12, of which waited for: 1 -> 8; matrix products, arithmetic and copies ran while one was open for 1% -> 5% of each run, Pallas kernels for 0% -> 0%
where the time goes in v2:
time: 269 us; the launch traced here: 267 us
  blocking collectives  95.9 us (36%)
  waiting for transfers between devices  85.5 us (32%)
  starting transfers between devices  46.7 us (17%)
  other arithmetic  14.2 us (5%)
  matrix products  12 us (4%)
  local copies, waits for them, and re-layouts  11.2 us (4%)
    all_to_all x7, blocking collectives, share(): return lax.all_to_all(copies, axis, 0, 0, axis_index_groups=groups)  95.9 us
    all_to_all x1, waiting for transfers between devices, local(): lax.all_to_all(jnp.stack(terms, axis=1), 'col', 0, 0, axis_index_groups=O...  51.3 us
    ppermute x3, starting transfers between devices, along_z(): return lax.ppermute(array, 'row', pairs)  15.2 us
    all_to_all x2, waiting for transfers between devices, share(): return lax.all_to_all(copies, axis, 0, 0, axis_index_groups=groups)  12.7 us
    all_to_all x2, starting transfers between devices, share(): return lax.all_to_all(copies, axis, 0, 0, axis_index_groups=groups)  10.8 us
    ppermute x3, starting transfers between devices, along_x(): return lax.ppermute(array, 'row', pairs)  9.32 us
    ppermute x3, waiting for transfers between devices, along_x(): return lax.ppermute(array, 'row', pairs)  8.65 us
    ppermute x3, waiting for transfers between devices, along_z(): return lax.ppermute(array, 'row', pairs)  7.63 us
  transfers between devices with their start and end apart: 12, of which 8 were waited for; matrix products, arithmetic and copies ran while one was open for 5% of the time, Pallas kernels for 0%

profile of v2, /device:TPU:6, one launch (start us, length us, event | category | flops | bytes accessed | tf_op | source)
XLA Modules:
  0.0 266.7 jit_solution(17622541989050262537)
XLA Ops:
  0.6 10.9 %collective-permute-start.1 = (bf16[64,1024]{1,0:T(8,128)(2,1)}, bf16[64,1024]{1,0:T(8,128)(2,1)S(1)}, u32[]{:S(2)}, u32[]{:S(2)}) collective-permute-start(bf16[64,1024]{1,0:T(8,128)(2,1)} %param.3), channel_id=1, source_target_pairs={{0,384},{16,400},{32,416},{48,432},{64,448},{80,464},{96,480},{112... | collective-permute-start | bytes 393224 | tf_op jit(solution)/shard_map/ppermute | solution.py:20
  11.6 1.9 collective-permute-start
  13.5 3.4 %collective-permute-start.6 = (bf16[512,128]{1,0:T(8,128)(2,1)}, bf16[512,128]{1,0:T(8,128)(2,1)S(1)}, u32[]{:S(2)}, u32[]{:S(2)}) collective-permute-start(bf16[512,128]{1,0:T(8,128)(2,1)} %param.2), channel_id=1, source_target_pairs={{0,8},{1,9},{2,10},{3,11},{4,12},{5,13},{6,14},{7,15},{8,0},{9,1},... | collective-permute-start | bytes 393224 | tf_op jit(solution)/shard_map/ppermute | solution.py:34
  18.1 4.4 %collective-permute-done.6 = bf16[512,128]{1,0:T(8,128)(2,1)S(1)} collective-permute-done((bf16[512,128]{1,0:T(8,128)(2,1)}, bf16[512,128]{1,0:T(8,128)(2,1)S(1)}, u32[]{:S(2)}, u32[]{:S(2)}) %collective-permute-start.6) | collective-permute-done | bytes 131104 | tf_op jit(solution)/shard_map/ppermute | solution.py:34
  25.5 7.1 %all-to-all-start = ((bf16[8,2,512,128]{2,3,1,0:T(8,128)(2,1)}), bf16[8,2,512,128]{2,3,1,0:T(8,128)(2,1)S(1)}, u32[]{:S(2)}, u32[]{:S(2)}) async-start(bf16[8,2,512,128]{2,3,1,0:T(8,128)(2,1)} %broadcast_in_dim.48), calls=%async_computation | async-start | bytes 4194304 | tf_op jit(solution)/shard_map/all_to_all | solution.py:40
  32.6 2.4 collective-permute-start.2
  35.1 7.6 %collective-permute-done.2 = bf16[64,1024]{1,0:T(8,128)(2,1)S(1)} collective-permute-done((bf16[64,1024]{1,0:T(8,128)(2,1)S(1)}, bf16[64,1024]{1,0:T(8,128)(2,1)S(1)}, u32[]{:S(2)}, u32[]{:S(2)}) %collective-permute-start.2) | collective-permute-done | bytes 131104 | tf_op jit(solution)/shard_map/ppermute | solution.py:20
  42.7 2.4 collective-permute-start.3
  45.1 3.5 %collective-permute-start.4 = (bf16[2,2,64,1024]{3,2,1,0:T(8,128)(2,1)S(1)}, bf16[2,2,64,1024]{3,2,1,0:T(8,128)(2,1)}, u32[]{:S(2)}, u32[]{:S(2)}) collective-permute-start(bf16[2,2,64,1024]{3,2,1,0:T(8,128)(2,1)S(1)} %bitcast_dynamic-update-slice_fusion.4), channel_id=1, source_target_pairs={{0,96},{16,112},{32,0},{48,16},{64,32},{80,48},{96,64},{112,80},{1... | collective-permute-start | bytes 1572872 | tf_op jit(solution)/shard_map/ppermute | solution.py:26
  48.7 6.1 %collective-permute-done.3 = bf16[2,2,64,1024]{3,2,1,0:T(8,128)(2,1)S(1)} collective-permute-done((bf16[2,2,64,1024]{3,2,1,0:T(8,128)(2,1)S(1)}, bf16[2,2,64,1024]{3,2,1,0:T(8,128)(2,1)S(1)}, u32[]{:S(2)}, u32[]{:S(2)}) %collective-permute-start.3) | collective-permute-done | bytes 524320 | tf_op jit(solution)/shard_map/ppermute | solution.py:26
  54.8 3.5 %collective-permute-start.5 = (bf16[2,2,64,1024]{3,2,1,0:T(8,128)(2,1)S(1)}, bf16[2,2,64,1024]{3,2,1,0:T(8,128)(2,1)S(1)}, u32[]{:S(2)}, u32[]{:S(2)}) collective-permute-start(bf16[2,2,64,1024]{3,2,1,0:T(8,128)(2,1)S(1)} %collective-permute-done.3), channel_id=1, source_target_pairs={{0,32},{16,48},{32,64},{48,80},{64,96},{80,112},{96,0},{112,16},{1... | collective-permute-start | bytes 1572872 | tf_op jit(solution)/shard_map/ppermute | solution.py:26
  63.4 2.5 collective-permute-done.5
  66.8 1.9 collective-permute-start.7
  68.7 2.1 multiply_reduce_fusion.1
  70.8 2.4 collective-permute-start.8
  74.0 6.5 %all-to-all-done = bf16[8,2,512,128]{2,3,1,0:T(8,128)(2,1)S(1)} async-done(((bf16[8,2,512,128]{2,3,1,0:T(8,128)(2,1)}), bf16[8,2,512,128]{2,3,1,0:T(8,128)(2,1)S(1)}, u32[]{:S(2)}, u32[]{:S(2)}) %all-to-all-start) | async-done | bytes 2097184 | tf_op jit(solution)/shard_map/all_to_all | solution.py:40
  81.9 2.9 %fusion.6 = f32[512,1024]{1,0:T(8,128)S(1)} fusion(bf16[512,1024]{0,1:T(8,128)(2,1)S(1)} %bitcast.62, bf16[1024,1024]{1,0:T(8,128)(2,1)} %collective-permute-done.7), kind=kOutput, calls=%fused_computation.57 | convolution fusion | flops 1073741824 | bytes 5242880 | tf_op jit(solution)/shard_map/dot_general | solution.py:99
  84.7 3.0 %subtract_reduce_fusion = (f32[512]{0:T(512)S(1)}, f32[512,1024]{1,0:T(8,128)S(1)}) fusion(f32[1024]{0:T(1024)S(1)} %broadcast_multiply_fusion, f32[512,1024]{1,0:T(8,128)S(1)} %fusion.6, bf16[512,1024]{0,1:T(8,128)(2,1)S(1)} %bitcast.63, bf16[1024,1024]{1,0:T(8,128)(2,1)} %bitcast.11), kind=kOutput, calls=%fused_computation.14 | convolution fusion | flops 1075838464 | bytes 7346176 | tf_op jit(solution)/shard_map/dot_general | solution.py:98
  88.2 12.1 %all_to_all.64 = f32[16,1,512]{2,1,0:T(1,128)S(1)} all-to-all(f32[16,1,512]{2,1,0:T(1,128)S(1)} %broadcast_in_dim.49), channel_id=1, replica_groups=mesh['row'=32,'col'=16] {'col'}, dimensions={0} | all-to-all | bytes 65536 | tf_op jit(solution)/shard_map/all_to_all | solution.py:40
  101.2 19.8 %all_to_all.65 = f32[32,1,1024]{2,1,0:T(1,128)S(1)} all-to-all(f32[32,1,1024]{2,1,0:T(1,128)S(1)} %broadcast_in_dim.50), channel_id=1, replica_groups=mesh['row'=32,'col'=16] {'row'}, dimensions={0} | all-to-all | bytes 262144 | tf_op jit(solution)/shard_map/all_to_all | solution.py:40
  121.7 11.1 %all_to_all.66 = f32[16,1,512]{2,1,0:T(1,128)S(1)} all-to-all(f32[16,1,512]{2,1,0:T(1,128)S(1)} %broadcast_in_dim.51), channel_id=1, replica_groups=mesh['row'=32,'col'=16] {'col'}, dimensions={0} | all-to-all | bytes 65536 | tf_op jit(solution)/shard_map/all_to_all | solution.py:40
  133.5 13.9 %all_to_all.67 = f32[32,1,1024]{2,1,0:T(1,128)S(1)} all-to-all(f32[32,1,1024]{2,1,0:T(1,128)S(1)} %broadcast_in_dim.52), channel_id=1, replica_groups=mesh['row'=32,'col'=16] {'row'}, dimensions={0} | all-to-all | bytes 262144 | tf_op jit(solution)/shard_map/all_to_all | solution.py:40
  148.1 11.1 %all_to_all.68 = f32[16,1,512]{2,1,0:T(1,128)S(1)} all-to-all(f32[16,1,512]{2,1,0:T(1,128)S(1)} %broadcast_in_dim.53), channel_id=1, replica_groups=mesh['row'=32,'col'=16] {'col'}, dimensions={0} | all-to-all | bytes 65536 | tf_op jit(solution)/shard_map/all_to_all | solution.py:40
  159.9 13.9 %all_to_all.69 = f32[32,1,1024]{2,1,0:T(1,128)S(1)} all-to-all(f32[32,1,1024]{2,1,0:T(1,128)S(1)} %broadcast_in_dim.54), channel_id=1, replica_groups=mesh['row'=32,'col'=16] {'row'}, dimensions={0} | all-to-all | bytes 262144 | tf_op jit(solution)/shard_map/all_to_all | solution.py:40
  175.1 3.7 %all-to-all-start.7 = ((f32[16,1,512]{2,1,0:T(1,128)}), f32[16,1,512]{2,1,0:T(1,128)S(1)}, u32[]{:S(2)}, u32[]{:S(2)}) async-start(f32[16,1,512]{2,1,0:T(1,128)} %broadcast_in_dim.55), calls=%async_computation.7 | async-start | bytes 65536 | tf_op jit(solution)/shard_map/all_to_all | solution.py:40
  178.8 2.1 multiply_reduce_fusion
  180.9 6.2 %all-to-all-done.7 = f32[16,1,512]{2,1,0:T(1,128)S(1)} async-done(((f32[16,1,512]{2,1,0:T(1,128)}), f32[16,1,512]{2,1,0:T(1,128)S(1)}, u32[]{:S(2)}, u32[]{:S(2)}) %all-to-all-start.7) | async-done | bytes 32800 | tf_op jit(solution)/shard_map/all_to_all | solution.py:40
  188.3 14.0 %all_to_all.70 = f32[32,1,1024]{2,1,0:T(1,128)S(1)} all-to-all(f32[32,1,1024]{2,1,0:T(1,128)S(1)} %broadcast_in_dim.56), channel_id=1, replica_groups=mesh['row'=32,'col'=16] {'row'}, dimensions={0} | all-to-all | bytes 262144 | tf_op jit(solution)/shard_map/all_to_all | solution.py:40
  203.0 3.1 %convolution_convert_fusion.1 = bf16[1024,512]{1,0:T(8,128)(2,1)S(1)} fusion(bf16[1024,1024]{1,0:T(8,128)(2,1)} %bitcast.11, f32[1024]{0:T(1024)S(1)} %get-tuple-element.12, f32[512]{0:T(512)S(1)} %get-tuple-element.15, f32[512,1024]{1,0:T(8,128)S(1)} %get-tuple-element.17, f32[1024]{0:T(1024)S(1)} %add_subtract_fusion, f32[512]{0:T(512)S(1)} %add_subtract_fusion.1), kind=kOutput, calls=%fused_computation.17 | convolution fusion | flops 1076887552 | bytes 5255168 | tf_op jit(solution)/shard_map/dot_general | solution.py:124
  206.1 3.1 %convolution_convert_fusion = bf16[1024,512]{1,0:T(8,128)(2,1)S(1)} fusion(bf16[1024,1024]{1,0:T(8,128)(2,1)} %collective-permute-done.7, f32[1024]{0:T(1024)S(1)} %get-tuple-element.12, f32[512]{0:T(512)S(1)} %get-tuple-element.15, f32[512,1024]{1,0:T(8,128)S(1)} %get-tuple-element.17, f32[1024]{0:T(1024)S(1)} %add_subtract_fusion, ...), kind=kOutput, calls=%fused_computation.16 | convolution fusion | flops 1076887552 | bytes 5255168 | tf_op jit(solution)/shard_map/dot_general | solution.py:124
  210.7 3.7 %all-to-all-start.9 = ((bf16[16,2,64,512]{3,2,1,0:T(8,128)(2,1)}), bf16[16,2,64,512]{3,2,1,0:T(8,128)(2,1)S(1)}, u32[]{:S(2)}, u32[]{:S(2)}) async-start(bf16[16,2,64,512]{3,2,1,0:T(8,128)(2,1)} %pad_maximum_fusion), calls=%async_computation.9 | async-start | bytes 4194304 | tf_op jit(solution)/shard_map/all_to_all | solution.py:129
  214.4 51.3 %all-to-all-done.9 = bf16[16,2,64,512]{3,2,1,0:T(8,128)(2,1)S(1)} async-done(((bf16[16,2,64,512]{3,2,1,0:T(8,128)(2,1)}), bf16[16,2,64,512]{3,2,1,0:T(8,128)(2,1)S(1)}, u32[]{:S(2)}, u32[]{:S(2)}) %all-to-all-start.9) | async-done | bytes 2097184 | tf_op jit(solution)/shard_map/all_to_all | solution.py:129
  (66 shorter events, 22.0 us)
Async XLA Ops:
  0.6 34.4 %collective-permute-start.1 = (bf16[64,1024]{1,0:T(8,128)(2,1)}, bf16[64,1024]{1,0:T(8,128)(2,1)S(1)}, u32[]{:S(2)}, u32[]{:S(2)}) collective-permute-start(bf16[64,1024]{1,0:T(8,128)(2,1)} %param.3), channel_id=1, source_target_pairs={{0,384},{16,400},{32,416},{48,432},{64,448},{80,464},{96,480},{112... | collective-permute-start | bytes 393224 | tf_op jit(solution)/shard_map/ppermute | solution.py:20
  11.6 21.0 %collective-permute-start = (bf16[64,1024]{1,0:T(8,128)(2,1)}, bf16[64,1024]{1,0:T(8,128)(2,1)S(1)}, u32[]{:S(2)}, u32[]{:S(2)}) collective-permute-start(bf16[64,1024]{1,0:T(8,128)(2,1)} %param.3), channel_id=1, source_target_pairs={{0,128},{16,144},{32,160},{48,176},{64,192},{80,208},{96,224},{112... | collective-permute-start | bytes 393224 | tf_op jit(solution)/shard_map/ppermute | solution.py:20
  13.5 9.0 %collective-permute-start.6 = (bf16[512,128]{1,0:T(8,128)(2,1)}, bf16[512,128]{1,0:T(8,128)(2,1)S(1)}, u32[]{:S(2)}, u32[]{:S(2)}) collective-permute-start(bf16[512,128]{1,0:T(8,128)(2,1)} %param.2), channel_id=1, source_target_pairs={{0,8},{1,9},{2,10},{3,11},{4,12},{5,13},{6,14},{7,15},{8,0},{9,1},... | collective-permute-start | bytes 393224 | tf_op jit(solution)/shard_map/ppermute | solution.py:34
  25.5 55.0 %all-to-all-start = ((bf16[8,2,512,128]{2,3,1,0:T(8,128)(2,1)}), bf16[8,2,512,128]{2,3,1,0:T(8,128)(2,1)S(1)}, u32[]{:S(2)}, u32[]{:S(2)}) async-start(bf16[8,2,512,128]{2,3,1,0:T(8,128)(2,1)} %broadcast_in_dim.48), calls=%async_computation | async-start | bytes 4194304 | tf_op jit(solution)/shard_map/all_to_all | solution.py:40
  32.6 10.1 %collective-permute-start.2 = (bf16[64,1024]{1,0:T(8,128)(2,1)S(1)}, bf16[64,1024]{1,0:T(8,128)(2,1)S(1)}, u32[]{:S(2)}, u32[]{:S(2)}) collective-permute-start(bf16[64,1024]{1,0:T(8,128)(2,1)S(1)} %collective-permute-done), channel_id=1, source_target_pairs={{0,128},{16,144},{32,160},{48,176},{64,192},{80,208},{96,224},{112... | collective-permute-start | bytes 393224 | tf_op jit(solution)/shard_map/ppermute | solution.py:20
  42.7 12.1 %collective-permute-start.3 = (bf16[2,2,64,1024]{3,2,1,0:T(8,128)(2,1)S(1)}, bf16[2,2,64,1024]{3,2,1,0:T(8,128)(2,1)S(1)}, u32[]{:S(2)}, u32[]{:S(2)}) collective-permute-start(bf16[2,2,64,1024]{3,2,1,0:T(8,128)(2,1)S(1)} %bitcast_dynamic-update-slice_fusion.4), channel_id=1, source_target_pairs={{0,32},{16,48},{32,64},{48,80},{64,96},{80,112},{96,0},{112,16},{1... | collective-permute-start | bytes 1572872 | tf_op jit(solution)/shard_map/ppermute | solution.py:26
  45.1 16.5 %collective-permute-start.4 = (bf16[2,2,64,1024]{3,2,1,0:T(8,128)(2,1)S(1)}, bf16[2,2,64,1024]{3,2,1,0:T(8,128)(2,1)}, u32[]{:S(2)}, u32[]{:S(2)}) collective-permute-start(bf16[2,2,64,1024]{3,2,1,0:T(8,128)(2,1)S(1)} %bitcast_dynamic-update-slice_fusion.4), channel_id=1, source_target_pairs={{0,96},{16,112},{32,0},{48,16},{64,32},{80,48},{96,64},{112,80},{1... | collective-permute-start | bytes 1572872 | tf_op jit(solution)/shard_map/ppermute | solution.py:26
  54.8 11.1 %collective-permute-start.5 = (bf16[2,2,64,1024]{3,2,1,0:T(8,128)(2,1)S(1)}, bf16[2,2,64,1024]{3,2,1,0:T(8,128)(2,1)S(1)}, u32[]{:S(2)}, u32[]{:S(2)}) collective-permute-start(bf16[2,2,64,1024]{3,2,1,0:T(8,128)(2,1)S(1)} %collective-permute-done.3), channel_id=1, source_target_pairs={{0,32},{16,48},{32,64},{48,80},{64,96},{80,112},{96,0},{112,16},{1... | collective-permute-start | bytes 1572872 | tf_op jit(solution)/shard_map/ppermute | solution.py:26
  66.8 15.1 %collective-permute-start.7 = (bf16[1024,1024]{1,0:T(8,128)(2,1)}, bf16[1024,1024]{1,0:T(8,128)(2,1)}, u32[]{:S(2)}, u32[]{:S(2)}) collective-permute-start(bf16[1024,1024]{1,0:T(8,128)(2,1)} %bitcast.11), channel_id=1, source_target_pairs={{0,16},{16,0},{32,48},{48,32},{64,80},{80,64},{96,112},{112,96},{1... | collective-permute-start | bytes 6291464 | tf_op jit(solution)/shard_map/ppermute | solution.py:30
  70.8 3.2 %collective-permute-start.8 = (f32[1024]{0:T(1024)S(1)}, f32[1024]{0:T(1024)S(1)}, u32[]{:S(2)}, u32[]{:S(2)}) collective-permute-start(f32[1024]{0:T(1024)S(1)} %multiply_reduce_fusion.1), channel_id=1, source_target_pairs={{0,16},{16,0},{32,48},{48,32},{64,80},{80,64},{96,112},{112,96},{1... | collective-permute-start | bytes 12296 | tf_op jit(solution)/shard_map/ppermute | solution.py:30
  80.5 1.4 copy-start
  175.1 12.0 %all-to-all-start.7 = ((f32[16,1,512]{2,1,0:T(1,128)}), f32[16,1,512]{2,1,0:T(1,128)S(1)}, u32[]{:S(2)}, u32[]{:S(2)}) async-start(f32[16,1,512]{2,1,0:T(1,128)} %broadcast_in_dim.55), calls=%async_computation.7 | async-start | bytes 65536 | tf_op jit(solution)/shard_map/all_to_all | solution.py:40
  210.7 55.0 %all-to-all-start.9 = ((bf16[16,2,64,512]{3,2,1,0:T(8,128)(2,1)}), bf16[16,2,64,512]{3,2,1,0:T(8,128)(2,1)S(1)}, u32[]{:S(2)}, u32[]{:S(2)}) async-start(bf16[16,2,64,512]{3,2,1,0:T(8,128)(2,1)} %pad_maximum_fusion), calls=%async_computation.9 | async-start | bytes 4194304 | tf_op jit(solution)/shard_map/all_to_all | solution.py:129

commit v3 on v2

--- a/solution.py
+++ b/solution.py
@@ -10,8 +10,7 @@
 
 Z_HI, X, CORE = 4, 4, 2
 Z_LO, Y = 2, 8
-Y_GROUPS = [[z * Y + y for y in range(Y)] for z in range(Z_LO)]
-OWNERS = [[z * Y + y for y in range(Y) for z in range(Z_LO)]]
+PARITIES = [[z * Y + y + q for z in range(Z_LO) for y in range(0, Y, 2)] for q in range(2)]
 
 
 def along_z(array, by):
@@ -30,8 +29,13 @@
     return lax.ppermute(array, "row", [(i, i ^ 1) for i in range(Z_HI * X * CORE)])
 
 
-def other_z(array):
-    return lax.ppermute(array, "col", [(i, (i + Y) % (Z_LO * Y)) for i in range(Z_LO * Y)])
+def neighbour(array, by):
+    pairs = [
+        (z * Y + y, z * Y + (y + (by if y % 2 == 0 else -by)) % Y)
+        for z in range(Z_LO)
+        for y in range(Y)
+    ]
+    return lax.ppermute(array, "col", pairs)
 
 
 def share(part, axis, groups=None):
@@ -40,33 +44,20 @@
     return lax.all_to_all(copies, axis, 0, 0, axis_index_groups=groups)
 
 
-def gather_noise(noise):
-    there = other_z(noise)
-    first = lax.axis_index("col") < Y
-    low, high = jnp.where(first, noise, there), jnp.where(first, there, noise)
-    half = noise.shape[1] // 2
-    halves = [
-        jnp.concatenate([low[:, k : k + half], high[:, k : k + half]], axis=1)
-        for k in (0, half)
-    ]
-    return share(jnp.stack(halves), "col", Y_GROUPS)
-
-
 def gather_data(data):
     row = lax.axis_index("row")
     z, x = row // (X * CORE), row // CORE % X
     up, down = along_z(data, 1), along_z(data, -1)
     far = along_z(up, 1)
-    plane = jnp.zeros((2, Z_LO) + data.shape, data.dtype)
+    plane = jnp.zeros((Z_HI,) + data.shape, data.dtype)
     for piece, by in ((data, 0), (up, 3), (down, 1), (far, 2)):
-        at = (z + by) % Z_HI
-        plane = lax.dynamic_update_slice(plane, piece[None, None], (at % 2, at // 2, 0, 0))
+        plane = lax.dynamic_update_slice(plane, piece[None], ((z + by) % Z_HI, 0, 0))
     up, down = along_x(plane, 1), along_x(plane, -1)
     far = along_x(up, 1)
-    whole = jnp.zeros((2, X, Z_LO) + data.shape, data.dtype)
+    whole = jnp.zeros((Z_HI, X) + data.shape, data.dtype)
     for piece, by in ((plane, 0), (up, 3), (down, 1), (far, 2)):
-        whole = lax.dynamic_update_slice(whole, piece[:, None], (0, (x + by) % X, 0, 0, 0))
-    return whole.reshape(-1, data.shape[1])
+        whole = lax.dynamic_update_slice(whole, piece[:, None], (0, (x + by) % X, 0, 0))
+    return whole
 
 
 def log_total(scores, dim, axis):
@@ -84,19 +75,24 @@
     cols_all = cols * lax.axis_size("col")
     core = lax.axis_index("row") % CORE
 
-    noise_all = gather_noise(noise)
+    noise_all = share(noise, "col")
     here = gather_data(data)
     there = other_core(here)
-    sq = jnp.sum(here.astype(jnp.float32) ** 2, axis=0)
+    sq = jnp.sum(here.astype(jnp.float32) ** 2, axis=(0, 1, 2))
     data_sq = sq + other_core(sq)
-    noise_sq = jnp.sum(noise_all.astype(jnp.float32) ** 2, axis=(0, 1, 3))
+    noise_sq = jnp.sum(noise_all.astype(jnp.float32) ** 2, axis=(0, 2))
 
     def half(which):
-        part = lax.dynamic_index_in_dim(noise_all, which, 1, keepdims=False)
+        size = noise.shape[1] // CORE
+        part = noise_all[:, :, which * size : (which + 1) * size]
+        part = jnp.concatenate([part[0::2], part[1::2]], axis=2)
         return part.transpose(1, 0, 2).reshape(rows, -1)
 
-    cross = jnp.dot(half(core), here, preferred_element_type=jnp.float32)
-    cross += jnp.dot(half(1 - core), there, preferred_element_type=jnp.float32)
+    first, second = half(0), half(1)
+    mine = jnp.where(core == 0, first, second)
+    others = jnp.where(core == 0, second, first)
+    cross = jnp.dot(mine, here.reshape(-1, cols), preferred_element_type=jnp.float32)
+    cross += jnp.dot(others, there.reshape(-1, cols), preferred_element_type=jnp.float32)
 
     unit = 1.0 / (width * EPS)
     logits = cross * (2.0 * unit)
@@ -119,16 +115,29 @@
     weights = (plan * ((rows_all / lift) * by_row)[:, None] * by_col[None, :]).astype(
         jnp.bfloat16
     )
-    contract = (((1,), (1,)), ((), ()))
-    terms = [
-        lax.dot_general(part, weights, contract, preferred_element_type=jnp.float32)
-        .astype(jnp.bfloat16)
-        .reshape(Z_LO * Y, -1, rows)
-        for part in (here, there)
+
+    def features(parity):
+        shape = (Z_HI, X // 2, 2, -1, cols)
+        a = lax.dynamic_index_in_dim(here.reshape(shape), parity, 2, keepdims=False)
+        b = lax.dynamic_index_in_dim(there.reshape(shape), parity, 2, keepdims=False)
+        both = [jnp.where(core == 0, a, b), jnp.where(core == 0, b, a)]
+        return jnp.stack(both, axis=2).reshape(Z_LO, -1, cols)
+
+    def terms(part):
+        contract = (((1,), (1,)), ((), ()))
+        return lax.dot_general(part, weights, contract, preferred_element_type=jnp.float32)
+
+    odd = lax.axis_index("col") % 2
+    away, kept = features(1 - odd), features(odd)
+    sums = [
+        (terms(kept[z]) + neighbour(terms(away[z]).astype(jnp.bfloat16), by)).astype(
+            jnp.bfloat16
+        )
+        for z, by in ((0, 1), (1, -1))
     ]
-    parts = lax.all_to_all(jnp.stack(terms, axis=1), "col", 0, 0, axis_index_groups=OWNERS)
+    sums = jnp.stack(sums).reshape(len(PARITIES[0]), -1, rows)
+    parts = lax.all_to_all(sums, "col", 0, 0, axis_index_groups=PARITIES)
     targets = jnp.sum(parts.astype(jnp.float32), axis=0).astype(jnp.bfloat16)
-    targets = jnp.where(core == 0, targets, targets[::-1]).reshape(-1, rows)
     return (targets, row_potential, col_potential)
 
 

time: 269 us -> 278 us (1.033)
  blocking collectives: 95.9 us -> 109 us
  starting transfers between devices: 46.7 us -> 57.2 us
  waiting for transfers between devices: 85.5 us -> 75.7 us
  matrix products: 12 us -> 7.45 us
  local copies, waits for them, and re-layouts: 11.2 us -> 8.41 us
    all_to_all x1 -> x0, waiting for transfers between devices: 51.3 us -> none  [local(): lax.all_to_all(jnp.stack(terms, axis=1), 'col', 0, 0, axis_index_groups=O...]
    all_to_all x0 -> x1, blocking collectives: none -> 31.1 us  [local(): parts = lax.all_to_all(sums, 'col', 0, 0, axis_index_groups=PARITIES)]
    all_to_all x7 -> x5, blocking collectives: 95.9 us -> 78 us  [share(): return lax.all_to_all(copies, axis, 0, 0, axis_index_groups=groups)]
    ppermute x3, waiting for transfers between devices: 7.63 us -> 23.8 us  [along_z(): return lax.ppermute(array, 'row', pairs)]
    all_to_all x2 -> x4, starting transfers between devices: 10.8 us -> 24.2 us  [share(): return lax.all_to_all(copies, axis, 0, 0, axis_index_groups=groups)]
    ppermute x3, waiting for transfers between devices: 8.65 us -> 18.2 us  [along_x(): return lax.ppermute(array, 'row', pairs)]
    ppermute x1 -> x2, waiting for transfers between devices: 4.37 us -> 12.7 us  [neighbour(): return lax.ppermute(array, 'col', pairs)]
    all_to_all x2 -> x4, waiting for transfers between devices: 12.7 us -> 19.8 us  [share(): return lax.all_to_all(copies, axis, 0, 0, axis_index_groups=groups)]
  transfers between devices with their start and end apart: 12 -> 14, of which waited for: 8 -> 10; matrix products, arithmetic and copies ran while one was open for 5% -> 4% of each run, Pallas kernels for 0% -> 0%
where the time goes in v3:
time: 278 us; the launch traced here: 274 us
  blocking collectives  109 us (39%)
  waiting for transfers between devices  75.7 us (27%)
  starting transfers between devices  57.2 us (21%)
  other arithmetic  14.9 us (5%)
  local copies, waits for them, and re-layouts  8.41 us (3%)
  matrix products  7.45 us (3%)
    all_to_all x5, blocking collectives, share(): return lax.all_to_all(copies, axis, 0, 0, axis_index_groups=groups)  78 us
    all_to_all x1, blocking collectives, local(): parts = lax.all_to_all(sums, 'col', 0, 0, axis_index_groups=PARITIES)  31.1 us
    all_to_all x4, starting transfers between devices, share(): return lax.all_to_all(copies, axis, 0, 0, axis_index_groups=groups)  24.2 us
    ppermute x3, waiting for transfers between devices, along_z(): return lax.ppermute(array, 'row', pairs)  23.8 us
    all_to_all x4, waiting for transfers between devices, share(): return lax.all_to_all(copies, axis, 0, 0, axis_index_groups=groups)  19.8 us
    ppermute x3, waiting for transfers between devices, along_x(): return lax.ppermute(array, 'row', pairs)  18.2 us
    ppermute x3, starting transfers between devices, along_z(): return lax.ppermute(array, 'row', pairs)  13.9 us
    ppermute x2, waiting for transfers between devices, neighbour(): return lax.ppermute(array, 'col', pairs)  12.7 us
  transfers between devices with their start and end apart: 14, of which 10 were waited for; matrix products, arithmetic and copies ran while one was open for 4% of the time, Pallas kernels for 0%

profile of v3, /device:TPU:6, one launch (start us, length us, event | category | flops | bytes accessed | tf_op | source)
XLA Modules:
  0.0 274.1 jit_solution(1106143219262681115)
XLA Ops:
  3.1 9.2 %all-to-all-start = ((bf16[16,512,128]{1,2,0:T(8,128)(2,1)}), bf16[16,512,128]{1,2,0:T(8,128)(2,1)}, u32[]{:S(2)}, u32[]{:S(2)}) async-start(bf16[16,512,128]{1,2,0:T(8,128)(2,1)} %broadcast_in_dim.48), calls=%async_computation | async-start | bytes 4194304 | tf_op jit(solution)/shard_map/all_to_all | solution.py:44
  12.4 10.0 %collective-permute-start.1 = (bf16[64,1024]{1,0:T(8,128)(2,1)S(1)}, bf16[64,1024]{1,0:T(8,128)(2,1)S(1)}, u32[]{:S(2)}, u32[]{:S(2)}) collective-permute-start(bf16[64,1024]{1,0:T(8,128)(2,1)S(1)} %copy-done.5), channel_id=1, source_target_pairs={{0,384},{16,400},{32,416},{48,432},{64,448},{80,464},{96,480},{112... | collective-permute-start | bytes 393224 | tf_op jit(solution)/shard_map/ppermute | solution.py:19
  22.4 1.9 collective-permute-start
  24.5 14.3 %collective-permute-done = bf16[64,1024]{1,0:T(8,128)(2,1)S(1)} collective-permute-done((bf16[64,1024]{1,0:T(8,128)(2,1)S(1)}, bf16[64,1024]{1,0:T(8,128)(2,1)S(1)}, u32[]{:S(2)}, u32[]{:S(2)}) %collective-permute-start) | collective-permute-done | bytes 131104 | tf_op jit(solution)/shard_map/ppermute | solution.py:19
  38.8 1.9 collective-permute-start.2
  40.8 9.5 %collective-permute-done.2 = bf16[64,1024]{1,0:T(8,128)(2,1)S(1)} collective-permute-done((bf16[64,1024]{1,0:T(8,128)(2,1)S(1)}, bf16[64,1024]{1,0:T(8,128)(2,1)S(1)}, u32[]{:S(2)}, u32[]{:S(2)}) %collective-permute-start.2) | collective-permute-done | bytes 131104 | tf_op jit(solution)/shard_map/ppermute | solution.py:19
  50.3 2.4 collective-permute-start.3
  52.7 3.5 %collective-permute-start.4 = (bf16[4,64,1024]{2,1,0:T(8,128)(2,1)S(1)}, bf16[4,64,1024]{2,1,0:T(8,128)(2,1)}, u32[]{:S(2)}, u32[]{:S(2)}) collective-permute-start(bf16[4,64,1024]{2,1,0:T(8,128)(2,1)S(1)} %bitcast_dynamic-update-slice_fusion.4), channel_id=1, source_target_pairs={{0,96},{16,112},{32,0},{48,16},{64,32},{80,48},{96,64},{112,80},{1... | collective-permute-start | bytes 1572872 | tf_op jit(solution)/shard_map/ppermute | solution.py:25
  56.3 9.1 %collective-permute-done.3 = bf16[4,64,1024]{2,1,0:T(8,128)(2,1)S(1)} collective-permute-done((bf16[4,64,1024]{2,1,0:T(8,128)(2,1)S(1)}, bf16[4,64,1024]{2,1,0:T(8,128)(2,1)S(1)}, u32[]{:S(2)}, u32[]{:S(2)}) %collective-permute-start.3) | collective-permute-done | bytes 524320 | tf_op jit(solution)/shard_map/ppermute | solution.py:25
  65.4 3.7 %collective-permute-start.5 = (bf16[4,64,1024]{2,1,0:T(8,128)(2,1)S(1)}, bf16[4,64,1024]{2,1,0:T(8,128)(2,1)S(1)}, u32[]{:S(2)}, u32[]{:S(2)}) collective-permute-start(bf16[4,64,1024]{2,1,0:T(8,128)(2,1)S(1)} %collective-permute-done.3), channel_id=1, source_target_pairs={{0,32},{16,48},{32,64},{48,80},{64,96},{80,112},{96,0},{112,16},{1... | collective-permute-start | bytes 1572872 | tf_op jit(solution)/shard_map/ppermute | solution.py:25
  70.6 9.1 %collective-permute-done.5 = bf16[4,64,1024]{2,1,0:T(8,128)(2,1)S(1)} collective-permute-done((bf16[4,64,1024]{2,1,0:T(8,128)(2,1)S(1)}, bf16[4,64,1024]{2,1,0:T(8,128)(2,1)S(1)}, u32[]{:S(2)}, u32[]{:S(2)}) %collective-permute-start.5) | collective-permute-done | bytes 524320 | tf_op jit(solution)/shard_map/ppermute | solution.py:25
  79.7 1.9 collective-permute-start.6
  82.1 2.4 collective-permute-start.7
  85.8 1.8 fusion.8
  88.2 3.0 %fusion.11 = f32[512,1024]{1,0:T(8,128)S(1)} fusion(bf16[512,1024]{0,1:T(8,128)(2,1)S(1)} %bitcast.67, bf16[1024,1024]{1,0:T(8,128)(2,1)} %bitcast.19), kind=kOutput, calls=%fused_computation.70 | convolution fusion | flops 1073741824 | bytes 5242880 | tf_op jit(solution)/shard_map/dot_general | solution.py:95
  93.1 27.4 %all_to_all.64 = f32[16,1,512]{2,1,0:T(1,128)S(1)} all-to-all(f32[16,1,512]{2,1,0:T(1,128)S(1)} %broadcast_in_dim.49), channel_id=1, replica_groups=mesh['row'=32,'col'=16] {'col'}, dimensions={0} | all-to-all | bytes 65536 | tf_op jit(solution)/shard_map/all_to_all | solution.py:44
  121.3 14.4 %all_to_all.65 = f32[32,1,1024]{2,1,0:T(1,128)S(1)} all-to-all(f32[32,1,1024]{2,1,0:T(1,128)S(1)} %broadcast_in_dim.50), channel_id=1, replica_groups=mesh['row'=32,'col'=16] {'row'}, dimensions={0} | all-to-all | bytes 262144 | tf_op jit(solution)/shard_map/all_to_all | solution.py:44
  136.4 11.2 %all_to_all.66 = f32[16,1,512]{2,1,0:T(1,128)S(1)} all-to-all(f32[16,1,512]{2,1,0:T(1,128)S(1)} %broadcast_in_dim.51), channel_id=1, replica_groups=mesh['row'=32,'col'=16] {'col'}, dimensions={0} | all-to-all | bytes 65536 | tf_op jit(solution)/shard_map/all_to_all | solution.py:44
  148.2 14.0 %all_to_all.67 = f32[32,1,1024]{2,1,0:T(1,128)S(1)} all-to-all(f32[32,1,1024]{2,1,0:T(1,128)S(1)} %broadcast_in_dim.52), channel_id=1, replica_groups=mesh['row'=32,'col'=16] {'row'}, dimensions={0} | all-to-all | bytes 262144 | tf_op jit(solution)/shard_map/all_to_all | solution.py:44
  163.0 11.1 %all_to_all.68 = f32[16,1,512]{2,1,0:T(1,128)S(1)} all-to-all(f32[16,1,512]{2,1,0:T(1,128)S(1)} %broadcast_in_dim.53), channel_id=1, replica_groups=mesh['row'=32,'col'=16] {'col'}, dimensions={0} | all-to-all | bytes 65536 | tf_op jit(solution)/shard_map/all_to_all | solution.py:44
  175.3 5.7 %all-to-all-start.6 = ((f32[32,1,1024]{2,1,0:T(1,128)}), f32[32,1,1024]{2,1,0:T(1,128)S(1)}, u32[]{:S(2)}, u32[]{:S(2)}) async-start(f32[32,1,1024]{2,1,0:T(1,128)} %broadcast_in_dim.54), calls=%async_computation.6 | async-start | bytes 262144 | tf_op jit(solution)/shard_map/all_to_all | solution.py:44
  181.1 8.9 %all-to-all-done.6 = f32[32,1,1024]{2,1,0:T(1,128)S(1)} async-done(((f32[32,1,1024]{2,1,0:T(1,128)}), f32[32,1,1024]{2,1,0:T(1,128)S(1)}, u32[]{:S(2)}, u32[]{:S(2)}) %all-to-all-start.6) | async-done | bytes 131104 | tf_op jit(solution)/shard_map/all_to_all | solution.py:44
  191.3 3.7 %all-to-all-start.7 = ((f32[16,1,512]{2,1,0:T(1,128)}), f32[16,1,512]{2,1,0:T(1,128)S(1)}, u32[]{:S(2)}, u32[]{:S(2)}) async-start(f32[16,1,512]{2,1,0:T(1,128)} %broadcast_in_dim.55), calls=%async_computation.7 | async-start | bytes 65536 | tf_op jit(solution)/shard_map/all_to_all | solution.py:44
  195.0 2.1 multiply_reduce_fusion
  197.1 6.2 %all-to-all-done.7 = f32[16,1,512]{2,1,0:T(1,128)S(1)} async-done(((f32[16,1,512]{2,1,0:T(1,128)}), f32[16,1,512]{2,1,0:T(1,128)S(1)}, u32[]{:S(2)}, u32[]{:S(2)}) %all-to-all-start.7) | async-done | bytes 32800 | tf_op jit(solution)/shard_map/all_to_all | solution.py:44
  205.2 5.6 %all-to-all-start.8 = ((f32[32,1,1024]{2,1,0:T(1,128)}), f32[32,1,1024]{2,1,0:T(1,128)S(1)}, u32[]{:S(2)}, u32[]{:S(2)}) async-start(f32[32,1,1024]{2,1,0:T(1,128)} %broadcast_in_dim.56), calls=%async_computation.8 | async-start | bytes 262144 | tf_op jit(solution)/shard_map/all_to_all | solution.py:44
  210.8 2.5 broadcast_select_fusion.3
  215.0 4.7 %all-to-all-done.8 = f32[32,1,1024]{2,1,0:T(1,128)S(1)} async-done(((f32[32,1,1024]{2,1,0:T(1,128)}), f32[32,1,1024]{2,1,0:T(1,128)S(1)}, u32[]{:S(2)}, u32[]{:S(2)}) %all-to-all-start.8) | async-done | bytes 131104 | tf_op jit(solution)/shard_map/all_to_all | solution.py:44
  221.8 2.9 %collective-permute-start.9 = (bf16[512,512]{1,0:T(8,128)(2,1)S(1)}, bf16[512,512]{1,0:T(8,128)(2,1)S(1)}, u32[]{:S(2)}, u32[]{:S(2)}) collective-permute-start(bf16[512,512]{1,0:T(8,128)(2,1)S(1)} %convolution_convert_fusion), channel_id=1, source_target_pairs={{0,7},{1,2},{2,1},{3,4},{4,3},{5,6},{6,5},{7,0},{8,15},{9,10},{10,... | collective-permute-start | bytes 1572872 | tf_op jit(solution)/shard_map/ppermute | solution.py:38
  225.5 2.4 collective-permute-start.8
  227.9 11.3 %collective-permute-done.9 = bf16[512,512]{1,0:T(8,128)(2,1)S(1)} collective-permute-done((bf16[512,512]{1,0:T(8,128)(2,1)S(1)}, bf16[512,512]{1,0:T(8,128)(2,1)S(1)}, u32[]{:S(2)}, u32[]{:S(2)}) %collective-permute-start.9) | collective-permute-done | bytes 524320 | tf_op jit(solution)/shard_map/ppermute | solution.py:38
  242.2 31.1 %all_to_all.69 = bf16[8,128,512]{2,1,0:T(8,128)(2,1)S(1)} all-to-all(bf16[8,128,512]{2,1,0:T(8,128)(2,1)S(1)} %bitcast.68), channel_id=1, replica_groups={{0,2,4,6,8,10,12,14},{1,3,5,7,9,11,13,15},{16,18,20,22,24,26,28,30},{17..., dimensions={0} | all-to-all | bytes 2097152 | tf_op jit(solution)/shard_map/all_to_all | solution.py:139
  (80 shorter events, 24.1 us)
Async XLA Ops:
  3.1 9.2 %copy-start.5 = (bf16[64,1024]{1,0:T(8,128)(2,1)S(1)}, bf16[64,1024]{1,0:T(8,128)(2,1)}, u32[]{:S(2)}) copy-start(bf16[64,1024]{1,0:T(8,128)(2,1)} %param.3) | copy-start | bytes 393220
  3.1 82.6 %all-to-all-start = ((bf16[16,512,128]{1,2,0:T(8,128)(2,1)}), bf16[16,512,128]{1,2,0:T(8,128)(2,1)}, u32[]{:S(2)}, u32[]{:S(2)}) async-start(bf16[16,512,128]{1,2,0:T(8,128)(2,1)} %broadcast_in_dim.48), calls=%async_computation | async-start | bytes 4194304 | tf_op jit(solution)/shard_map/all_to_all | solution.py:44
  12.4 28.4 %collective-permute-start.1 = (bf16[64,1024]{1,0:T(8,128)(2,1)S(1)}, bf16[64,1024]{1,0:T(8,128)(2,1)S(1)}, u32[]{:S(2)}, u32[]{:S(2)}) collective-permute-start(bf16[64,1024]{1,0:T(8,128)(2,1)S(1)} %copy-done.5), channel_id=1, source_target_pairs={{0,384},{16,400},{32,416},{48,432},{64,448},{80,464},{96,480},{112... | collective-permute-start | bytes 393224 | tf_op jit(solution)/shard_map/ppermute | solution.py:19
  22.4 16.4 %collective-permute-start = (bf16[64,1024]{1,0:T(8,128)(2,1)S(1)}, bf16[64,1024]{1,0:T(8,128)(2,1)S(1)}, u32[]{:S(2)}, u32[]{:S(2)}) collective-permute-start(bf16[64,1024]{1,0:T(8,128)(2,1)S(1)} %copy-done.5), channel_id=1, source_target_pairs={{0,128},{16,144},{32,160},{48,176},{64,192},{80,208},{96,224},{112... | collective-permute-start | bytes 393224 | tf_op jit(solution)/shard_map/ppermute | solution.py:19
  38.8 11.5 %collective-permute-start.2 = (bf16[64,1024]{1,0:T(8,128)(2,1)S(1)}, bf16[64,1024]{1,0:T(8,128)(2,1)S(1)}, u32[]{:S(2)}, u32[]{:S(2)}) collective-permute-start(bf16[64,1024]{1,0:T(8,128)(2,1)S(1)} %collective-permute-done), channel_id=1, source_target_pairs={{0,128},{16,144},{32,160},{48,176},{64,192},{80,208},{96,224},{112... | collective-permute-start | bytes 393224 | tf_op jit(solution)/shard_map/ppermute | solution.py:19
  50.3 15.1 %collective-permute-start.3 = (bf16[4,64,1024]{2,1,0:T(8,128)(2,1)S(1)}, bf16[4,64,1024]{2,1,0:T(8,128)(2,1)S(1)}, u32[]{:S(2)}, u32[]{:S(2)}) collective-permute-start(bf16[4,64,1024]{2,1,0:T(8,128)(2,1)S(1)} %bitcast_dynamic-update-slice_fusion.4), channel_id=1, source_target_pairs={{0,32},{16,48},{32,64},{48,80},{64,96},{80,112},{96,0},{112,16},{1... | collective-permute-start | bytes 1572872 | tf_op jit(solution)/shard_map/ppermute | solution.py:25
  52.7 16.7 %collective-permute-start.4 = (bf16[4,64,1024]{2,1,0:T(8,128)(2,1)S(1)}, bf16[4,64,1024]{2,1,0:T(8,128)(2,1)}, u32[]{:S(2)}, u32[]{:S(2)}) collective-permute-start(bf16[4,64,1024]{2,1,0:T(8,128)(2,1)S(1)} %bitcast_dynamic-update-slice_fusion.4), channel_id=1, source_target_pairs={{0,96},{16,112},{32,0},{48,16},{64,32},{80,48},{96,64},{112,80},{1... | collective-permute-start | bytes 1572872 | tf_op jit(solution)/shard_map/ppermute | solution.py:25
  65.4 14.2 %collective-permute-start.5 = (bf16[4,64,1024]{2,1,0:T(8,128)(2,1)S(1)}, bf16[4,64,1024]{2,1,0:T(8,128)(2,1)S(1)}, u32[]{:S(2)}, u32[]{:S(2)}) collective-permute-start(bf16[4,64,1024]{2,1,0:T(8,128)(2,1)S(1)} %collective-permute-done.3), channel_id=1, source_target_pairs={{0,32},{16,48},{32,64},{48,80},{64,96},{80,112},{96,0},{112,16},{1... | collective-permute-start | bytes 1572872 | tf_op jit(solution)/shard_map/ppermute | solution.py:25
  79.7 7.9 %copy-start = (bf16[4,4,64,1024]{3,2,1,0:T(8,128)(2,1)}, bf16[4,4,64,1024]{3,2,1,0:T(8,128)(2,1)S(1)}, u32[]{:S(2)}) copy-start(bf16[4,4,64,1024]{3,2,1,0:T(8,128)(2,1)S(1)} %bitcast_dynamic-update-slice_fusion.3) | copy-start | bytes 6291460
  79.7 8.5 %collective-permute-start.6 = (bf16[4,4,64,1024]{3,2,1,0:T(8,128)(2,1)S(1)}, bf16[4,4,64,1024]{3,2,1,0:T(8,128)(2,1)}, u32[]{:S(2)}, u32[]{:S(2)}) collective-permute-start(bf16[4,4,64,1024]{3,2,1,0:T(8,128)(2,1)S(1)} %bitcast_dynamic-update-slice_fusion.3), channel_id=1, source_target_pairs={{0,16},{16,0},{32,48},{48,32},{64,80},{80,64},{96,112},{112,96},{1... | collective-permute-start | bytes 6291464 | tf_op jit(solution)/shard_map/ppermute | solution.py:29
  82.1 3.7 %collective-permute-start.7 = (f32[1024]{0:T(1024)S(1)}, f32[1024]{0:T(1024)S(1)}, u32[]{:S(2)}, u32[]{:S(2)}) collective-permute-start(f32[1024]{0:T(1024)S(1)} %multiply_reduce_fusion.1), channel_id=1, source_target_pairs={{0,16},{16,0},{32,48},{48,32},{64,80},{80,64},{96,112},{112,96},{1... | collective-permute-start | bytes 12296 | tf_op jit(solution)/shard_map/ppermute | solution.py:29
  88.2 3.0 %copy-start.1 = (bf16[4,4,64,1024]{3,2,1,0:T(8,128)(2,1)S(1)}, bf16[4,4,64,1024]{3,2,1,0:T(8,128)(2,1)}, u32[]{:S(2)}) copy-start(bf16[4,4,64,1024]{3,2,1,0:T(8,128)(2,1)} %copy-done) | copy-start | bytes 6291460
  175.3 14.6 %all-to-all-start.6 = ((f32[32,1,1024]{2,1,0:T(1,128)}), f32[32,1,1024]{2,1,0:T(1,128)S(1)}, u32[]{:S(2)}, u32[]{:S(2)}) async-start(f32[32,1,1024]{2,1,0:T(1,128)} %broadcast_in_dim.54), calls=%async_computation.6 | async-start | bytes 262144 | tf_op jit(solution)/shard_map/all_to_all | solution.py:44
  191.3 12.0 %all-to-all-start.7 = ((f32[16,1,512]{2,1,0:T(1,128)}), f32[16,1,512]{2,1,0:T(1,128)S(1)}, u32[]{:S(2)}, u32[]{:S(2)}) async-start(f32[16,1,512]{2,1,0:T(1,128)} %broadcast_in_dim.55), calls=%async_computation.7 | async-start | bytes 65536 | tf_op jit(solution)/shard_map/all_to_all | solution.py:44
  205.2 14.5 %all-to-all-start.8 = ((f32[32,1,1024]{2,1,0:T(1,128)}), f32[32,1,1024]{2,1,0:T(1,128)S(1)}, u32[]{:S(2)}, u32[]{:S(2)}) async-start(f32[32,1,1024]{2,1,0:T(1,128)} %broadcast_in_dim.56), calls=%async_computation.8 | async-start | bytes 262144 | tf_op jit(solution)/shard_map/all_to_all | solution.py:44
  219.8 1.2 copy-start.4
  220.9 3.8 %copy-start.3 = (bf16[2,2,2,64,1024]{4,3,2,1,0:T(8,128)(2,1)S(1)}, bf16[2,2,2,64,1024]{4,3,2,1,0:T(8,128)(2,1)}, u32[]{:S(2)}) copy-start(bf16[2,2,2,64,1024]{4,3,2,1,0:T(8,128)(2,1)} %get-tuple-element.7) | copy-start | bytes 3145732
  221.7 17.5 %copy-start.2 = (bf16[2,2,2,64,1024]{4,3,2,1,0:T(8,128)(2,1)S(1)}, bf16[2,2,2,64,1024]{4,3,2,1,0:T(8,128)(2,1)}, u32[]{:S(2)}) copy-start(bf16[2,2,2,64,1024]{4,3,2,1,0:T(8,128)(2,1)} %get-tuple-element.26) | copy-start | bytes 3145732
  221.8 17.5 %collective-permute-start.9 = (bf16[512,512]{1,0:T(8,128)(2,1)S(1)}, bf16[512,512]{1,0:T(8,128)(2,1)S(1)}, u32[]{:S(2)}, u32[]{:S(2)}) collective-permute-start(bf16[512,512]{1,0:T(8,128)(2,1)S(1)} %convolution_convert_fusion), channel_id=1, source_target_pairs={{0,7},{1,2},{2,1},{3,4},{4,3},{5,6},{6,5},{7,0},{8,15},{9,10},{10,... | collective-permute-start | bytes 1572872 | tf_op jit(solution)/shard_map/ppermute | solution.py:38
  225.5 15.8 %collective-permute-start.8 = (bf16[512,512]{1,0:T(8,128)(2,1)S(1)}, bf16[512,512]{1,0:T(8,128)(2,1)S(1)}, u32[]{:S(2)}, u32[]{:S(2)}) collective-permute-start(bf16[512,512]{1,0:T(8,128)(2,1)S(1)} %convolution_convert_fusion.1), channel_id=1, source_target_pairs={{0,1},{1,0},{2,3},{3,2},{4,5},{5,4},{6,7},{7,6},{8,9},{9,8},{10,11... | collective-permute-start | bytes 1572872 | tf_op jit(solution)/shard_map/ppermute | solution.py:38

commit v4 on v3

--- a/solution.py
+++ b/solution.py
@@ -44,20 +44,26 @@
     return lax.all_to_all(copies, axis, 0, 0, axis_index_groups=groups)
 
 
-def gather_data(data):
-    row = lax.axis_index("row")
+def gather(noise, data):
+    row, odd = lax.axis_index("row"), lax.axis_index("col") % 2
     z, x = row // (X * CORE), row // CORE % X
-    up, down = along_z(data, 1), along_z(data, -1)
-    far = along_z(up, 1)
+    same = share(noise, "col", PARITIES)
+    up, down, far = along_z(data, 1), along_z(data, -1), along_z(data, 2)
     plane = jnp.zeros((Z_HI,) + data.shape, data.dtype)
     for piece, by in ((data, 0), (up, 3), (down, 1), (far, 2)):
         plane = lax.dynamic_update_slice(plane, piece[None], ((z + by) % Z_HI, 0, 0))
     up, down = along_x(plane, 1), along_x(plane, -1)
+    up, same = lax.optimization_barrier((up, same))
     far = along_x(up, 1)
+    n = len(PARITIES[0])
+    above, below = neighbour(same[: n // 2], 1), neighbour(same[n // 2 :], -1)
+    far, above, below = lax.optimization_barrier((far, above, below))
     whole = jnp.zeros((Z_HI, X) + data.shape, data.dtype)
     for piece, by in ((plane, 0), (up, 3), (down, 1), (far, 2)):
         whole = lax.dynamic_update_slice(whole, piece[:, None], (0, (x + by) % X, 0, 0))
-    return whole
+    other = jnp.concatenate([above, below])
+    by_parity = [jnp.where(odd == 0, same, other), jnp.where(odd == 0, other, same)]
+    return by_parity, whole
 
 
 def log_total(scores, dim, axis):
@@ -75,17 +81,16 @@
     cols_all = cols * lax.axis_size("col")
     core = lax.axis_index("row") % CORE
 
-    noise_all = share(noise, "col")
-    here = gather_data(data)
+    by_parity, here = gather(noise, data)
     there = other_core(here)
     sq = jnp.sum(here.astype(jnp.float32) ** 2, axis=(0, 1, 2))
     data_sq = sq + other_core(sq)
-    noise_sq = jnp.sum(noise_all.astype(jnp.float32) ** 2, axis=(0, 2))
+    noise_sq = sum(jnp.sum(part.astype(jnp.float32) ** 2, axis=(0, 2)) for part in by_parity)
 
     def half(which):
         size = noise.shape[1] // CORE
-        part = noise_all[:, :, which * size : (which + 1) * size]
-        part = jnp.concatenate([part[0::2], part[1::2]], axis=2)
+        part = [p[:, :, which * size : (which + 1) * size] for p in by_parity]
+        part = jnp.concatenate(part, axis=2)
         return part.transpose(1, 0, 2).reshape(rows, -1)
 
     first, second = half(0), half(1)

time: 278 us -> 265 us (0.953)
  waiting for transfers between devices: 75.7 us -> 54.9 us
  starting transfers between devices: 57.2 us -> 61.9 us
  local copies, waits for them, and re-layouts: 8.41 us -> 12 us
    ppermute x3, waiting for transfers between devices: 23.8 us -> 10.9 us  [along_z(): return lax.ppermute(array, 'row', pairs)]
    ppermute x3, waiting for transfers between devices: 18.2 us -> 9.32 us  [along_x(): return lax.ppermute(array, 'row', pairs)]
    ppermute x2 -> x4, waiting for transfers between devices: 12.7 us -> 21.5 us  [neighbour(): return lax.ppermute(array, 'col', pairs)]
    ppermute x2 -> x4, starting transfers between devices: 5.32 us -> 13.4 us  [neighbour(): return lax.ppermute(array, 'col', pairs)]
    all_to_all x4 -> x3, waiting for transfers between devices: 19.8 us -> 13.2 us  [share(): return lax.all_to_all(copies, axis, 0, 0, axis_index_groups=groups)]
    all_to_all x4 -> x3, starting transfers between devices: 24.2 us -> 18 us  [share(): return lax.all_to_all(copies, axis, 0, 0, axis_index_groups=groups)]
    dynamic_update_slice x8, local copies, waits for them, and re-layouts: 1.28 us -> 5.92 us  [the longest x4 3.29 us: gather(): lax.dynamic_update_slice(whole, piece[:, None], (0, (x + by) % X, 0, 0))]
    ppermute x3, starting transfers between devices: 13.9 us -> 18 us  [along_z(): return lax.ppermute(array, 'row', pairs)]
  transfers between devices with their start and end apart: 14 -> 15, of which waited for: 10 -> 8; matrix products, arithmetic and copies ran while one was open for 4% -> 6% of each run, Pallas kernels for 0% -> 0%
where the time goes in v4:
time: 265 us; the launch traced here: 261 us
  blocking collectives  110 us (42%)
  starting transfers between devices  61.9 us (23%)
  waiting for transfers between devices  54.9 us (21%)
  other arithmetic  13.5 us (5%)
  local copies, waits for them, and re-layouts  12 us (5%)
  matrix products  7.45 us (3%)
    all_to_all x6, blocking collectives, share(): return lax.all_to_all(copies, axis, 0, 0, axis_index_groups=groups)  79.5 us
    all_to_all x1, blocking collectives, local(): parts = lax.all_to_all(sums, 'col', 0, 0, axis_index_groups=PARITIES)  30.1 us
    ppermute x4, waiting for transfers between devices, neighbour(): return lax.ppermute(array, 'col', pairs)  21.5 us
    all_to_all x3, starting transfers between devices, share(): return lax.all_to_all(copies, axis, 0, 0, axis_index_groups=groups)  18 us
    ppermute x3, starting transfers between devices, along_z(): return lax.ppermute(array, 'row', pairs)  18 us
    ppermute x4, starting transfers between devices, neighbour(): return lax.ppermute(array, 'col', pairs)  13.4 us
    all_to_all x3, waiting for transfers between devices, share(): return lax.all_to_all(copies, axis, 0, 0, axis_index_groups=groups)  13.2 us
    ppermute x3, waiting for transfers between devices, along_z(): return lax.ppermute(array, 'row', pairs)  10.9 us
  transfers between devices with their start and end apart: 15, of which 8 were waited for; matrix products, arithmetic and copies ran while one was open for 6% of the time, Pallas kernels for 0%

profile of v4, /device:TPU:6, one launch (start us, length us, event | category | flops | bytes accessed | tf_op | source)
XLA Modules:
  0.0 260.7 jit_solution(1733678731058204013)
XLA Ops:
  2.8 8.9 %all-to-all-start = ((bf16[8,512,128]{1,2,0:T(8,128)(2,1)}), bf16[8,512,128]{1,2,0:T(8,128)(2,1)S(1)}, u32[]{:S(2)}, u32[]{:S(2)}) async-start(bf16[8,512,128]{1,2,0:T(8,128)(2,1)} %broadcast_in_dim.45), calls=%async_computation | async-start | bytes 2097152 | tf_op jit(solution)/shard_map/all_to_all | solution.py:44
  11.7 6.1 %collective-permute-start = (bf16[64,1024]{1,0:T(8,128)(2,1)S(1)}, bf16[64,1024]{1,0:T(8,128)(2,1)S(1)}, u32[]{:S(2)}, u32[]{:S(2)}) collective-permute-start(bf16[64,1024]{1,0:T(8,128)(2,1)S(1)} %copy-done.9), channel_id=1, source_target_pairs={{0,128},{16,144},{32,160},{48,176},{64,192},{80,208},{96,224},{112... | collective-permute-start | bytes 393224 | tf_op jit(solution)/shard_map/ppermute | solution.py:19
  17.8 8.2 %collective-permute-start.2 = (bf16[64,1024]{1,0:T(8,128)(2,1)S(1)}, bf16[64,1024]{1,0:T(8,128)(2,1)S(1)}, u32[]{:S(2)}, u32[]{:S(2)}) collective-permute-start(bf16[64,1024]{1,0:T(8,128)(2,1)S(1)} %copy-done.9), channel_id=1, source_target_pairs={{0,256},{16,272},{32,288},{48,304},{64,320},{80,336},{96,352},{112... | collective-permute-start | bytes 393224 | tf_op jit(solution)/shard_map/ppermute | solution.py:19
  26.0 3.7 %collective-permute-start.1 = (bf16[64,1024]{1,0:T(8,128)(2,1)S(1)}, bf16[64,1024]{1,0:T(8,128)(2,1)S(1)}, u32[]{:S(2)}, u32[]{:S(2)}) collective-permute-start(bf16[64,1024]{1,0:T(8,128)(2,1)S(1)} %copy-done.9), channel_id=1, source_target_pairs={{0,384},{16,400},{32,416},{48,432},{64,448},{80,464},{96,480},{112... | collective-permute-start | bytes 393224 | tf_op jit(solution)/shard_map/ppermute | solution.py:19
  32.0 10.9 %collective-permute-done.1 = bf16[64,1024]{1,0:T(8,128)(2,1)S(1)} collective-permute-done((bf16[64,1024]{1,0:T(8,128)(2,1)S(1)}, bf16[64,1024]{1,0:T(8,128)(2,1)S(1)}, u32[]{:S(2)}, u32[]{:S(2)}) %collective-permute-start.1) | collective-permute-done | bytes 131104 | tf_op jit(solution)/shard_map/ppermute | solution.py:19
  44.2 2.4 collective-permute-start.3
  46.6 3.5 %collective-permute-start.4 = (bf16[4,64,1024]{2,1,0:T(8,128)(2,1)}, bf16[4,64,1024]{2,1,0:T(8,128)(2,1)}, u32[]{:S(2)}, u32[]{:S(2)}) collective-permute-start(bf16[4,64,1024]{2,1,0:T(8,128)(2,1)} %bitcast_dynamic-update-slice_fusion.4), channel_id=1, source_target_pairs={{0,96},{16,112},{32,0},{48,16},{64,32},{80,48},{96,64},{112,80},{1... | collective-permute-start | bytes 1572872 | tf_op jit(solution)/shard_map/ppermute | solution.py:25
  50.1 9.3 %collective-permute-done.3 = bf16[4,64,1024]{2,1,0:T(8,128)(2,1)} collective-permute-done((bf16[4,64,1024]{2,1,0:T(8,128)(2,1)}, bf16[4,64,1024]{2,1,0:T(8,128)(2,1)}, u32[]{:S(2)}, u32[]{:S(2)}) %collective-permute-start.3) | collective-permute-done | bytes 524320 | tf_op jit(solution)/shard_map/ppermute | solution.py:25
  59.4 2.4 collective-permute-start.5
  61.9 6.1 %collective-permute-start.7 = (bf16[4,512,128]{1,2,0:T(8,128)(2,1)S(1)}, bf16[4,512,128]{1,2,0:T(8,128)(2,1)S(1)}, u32[]{:S(2)}, u32[]{:S(2)}) collective-permute-start(bf16[4,512,128]{1,2,0:T(8,128)(2,1)S(1)} %get-tuple-element.33), channel_id=1, source_target_pairs={{0,7},{1,2},{2,1},{3,4},{4,3},{5,6},{6,5},{7,0},{8,15},{9,10},{10,... | collective-permute-start | bytes 1572872 | tf_op jit(solution)/shard_map/ppermute | solution.py:38
  68.0 1.9 collective-permute-start.6
  73.5 5.4 %collective-permute-done.7 = bf16[4,512,128]{1,2,0:T(8,128)(2,1)S(1)} collective-permute-done((bf16[4,512,128]{1,2,0:T(8,128)(2,1)S(1)}, bf16[4,512,128]{1,2,0:T(8,128)(2,1)S(1)}, u32[]{:S(2)}, u32[]{:S(2)}) %collective-permute-start.7) | collective-permute-done | bytes 524320 | tf_op jit(solution)/shard_map/ppermute | solution.py:38
  79.0 3.4 %collective-permute-done.6 = bf16[4,512,128]{1,2,0:T(8,128)(2,1)S(1)} collective-permute-done((bf16[4,512,128]{1,2,0:T(8,128)(2,1)S(1)}, bf16[4,512,128]{1,2,0:T(8,128)(2,1)S(1)}, u32[]{:S(2)}, u32[]{:S(2)}) %collective-permute-start.6) | collective-permute-done | bytes 524320 | tf_op jit(solution)/shard_map/ppermute | solution.py:38
  83.2 1.9 collective-permute-start.8
  85.6 2.4 collective-permute-start.9
  89.4 3.0 %fusion.11 = f32[512,1024]{1,0:T(8,128)S(1)} fusion(bf16[512,1024]{0,1:T(8,128)(2,1)S(1)} %bitcast.67, bf16[1024,1024]{1,0:T(8,128)(2,1)} %bitcast.19), kind=kOutput, calls=%fused_computation.75 | convolution fusion | flops 1073741824 | bytes 5242880 | tf_op jit(solution)/shard_map/dot_general | solution.py:100
  94.4 14.4 %all_to_all.64 = f32[16,1,512]{2,1,0:T(1,128)S(1)} all-to-all(f32[16,1,512]{2,1,0:T(1,128)S(1)} %broadcast_in_dim.49), channel_id=1, replica_groups=mesh['row'=32,'col'=16] {'col'}, dimensions={0} | all-to-all | bytes 65536 | tf_op jit(solution)/shard_map/all_to_all | solution.py:44
  109.6 15.2 %all_to_all.65 = f32[32,1,1024]{2,1,0:T(1,128)S(1)} all-to-all(f32[32,1,1024]{2,1,0:T(1,128)S(1)} %broadcast_in_dim.50), channel_id=1, replica_groups=mesh['row'=32,'col'=16] {'row'}, dimensions={0} | all-to-all | bytes 262144 | tf_op jit(solution)/shard_map/all_to_all | solution.py:44
  125.5 11.1 %all_to_all.66 = f32[16,1,512]{2,1,0:T(1,128)S(1)} all-to-all(f32[16,1,512]{2,1,0:T(1,128)S(1)} %broadcast_in_dim.51), channel_id=1, replica_groups=mesh['row'=32,'col'=16] {'col'}, dimensions={0} | all-to-all | bytes 65536 | tf_op jit(solution)/shard_map/all_to_all | solution.py:44
  137.2 13.9 %all_to_all.67 = f32[32,1,1024]{2,1,0:T(1,128)S(1)} all-to-all(f32[32,1,1024]{2,1,0:T(1,128)S(1)} %broadcast_in_dim.52), channel_id=1, replica_groups=mesh['row'=32,'col'=16] {'row'}, dimensions={0} | all-to-all | bytes 262144 | tf_op jit(solution)/shard_map/all_to_all | solution.py:44
  151.9 11.1 %all_to_all.68 = f32[16,1,512]{2,1,0:T(1,128)S(1)} all-to-all(f32[16,1,512]{2,1,0:T(1,128)S(1)} %broadcast_in_dim.53), channel_id=1, replica_groups=mesh['row'=32,'col'=16] {'col'}, dimensions={0} | all-to-all | bytes 65536 | tf_op jit(solution)/shard_map/all_to_all | solution.py:44
  163.7 13.9 %all_to_all.69 = f32[32,1,1024]{2,1,0:T(1,128)S(1)} all-to-all(f32[32,1,1024]{2,1,0:T(1,128)S(1)} %broadcast_in_dim.54), channel_id=1, replica_groups=mesh['row'=32,'col'=16] {'row'}, dimensions={0} | all-to-all | bytes 262144 | tf_op jit(solution)/shard_map/all_to_all | solution.py:44
  178.9 3.5 %all-to-all-start.7 = ((f32[16,1,512]{2,1,0:T(1,128)}), f32[16,1,512]{2,1,0:T(1,128)S(1)}, u32[]{:S(2)}, u32[]{:S(2)}) async-start(f32[16,1,512]{2,1,0:T(1,128)} %broadcast_in_dim.55), calls=%async_computation.7 | async-start | bytes 65536 | tf_op jit(solution)/shard_map/all_to_all | solution.py:44
  182.4 8.5 %all-to-all-done.7 = f32[16,1,512]{2,1,0:T(1,128)S(1)} async-done(((f32[16,1,512]{2,1,0:T(1,128)}), f32[16,1,512]{2,1,0:T(1,128)S(1)}, u32[]{:S(2)}, u32[]{:S(2)}) %all-to-all-start.7) | async-done | bytes 32800 | tf_op jit(solution)/shard_map/all_to_all | solution.py:44
  192.8 5.6 %all-to-all-start.8 = ((f32[32,1,1024]{2,1,0:T(1,128)}), f32[32,1,1024]{2,1,0:T(1,128)S(1)}, u32[]{:S(2)}, u32[]{:S(2)}) async-start(f32[32,1,1024]{2,1,0:T(1,128)} %broadcast_in_dim.56), calls=%async_computation.8 | async-start | bytes 262144 | tf_op jit(solution)/shard_map/all_to_all | solution.py:44
  198.4 2.5 broadcast_select_fusion.5
  200.8 1.7 fusion
  202.6 4.7 %all-to-all-done.8 = f32[32,1,1024]{2,1,0:T(1,128)S(1)} async-done(((f32[32,1,1024]{2,1,0:T(1,128)}), f32[32,1,1024]{2,1,0:T(1,128)S(1)}, u32[]{:S(2)}, u32[]{:S(2)}) %all-to-all-start.8) | async-done | bytes 131104 | tf_op jit(solution)/shard_map/all_to_all | solution.py:44
  209.3 2.9 %collective-permute-start.11 = (bf16[512,512]{1,0:T(8,128)(2,1)S(1)}, bf16[512,512]{1,0:T(8,128)(2,1)S(1)}, u32[]{:S(2)}, u32[]{:S(2)}) collective-permute-start(bf16[512,512]{1,0:T(8,128)(2,1)S(1)} %convolution_convert_fusion), channel_id=1, source_target_pairs={{0,7},{1,2},{2,1},{3,4},{4,3},{5,6},{6,5},{7,0},{8,15},{9,10},{10,... | collective-permute-start | bytes 1572872 | tf_op jit(solution)/shard_map/ppermute | solution.py:38
  213.1 2.4 collective-permute-start.10
  215.5 11.3 %collective-permute-done.11 = bf16[512,512]{1,0:T(8,128)(2,1)S(1)} collective-permute-done((bf16[512,512]{1,0:T(8,128)(2,1)S(1)}, bf16[512,512]{1,0:T(8,128)(2,1)S(1)}, u32[]{:S(2)}, u32[]{:S(2)}) %collective-permute-start.11) | collective-permute-done | bytes 524320 | tf_op jit(solution)/shard_map/ppermute | solution.py:38
  229.8 30.1 %all_to_all.70 = bf16[8,128,512]{2,1,0:T(8,128)(2,1)S(1)} all-to-all(bf16[8,128,512]{2,1,0:T(8,128)(2,1)S(1)} %bitcast.68), channel_id=1, replica_groups={{0,2,4,6,8,10,12,14},{1,3,5,7,9,11,13,15},{16,18,20,22,24,26,28,30},{17..., dimensions={0} | all-to-all | bytes 2097152 | tf_op jit(solution)/shard_map/all_to_all | solution.py:144
  (93 shorter events, 27.1 us)
Async XLA Ops:
  0.6 11.1 %copy-start.9 = (bf16[64,1024]{1,0:T(8,128)(2,1)S(1)}, bf16[64,1024]{1,0:T(8,128)(2,1)}, u32[]{:S(2)}) copy-start(bf16[64,1024]{1,0:T(8,128)(2,1)} %param.3) | copy-start | bytes 393220
  2.8 56.7 %all-to-all-start = ((bf16[8,512,128]{1,2,0:T(8,128)(2,1)}), bf16[8,512,128]{1,2,0:T(8,128)(2,1)S(1)}, u32[]{:S(2)}, u32[]{:S(2)}) async-start(bf16[8,512,128]{1,2,0:T(8,128)(2,1)} %broadcast_in_dim.45), calls=%async_computation | async-start | bytes 2097152 | tf_op jit(solution)/shard_map/all_to_all | solution.py:44
  11.7 19.6 %collective-permute-start = (bf16[64,1024]{1,0:T(8,128)(2,1)S(1)}, bf16[64,1024]{1,0:T(8,128)(2,1)S(1)}, u32[]{:S(2)}, u32[]{:S(2)}) collective-permute-start(bf16[64,1024]{1,0:T(8,128)(2,1)S(1)} %copy-done.9), channel_id=1, source_target_pairs={{0,128},{16,144},{32,160},{48,176},{64,192},{80,208},{96,224},{112... | collective-permute-start | bytes 393224 | tf_op jit(solution)/shard_map/ppermute | solution.py:19
  17.8 25.7 %collective-permute-start.2 = (bf16[64,1024]{1,0:T(8,128)(2,1)S(1)}, bf16[64,1024]{1,0:T(8,128)(2,1)S(1)}, u32[]{:S(2)}, u32[]{:S(2)}) collective-permute-start(bf16[64,1024]{1,0:T(8,128)(2,1)S(1)} %copy-done.9), channel_id=1, source_target_pairs={{0,256},{16,272},{32,288},{48,304},{64,320},{80,336},{96,352},{112... | collective-permute-start | bytes 393224 | tf_op jit(solution)/shard_map/ppermute | solution.py:19
  26.0 16.8 %collective-permute-start.1 = (bf16[64,1024]{1,0:T(8,128)(2,1)S(1)}, bf16[64,1024]{1,0:T(8,128)(2,1)S(1)}, u32[]{:S(2)}, u32[]{:S(2)}) collective-permute-start(bf16[64,1024]{1,0:T(8,128)(2,1)S(1)} %copy-done.9), channel_id=1, source_target_pairs={{0,384},{16,400},{32,416},{48,432},{64,448},{80,464},{96,480},{112... | collective-permute-start | bytes 393224 | tf_op jit(solution)/shard_map/ppermute | solution.py:19
  44.2 15.3 %collective-permute-start.3 = (bf16[4,64,1024]{2,1,0:T(8,128)(2,1)}, bf16[4,64,1024]{2,1,0:T(8,128)(2,1)}, u32[]{:S(2)}, u32[]{:S(2)}) collective-permute-start(bf16[4,64,1024]{2,1,0:T(8,128)(2,1)} %bitcast_dynamic-update-slice_fusion.4), channel_id=1, source_target_pairs={{0,32},{16,48},{32,64},{48,80},{64,96},{80,112},{96,0},{112,16},{1... | collective-permute-start | bytes 1572872 | tf_op jit(solution)/shard_map/ppermute | solution.py:25
  46.6 25.8 %collective-permute-start.4 = (bf16[4,64,1024]{2,1,0:T(8,128)(2,1)}, bf16[4,64,1024]{2,1,0:T(8,128)(2,1)}, u32[]{:S(2)}, u32[]{:S(2)}) collective-permute-start(bf16[4,64,1024]{2,1,0:T(8,128)(2,1)} %bitcast_dynamic-update-slice_fusion.4), channel_id=1, source_target_pairs={{0,96},{16,112},{32,0},{48,16},{64,32},{80,48},{96,64},{112,80},{1... | collective-permute-start | bytes 1572872 | tf_op jit(solution)/shard_map/ppermute | solution.py:25
  59.4 14.1 %collective-permute-start.5 = (bf16[4,64,1024]{2,1,0:T(8,128)(2,1)}, bf16[4,64,1024]{2,1,0:T(8,128)(2,1)S(1)}, u32[]{:S(2)}, u32[]{:S(2)}) collective-permute-start(bf16[4,64,1024]{2,1,0:T(8,128)(2,1)} %collective-permute-done.3), channel_id=1, source_target_pairs={{0,32},{16,48},{32,64},{48,80},{64,96},{80,112},{96,0},{112,16},{1... | collective-permute-start | bytes 1572872 | tf_op jit(solution)/shard_map/ppermute | solution.py:25
  61.9 17.1 %collective-permute-start.7 = (bf16[4,512,128]{1,2,0:T(8,128)(2,1)S(1)}, bf16[4,512,128]{1,2,0:T(8,128)(2,1)S(1)}, u32[]{:S(2)}, u32[]{:S(2)}) collective-permute-start(bf16[4,512,128]{1,2,0:T(8,128)(2,1)S(1)} %get-tuple-element.33), channel_id=1, source_target_pairs={{0,7},{1,2},{2,1},{3,4},{4,3},{5,6},{6,5},{7,0},{8,15},{9,10},{10,... | collective-permute-start | bytes 1572872 | tf_op jit(solution)/shard_map/ppermute | solution.py:38
  68.0 14.3 %collective-permute-start.6 = (bf16[4,512,128]{1,2,0:T(8,128)(2,1)S(1)}, bf16[4,512,128]{1,2,0:T(8,128)(2,1)S(1)}, u32[]{:S(2)}, u32[]{:S(2)}) collective-permute-start(bf16[4,512,128]{1,2,0:T(8,128)(2,1)S(1)} %get-tuple-element.34), channel_id=1, source_target_pairs={{0,1},{1,0},{2,3},{3,2},{4,5},{5,4},{6,7},{7,6},{8,9},{9,8},{10,11... | collective-permute-start | bytes 1572872 | tf_op jit(solution)/shard_map/ppermute | solution.py:38
  79.0 3.4 %copy-start.5 = (bf16[4,512,128]{1,2,0:T(8,128)(2,1)}, bf16[4,512,128]{1,2,0:T(8,128)(2,1)S(1)}, u32[]{:S(2)}) copy-start(bf16[4,512,128]{1,2,0:T(8,128)(2,1)S(1)} %collective-permute-done.7) | copy-start | bytes 1572868
  82.3 0.8 copy-start.7
  83.2 5.0 %copy-start = (bf16[4,4,64,1024]{3,2,1,0:T(8,128)(2,1)}, bf16[4,4,64,1024]{3,2,1,0:T(8,128)(2,1)S(1)}, u32[]{:S(2)}) copy-start(bf16[4,4,64,1024]{3,2,1,0:T(8,128)(2,1)S(1)} %bitcast_dynamic-update-slice_fusion.3) | copy-start | bytes 6291460
  83.2 6.3 %collective-permute-start.8 = (bf16[4,4,64,1024]{3,2,1,0:T(8,128)(2,1)S(1)}, bf16[4,4,64,1024]{3,2,1,0:T(8,128)(2,1)}, u32[]{:S(2)}, u32[]{:S(2)}) collective-permute-start(bf16[4,4,64,1024]{3,2,1,0:T(8,128)(2,1)S(1)} %bitcast_dynamic-update-slice_fusion.3), channel_id=1, source_target_pairs={{0,16},{16,0},{32,48},{48,32},{64,80},{80,64},{96,112},{112,96},{1... | collective-permute-start | bytes 6291464 | tf_op jit(solution)/shard_map/ppermute | solution.py:29
  85.1 2.9 %copy-start.8 = (bf16[4,512,128]{1,2,0:T(8,128)(2,1)S(1)}, bf16[4,512,128]{1,2,0:T(8,128)(2,1)}, u32[]{:S(2)}) copy-start(bf16[4,512,128]{1,2,0:T(8,128)(2,1)} %copy-done.7) | copy-start | bytes 1572868
  85.1 3.0 %copy-start.6 = (bf16[4,512,128]{1,2,0:T(8,128)(2,1)S(1)}, bf16[4,512,128]{1,2,0:T(8,128)(2,1)}, u32[]{:S(2)}) copy-start(bf16[4,512,128]{1,2,0:T(8,128)(2,1)} %copy-done.5) | copy-start | bytes 1572868
  85.6 3.8 %collective-permute-start.9 = (f32[1024]{0:T(1024)S(1)}, f32[1024]{0:T(1024)S(1)}, u32[]{:S(2)}, u32[]{:S(2)}) collective-permute-start(f32[1024]{0:T(1024)S(1)} %multiply_reduce_fusion), channel_id=1, source_target_pairs={{0,16},{16,0},{32,48},{48,32},{64,80},{80,64},{96,112},{112,96},{1... | collective-permute-start | bytes 12296 | tf_op jit(solution)/shard_map/ppermute | solution.py:29
  89.4 3.0 %copy-start.1 = (bf16[4,4,64,1024]{3,2,1,0:T(8,128)(2,1)S(1)}, bf16[4,4,64,1024]{3,2,1,0:T(8,128)(2,1)}, u32[]{:S(2)}) copy-start(bf16[4,4,64,1024]{3,2,1,0:T(8,128)(2,1)} %copy-done) | copy-start | bytes 6291460
  178.9 12.0 %all-to-all-start.7 = ((f32[16,1,512]{2,1,0:T(1,128)}), f32[16,1,512]{2,1,0:T(1,128)S(1)}, u32[]{:S(2)}, u32[]{:S(2)}) async-start(f32[16,1,512]{2,1,0:T(1,128)} %broadcast_in_dim.55), calls=%async_computation.7 | async-start | bytes 65536 | tf_op jit(solution)/shard_map/all_to_all | solution.py:44
  192.8 14.5 %all-to-all-start.8 = ((f32[32,1,1024]{2,1,0:T(1,128)}), f32[32,1,1024]{2,1,0:T(1,128)S(1)}, u32[]{:S(2)}, u32[]{:S(2)}) async-start(f32[32,1,1024]{2,1,0:T(1,128)} %broadcast_in_dim.56), calls=%async_computation.8 | async-start | bytes 262144 | tf_op jit(solution)/shard_map/all_to_all | solution.py:44
  207.4 1.2 copy-start.4
  208.5 3.8 %copy-start.3 = (bf16[2,2,2,64,1024]{4,3,2,1,0:T(8,128)(2,1)S(1)}, bf16[2,2,2,64,1024]{4,3,2,1,0:T(8,128)(2,1)}, u32[]{:S(2)}) copy-start(bf16[2,2,2,64,1024]{4,3,2,1,0:T(8,128)(2,1)} %get-tuple-element.21) | copy-start | bytes 3145732
  209.3 17.5 %copy-start.2 = (bf16[2,2,2,64,1024]{4,3,2,1,0:T(8,128)(2,1)S(1)}, bf16[2,2,2,64,1024]{4,3,2,1,0:T(8,128)(2,1)}, u32[]{:S(2)}) copy-start(bf16[2,2,2,64,1024]{4,3,2,1,0:T(8,128)(2,1)} %get-tuple-element.42) | copy-start | bytes 3145732
  209.3 17.5 %collective-permute-start.11 = (bf16[512,512]{1,0:T(8,128)(2,1)S(1)}, bf16[512,512]{1,0:T(8,128)(2,1)S(1)}, u32[]{:S(2)}, u32[]{:S(2)}) collective-permute-start(bf16[512,512]{1,0:T(8,128)(2,1)S(1)} %convolution_convert_fusion), channel_id=1, source_target_pairs={{0,7},{1,2},{2,1},{3,4},{4,3},{5,6},{6,5},{7,0},{8,15},{9,10},{10,... | collective-permute-start | bytes 1572872 | tf_op jit(solution)/shard_map/ppermute | solution.py:38
  213.1 15.8 %collective-permute-start.10 = (bf16[512,512]{1,0:T(8,128)(2,1)S(1)}, bf16[512,512]{1,0:T(8,128)(2,1)S(1)}, u32[]{:S(2)}, u32[]{:S(2)}) collective-permute-start(bf16[512,512]{1,0:T(8,128)(2,1)S(1)} %convolution_convert_fusion.1), channel_id=1, source_target_pairs={{0,1},{1,0},{2,3},{3,2},{4,5},{5,4},{6,7},{7,6},{8,9},{9,8},{10,11... | collective-permute-start | bytes 1572872 | tf_op jit(solution)/shard_map/ppermute | solution.py:38

commit v5 on v4

--- a/solution.py
+++ b/solution.py
@@ -10,18 +10,16 @@
 
 Z_HI, X, CORE = 4, 4, 2
 Z_LO, Y = 2, 8
-PARITIES = [[z * Y + y + q for z in range(Z_LO) for y in range(0, Y, 2)] for q in range(2)]
+PARITIES = [
+    [z * Y + h * X + y + q for y in range(0, X, 2) for z in range(Z_LO) for h in range(Y // X)]
+    for q in range(2)
+]
+LINES = [[(z * X + x) * CORE + c for x in range(X)] for z in range(Z_HI) for c in range(CORE)]
 
 
 def along_z(array, by):
     step = X * CORE
     pairs = [(i, (i + by * step) % (Z_HI * step)) for i in range(Z_HI * step)]
-    return lax.ppermute(array, "row", pairs)
-
-
-def along_x(array, by):
-    step = X * CORE
-    pairs = [(i, i // step * step + (i + by * CORE) % step) for i in range(Z_HI * step)]
     return lax.ppermute(array, "row", pairs)
 
 
@@ -46,21 +44,17 @@
 
 def gather(noise, data):
     row, odd = lax.axis_index("row"), lax.axis_index("col") % 2
-    z, x = row // (X * CORE), row // CORE % X
+    z = row // (X * CORE)
     same = share(noise, "col", PARITIES)
-    up, down, far = along_z(data, 1), along_z(data, -1), along_z(data, 2)
     plane = jnp.zeros((Z_HI,) + data.shape, data.dtype)
-    for piece, by in ((data, 0), (up, 3), (down, 1), (far, 2)):
+    pieces = (data, along_z(data, -1), along_z(data, 2), along_z(data, 1))
+    for by, piece in enumerate(pieces):
         plane = lax.dynamic_update_slice(plane, piece[None], ((z + by) % Z_HI, 0, 0))
-    up, down = along_x(plane, 1), along_x(plane, -1)
-    up, same = lax.optimization_barrier((up, same))
-    far = along_x(up, 1)
-    n = len(PARITIES[0])
-    above, below = neighbour(same[: n // 2], 1), neighbour(same[n // 2 :], -1)
-    far, above, below = lax.optimization_barrier((far, above, below))
-    whole = jnp.zeros((Z_HI, X) + data.shape, data.dtype)
-    for piece, by in ((plane, 0), (up, 3), (down, 1), (far, 2)):
-        whole = lax.dynamic_update_slice(whole, piece[:, None], (0, (x + by) % X, 0, 0))
+    plane, same = lax.optimization_barrier((plane, same))
+    whole = share(plane, "row", LINES)
+    n = len(PARITIES[0]) // 2
+    above, below = neighbour(same[:n], 1), neighbour(same[n:], -1)
+    whole, above, below = lax.optimization_barrier((whole, above, below))
     other = jnp.concatenate([above, below])
     by_parity = [jnp.where(odd == 0, same, other), jnp.where(odd == 0, other, same)]
     return by_parity, whole
@@ -90,8 +84,8 @@
     def half(which):
         size = noise.shape[1] // CORE
         part = [p[:, :, which * size : (which + 1) * size] for p in by_parity]
-        part = jnp.concatenate(part, axis=2)
-        return part.transpose(1, 0, 2).reshape(rows, -1)
+        part = [p.reshape((X // 2, -1) + p.shape[1:]) for p in part]
+        return jnp.stack(part, axis=1).transpose(3, 0, 1, 2, 4).reshape(rows, -1)
 
     first, second = half(0), half(1)
     mine = jnp.where(core == 0, first, second)
@@ -122,11 +116,11 @@
     )
 
     def features(parity):
-        shape = (Z_HI, X // 2, 2, -1, cols)
-        a = lax.dynamic_index_in_dim(here.reshape(shape), parity, 2, keepdims=False)
-        b = lax.dynamic_index_in_dim(there.reshape(shape), parity, 2, keepdims=False)
+        shape = (X // 2, 2, Z_HI, -1, cols)
+        a = lax.dynamic_index_in_dim(here.reshape(shape), parity, 1, keepdims=False)
+        b = lax.dynamic_index_in_dim(there.reshape(shape), parity, 1, keepdims=False)
         both = [jnp.where(core == 0, a, b), jnp.where(core == 0, b, a)]
-        return jnp.stack(both, axis=2).reshape(Z_LO, -1, cols)
+        return jnp.stack(both, axis=2).reshape(X // 2, -1, cols)
 
     def terms(part):
         contract = (((1,), (1,)), ((), ()))

time: 265 us -> 260 us (0.981)
  blocking collectives: 110 us -> 96.5 us
  waiting for transfers between devices: 54.9 us -> 62.9 us
  other arithmetic: 13.5 us -> 17.5 us
    all_to_all x6 -> x5, blocking collectives: 79.5 us -> 65.7 us  [share(): return lax.all_to_all(copies, axis, 0, 0, axis_index_groups=groups)]
    all_to_all x3 -> x5, starting transfers between devices: 18 us -> 28.6 us  [share(): return lax.all_to_all(copies, axis, 0, 0, axis_index_groups=groups)]
    ppermute x3 -> x0, waiting for transfers between devices: 9.32 us -> none  [along_x(): return lax.ppermute(array, 'row', pairs)]
    all_to_all x3 -> x5, waiting for transfers between devices: 13.2 us -> 21.7 us  [share(): return lax.all_to_all(copies, axis, 0, 0, axis_index_groups=groups)]
    ppermute x3 -> x0, starting transfers between devices: 8.21 us -> none  [along_x(): return lax.ppermute(array, 'row', pairs)]
    ppermute x3, waiting for transfers between devices: 10.9 us -> 16.5 us  [along_z(): return lax.ppermute(array, 'row', pairs)]
    ppermute x4, starting transfers between devices: 13.4 us -> 9.76 us  [neighbour(): return lax.ppermute(array, 'col', pairs)]
    dynamic_update_slice x4 -> x0, local copies, waits for them, and re-layouts: 3.29 us -> none  [gather(): lax.dynamic_update_slice(whole, piece[:, None], (0, (x + by) % X, 0, 0))]
  transfers between devices with their start and end apart: 15 -> 14, of which waited for: 8 -> 10; matrix products, arithmetic and copies ran while one was open for 6% -> 6% of each run, Pallas kernels for 0% -> 0%
where the time goes in v5:
time: 260 us; the launch traced here: 256 us
  blocking collectives  96.5 us (37%)
  waiting for transfers between devices  62.9 us (24%)
  starting transfers between devices  59.5 us (23%)
  other arithmetic  17.5 us (7%)
  local copies, waits for them, and re-layouts  10.9 us (4%)
  matrix products  7.39 us (3%)
    all_to_all x5, blocking collectives, share(): return lax.all_to_all(copies, axis, 0, 0, axis_index_groups=groups)  65.7 us
    all_to_all x1, blocking collectives, local(): parts = lax.all_to_all(sums, 'col', 0, 0, axis_index_groups=PARITIES)  30.8 us
    all_to_all x5, starting transfers between devices, share(): return lax.all_to_all(copies, axis, 0, 0, axis_index_groups=groups)  28.6 us
    ppermute x4, waiting for transfers between devices, neighbour(): return lax.ppermute(array, 'col', pairs)  24.7 us
    all_to_all x5, waiting for transfers between devices, share(): return lax.all_to_all(copies, axis, 0, 0, axis_index_groups=groups)  21.7 us
    ppermute x3, starting transfers between devices, along_z(): return lax.ppermute(array, 'row', pairs)  16.8 us
    ppermute x3, waiting for transfers between devices, along_z(): return lax.ppermute(array, 'row', pairs)  16.5 us
    ppermute x4, starting transfers between devices, neighbour(): return lax.ppermute(array, 'col', pairs)  9.76 us
  transfers between devices with their start and end apart: 14, of which 10 were waited for; matrix products, arithmetic and copies ran while one was open for 6% of the time, Pallas kernels for 0%

profile of v5, /device:TPU:6, one launch (start us, length us, event | category | flops | bytes accessed | tf_op | source)
XLA Modules:
  0.0 255.9 jit_solution(4520715139913250632)
XLA Ops:
  2.8 8.9 %all-to-all-start = ((bf16[8,512,128]{1,2,0:T(8,128)(2,1)}), bf16[8,512,128]{1,2,0:T(8,128)(2,1)S(1)}, u32[]{:S(2)}, u32[]{:S(2)}) async-start(bf16[8,512,128]{1,2,0:T(8,128)(2,1)} %broadcast_in_dim.35), calls=%async_computation | async-start | bytes 2097152 | tf_op jit(solution)/shard_map/all_to_all | solution.py:42
  11.7 10.0 %collective-permute-start = (bf16[64,1024]{1,0:T(8,128)(2,1)S(1)}, bf16[64,1024]{1,0:T(8,128)(2,1)S(1)}, u32[]{:S(2)}, u32[]{:S(2)}) collective-permute-start(bf16[64,1024]{1,0:T(8,128)(2,1)S(1)} %copy-done.7), channel_id=1, source_target_pairs={{0,384},{16,400},{32,416},{48,432},{64,448},{80,464},{96,480},{112... | collective-permute-start | bytes 393224 | tf_op jit(solution)/shard_map/ppermute | solution.py:23
  21.7 1.9 collective-permute-start.2
  23.7 4.8 %collective-permute-start.1 = (bf16[64,1024]{1,0:T(8,128)(2,1)S(1)}, bf16[64,1024]{1,0:T(8,128)(2,1)S(1)}, u32[]{:S(2)}, u32[]{:S(2)}) collective-permute-start(bf16[64,1024]{1,0:T(8,128)(2,1)S(1)} %copy-done.7), channel_id=1, source_target_pairs={{0,256},{16,272},{32,288},{48,304},{64,320},{80,336},{96,352},{112... | collective-permute-start | bytes 393224 | tf_op jit(solution)/shard_map/ppermute | solution.py:23
  28.7 16.0 %collective-permute-done.1 = bf16[64,1024]{1,0:T(8,128)(2,1)S(1)} collective-permute-done((bf16[64,1024]{1,0:T(8,128)(2,1)S(1)}, bf16[64,1024]{1,0:T(8,128)(2,1)S(1)}, u32[]{:S(2)}, u32[]{:S(2)}) %collective-permute-start.1) | collective-permute-done | bytes 131104 | tf_op jit(solution)/shard_map/ppermute | solution.py:23
  45.2 1.6 broadcast_in_dim.36
  46.9 4.8 %all-to-all-start.1 = ((bf16[4,4,64,1024]{3,2,1,0:T(8,128)(2,1)}), bf16[4,4,64,1024]{3,2,1,0:T(8,128)(2,1)S(1)}, u32[]{:S(2)}, u32[]{:S(2)}) async-start(bf16[4,4,64,1024]{3,2,1,0:T(8,128)(2,1)} %broadcast_in_dim.36), calls=%async_computation.1 | async-start | bytes 4194304 | tf_op jit(solution)/shard_map/all_to_all | solution.py:42
  51.7 2.5 collective-permute-start.4
  54.2 1.9 collective-permute-start.3
  56.2 11.4 %collective-permute-done.4 = bf16[4,512,128]{1,2,0:T(8,128)(2,1)S(1)} collective-permute-done((bf16[4,512,128]{1,2,0:T(8,128)(2,1)S(1)}, bf16[4,512,128]{1,2,0:T(8,128)(2,1)S(1)}, u32[]{:S(2)}, u32[]{:S(2)}) %collective-permute-start.4) | collective-permute-done | bytes 524320 | tf_op jit(solution)/shard_map/ppermute | solution.py:36
  69.2 6.3 %all-to-all-done.1 = bf16[4,4,64,1024]{3,2,1,0:T(8,128)(2,1)S(1)} async-done(((bf16[4,4,64,1024]{3,2,1,0:T(8,128)(2,1)}), bf16[4,4,64,1024]{3,2,1,0:T(8,128)(2,1)S(1)}, u32[]{:S(2)}, u32[]{:S(2)}) %all-to-all-start.1) | async-done | bytes 2097184 | tf_op jit(solution)/shard_map/all_to_all | solution.py:42
  75.5 1.9 collective-permute-start.5
  78.0 2.4 collective-permute-start.6
  82.6 3.0 %fusion.15 = f32[512,1024]{1,0:T(8,128)S(1)} fusion(bf16[512,1024]{0,1:T(8,128)(2,1)S(1)} %bitcast.88, bf16[1024,1024]{1,0:T(8,128)(2,1)} %bitcast.18), kind=kOutput, calls=%fused_computation.75 | convolution fusion | flops 1073741824 | bytes 5242880 | tf_op jit(solution)/shard_map/dot_general | solution.py:94
  87.6 13.4 %all_to_all.69 = f32[16,1,512]{2,1,0:T(1,128)S(1)} all-to-all(f32[16,1,512]{2,1,0:T(1,128)S(1)} %broadcast_in_dim.37), channel_id=1, replica_groups=mesh['row'=32,'col'=16] {'col'}, dimensions={0} | all-to-all | bytes 65536 | tf_op jit(solution)/shard_map/all_to_all | solution.py:42
  101.8 16.2 %all_to_all.70 = f32[32,1,1024]{2,1,0:T(1,128)S(1)} all-to-all(f32[32,1,1024]{2,1,0:T(1,128)S(1)} %broadcast_in_dim.38), channel_id=1, replica_groups=mesh['row'=32,'col'=16] {'row'}, dimensions={0} | all-to-all | bytes 262144 | tf_op jit(solution)/shard_map/all_to_all | solution.py:42
  118.7 11.1 %all_to_all.71 = f32[16,1,512]{2,1,0:T(1,128)S(1)} all-to-all(f32[16,1,512]{2,1,0:T(1,128)S(1)} %broadcast_in_dim.39), channel_id=1, replica_groups=mesh['row'=32,'col'=16] {'col'}, dimensions={0} | all-to-all | bytes 65536 | tf_op jit(solution)/shard_map/all_to_all | solution.py:42
  130.4 13.9 %all_to_all.72 = f32[32,1,1024]{2,1,0:T(1,128)S(1)} all-to-all(f32[32,1,1024]{2,1,0:T(1,128)S(1)} %broadcast_in_dim.40), channel_id=1, replica_groups=mesh['row'=32,'col'=16] {'row'}, dimensions={0} | all-to-all | bytes 262144 | tf_op jit(solution)/shard_map/all_to_all | solution.py:42
  145.1 11.1 %all_to_all.73 = f32[16,1,512]{2,1,0:T(1,128)S(1)} all-to-all(f32[16,1,512]{2,1,0:T(1,128)S(1)} %broadcast_in_dim.41), channel_id=1, replica_groups=mesh['row'=32,'col'=16] {'col'}, dimensions={0} | all-to-all | bytes 65536 | tf_op jit(solution)/shard_map/all_to_all | solution.py:42
  157.5 5.7 %all-to-all-start.7 = ((f32[32,1,1024]{2,1,0:T(1,128)}), f32[32,1,1024]{2,1,0:T(1,128)S(1)}, u32[]{:S(2)}, u32[]{:S(2)}) async-start(f32[32,1,1024]{2,1,0:T(1,128)} %broadcast_in_dim.42), calls=%async_computation.7 | async-start | bytes 262144 | tf_op jit(solution)/shard_map/all_to_all | solution.py:42
  163.2 8.9 %all-to-all-done.7 = f32[32,1,1024]{2,1,0:T(1,128)S(1)} async-done(((f32[32,1,1024]{2,1,0:T(1,128)}), f32[32,1,1024]{2,1,0:T(1,128)S(1)}, u32[]{:S(2)}, u32[]{:S(2)}) %all-to-all-start.7) | async-done | bytes 131104 | tf_op jit(solution)/shard_map/all_to_all | solution.py:42
  173.4 3.7 %all-to-all-start.8 = ((f32[16,1,512]{2,1,0:T(1,128)}), f32[16,1,512]{2,1,0:T(1,128)S(1)}, u32[]{:S(2)}, u32[]{:S(2)}) async-start(f32[16,1,512]{2,1,0:T(1,128)} %broadcast_in_dim.43), calls=%async_computation.8 | async-start | bytes 65536 | tf_op jit(solution)/shard_map/all_to_all | solution.py:42
  177.1 4.0 %fusion.3 = (bf16[2,4,1,64,1024]{4,3,1,0,2:T(8,128)(2,1)}, bf16[2,4,1,64,1024]{4,3,1,0,2:T(8,128)(2,1)}, bf16[2,4,1,64,1024]{4,3,1,0,2:T(8,128)(2,1)}) fusion(pred[]{:T(512)S(6)} %eq.20, bf16[2,2,4,64,1024]{4,3,2,1,0:T(8,128)(2,1)} %bitcast.5, s32[]{:T(128)S(6)} %select_n.177, bf16[2,2,4,64,1024]{4,3,2,1,0:T(8,128)(2,1)} %bitcast.85, s32[]{:T(128)S(6)} %select_n.162), kind=kLoop, calls=%fused_computation.32 | loop fusion | flops 1572864 | bytes 7340041 | tf_op jit(solution)/shard_map/jit(_where)/select_n | solution.py:122
  181.1 4.3 %all-to-all-done.8 = f32[16,1,512]{2,1,0:T(1,128)S(1)} async-done(((f32[16,1,512]{2,1,0:T(1,128)}), f32[16,1,512]{2,1,0:T(1,128)S(1)}, u32[]{:S(2)}, u32[]{:S(2)}) %all-to-all-start.8) | async-done | bytes 32800 | tf_op jit(solution)/shard_map/all_to_all | solution.py:42
  187.3 5.6 %all-to-all-start.9 = ((f32[32,1,1024]{2,1,0:T(1,128)}), f32[32,1,1024]{2,1,0:T(1,128)S(1)}, u32[]{:S(2)}, u32[]{:S(2)}) async-start(f32[32,1,1024]{2,1,0:T(1,128)} %broadcast_in_dim.44), calls=%async_computation.9 | async-start | bytes 262144 | tf_op jit(solution)/shard_map/all_to_all | solution.py:42
  192.9 1.7 fusion
  194.6 2.8 %fusion.1 = (bf16[1,4,2,64,1024]{4,3,1,0,2:T(8,128)(2,1)S(1)}, bf16[1,4,2,64,1024]{4,3,1,0,2:T(8,128)(2,1)S(1)}, bf16[1,4,2,64,1024]{4,3,1,0,2:T(8,128)(2,1)}, bf16[1,4,2,64,1024]{4,3,1,0,2:T(8,128)(2,1)S(1)}) fusion(bf16[2,4,1,64,1024]{4,3,1,0,2:T(8,128)(2,1)} %get-tuple-element.17, bf16[2,4,1,64,1024]{4,3,1,0,2:T(8,128)(2,1)S(1)} %fusion, ...), kind=kLoop, calls=%fused_computation.24 | loop fusion | flops 2097152 | bytes 8388608 | tf_op jit(solution)/shard_map/stack | solution.py:123
  199.7 2.2 all-to-all-done.9
  203.9 2.9 %collective-permute-start.8 = (bf16[512,512]{1,0:T(8,128)(2,1)S(1)}, bf16[512,512]{1,0:T(8,128)(2,1)S(1)}, u32[]{:S(2)}, u32[]{:S(2)}) collective-permute-start(bf16[512,512]{1,0:T(8,128)(2,1)S(1)} %convolution_convert_fusion), channel_id=1, source_target_pairs={{0,7},{1,2},{2,1},{3,4},{4,3},{5,6},{6,5},{7,0},{8,15},{9,10},{10,... | collective-permute-start | bytes 1572872 | tf_op jit(solution)/shard_map/ppermute | solution.py:36
  207.7 2.4 collective-permute-start.7
  210.2 11.1 %collective-permute-done.8 = bf16[512,512]{1,0:T(8,128)(2,1)S(1)} collective-permute-done((bf16[512,512]{1,0:T(8,128)(2,1)S(1)}, bf16[512,512]{1,0:T(8,128)(2,1)S(1)}, u32[]{:S(2)}, u32[]{:S(2)}) %collective-permute-start.8) | collective-permute-done | bytes 524320 | tf_op jit(solution)/shard_map/ppermute | solution.py:36
  224.3 30.8 %all_to_all.74 = bf16[8,128,512]{2,1,0:T(8,128)(2,1)S(1)} all-to-all(bf16[8,128,512]{2,1,0:T(8,128)(2,1)S(1)} %bitcast.89), channel_id=1, replica_groups={{0,4,8,12,2,6,10,14},{1,5,9,13,3,7,11,15},{16,20,24,28,18,22,26,30},{17..., dimensions={0} | all-to-all | bytes 2097152 | tf_op jit(solution)/shard_map/all_to_all | solution.py:138
  (87 shorter events, 25.4 us)
Async XLA Ops:
  0.6 11.1 %copy-start.7 = (bf16[64,1024]{1,0:T(8,128)(2,1)S(1)}, bf16[64,1024]{1,0:T(8,128)(2,1)}, u32[]{:S(2)}) copy-start(bf16[64,1024]{1,0:T(8,128)(2,1)} %param.3) | copy-start | bytes 393220
  2.8 42.5 %all-to-all-start = ((bf16[8,512,128]{1,2,0:T(8,128)(2,1)}), bf16[8,512,128]{1,2,0:T(8,128)(2,1)S(1)}, u32[]{:S(2)}, u32[]{:S(2)}) async-start(bf16[8,512,128]{1,2,0:T(8,128)(2,1)} %broadcast_in_dim.35), calls=%async_computation | async-start | bytes 2097152 | tf_op jit(solution)/shard_map/all_to_all | solution.py:42
  11.7 17.0 %collective-permute-start = (bf16[64,1024]{1,0:T(8,128)(2,1)S(1)}, bf16[64,1024]{1,0:T(8,128)(2,1)S(1)}, u32[]{:S(2)}, u32[]{:S(2)}) collective-permute-start(bf16[64,1024]{1,0:T(8,128)(2,1)S(1)} %copy-done.7), channel_id=1, source_target_pairs={{0,384},{16,400},{32,416},{48,432},{64,448},{80,464},{96,480},{112... | collective-permute-start | bytes 393224 | tf_op jit(solution)/shard_map/ppermute | solution.py:23
  21.7 23.5 %collective-permute-start.2 = (bf16[64,1024]{1,0:T(8,128)(2,1)S(1)}, bf16[64,1024]{1,0:T(8,128)(2,1)S(1)}, u32[]{:S(2)}, u32[]{:S(2)}) collective-permute-start(bf16[64,1024]{1,0:T(8,128)(2,1)S(1)} %copy-done.7), channel_id=1, source_target_pairs={{0,128},{16,144},{32,160},{48,176},{64,192},{80,208},{96,224},{112... | collective-permute-start | bytes 393224 | tf_op jit(solution)/shard_map/ppermute | solution.py:23
  23.7 21.0 %collective-permute-start.1 = (bf16[64,1024]{1,0:T(8,128)(2,1)S(1)}, bf16[64,1024]{1,0:T(8,128)(2,1)S(1)}, u32[]{:S(2)}, u32[]{:S(2)}) collective-permute-start(bf16[64,1024]{1,0:T(8,128)(2,1)S(1)} %copy-done.7), channel_id=1, source_target_pairs={{0,256},{16,272},{32,288},{48,304},{64,320},{80,336},{96,352},{112... | collective-permute-start | bytes 393224 | tf_op jit(solution)/shard_map/ppermute | solution.py:23
  46.9 28.7 %all-to-all-start.1 = ((bf16[4,4,64,1024]{3,2,1,0:T(8,128)(2,1)}), bf16[4,4,64,1024]{3,2,1,0:T(8,128)(2,1)S(1)}, u32[]{:S(2)}, u32[]{:S(2)}) async-start(bf16[4,4,64,1024]{3,2,1,0:T(8,128)(2,1)} %broadcast_in_dim.36), calls=%async_computation.1 | async-start | bytes 4194304 | tf_op jit(solution)/shard_map/all_to_all | solution.py:42
  51.7 15.8 %collective-permute-start.4 = (bf16[4,512,128]{1,2,0:T(8,128)(2,1)S(1)}, bf16[4,512,128]{1,2,0:T(8,128)(2,1)S(1)}, u32[]{:S(2)}, u32[]{:S(2)}) collective-permute-start(bf16[4,512,128]{1,2,0:T(8,128)(2,1)S(1)} %get-tuple-element.32), channel_id=1, source_target_pairs={{0,7},{1,2},{2,1},{3,4},{4,3},{5,6},{6,5},{7,0},{8,15},{9,10},{10,... | collective-permute-start | bytes 1572872 | tf_op jit(solution)/shard_map/ppermute | solution.py:36
  54.2 15.0 %collective-permute-start.3 = (bf16[4,512,128]{1,2,0:T(8,128)(2,1)S(1)}, bf16[4,512,128]{1,2,0:T(8,128)(2,1)}, u32[]{:S(2)}, u32[]{:S(2)}) collective-permute-start(bf16[4,512,128]{1,2,0:T(8,128)(2,1)S(1)} %get-tuple-element.33), channel_id=1, source_target_pairs={{0,1},{1,0},{2,3},{3,2},{4,5},{5,4},{6,7},{7,6},{8,9},{9,8},{10,11... | collective-permute-start | bytes 1572872 | tf_op jit(solution)/shard_map/ppermute | solution.py:36
  67.5 0.8 copy-start.5
  75.5 6.0 %copy-start = (bf16[4,4,64,1024]{3,2,1,0:T(8,128)(2,1)}, bf16[4,4,64,1024]{3,2,1,0:T(8,128)(2,1)S(1)}, u32[]{:S(2)}) copy-start(bf16[4,4,64,1024]{3,2,1,0:T(8,128)(2,1)S(1)} %all-to-all-done.1) | copy-start | bytes 6291460
  75.5 7.1 %collective-permute-start.5 = (bf16[4,4,64,1024]{3,2,1,0:T(8,128)(2,1)S(1)}, bf16[4,4,64,1024]{3,2,1,0:T(8,128)(2,1)}, u32[]{:S(2)}, u32[]{:S(2)}) collective-permute-start(bf16[4,4,64,1024]{3,2,1,0:T(8,128)(2,1)S(1)} %all-to-all-done.1), channel_id=1, source_target_pairs={{0,16},{16,0},{32,48},{48,32},{64,80},{80,64},{96,112},{112,96},{1... | collective-permute-start | bytes 6291464 | tf_op jit(solution)/shard_map/ppermute | solution.py:27
  77.5 4.0 %copy-start.6 = (bf16[4,512,128]{1,2,0:T(8,128)(2,1)S(1)}, bf16[4,512,128]{1,2,0:T(8,128)(2,1)}, u32[]{:S(2)}) copy-start(bf16[4,512,128]{1,2,0:T(8,128)(2,1)} %copy-done.5) | copy-start | bytes 1572868
  78.0 4.6 %collective-permute-start.6 = (f32[1024]{0:T(1024)S(1)}, f32[1024]{0:T(1024)S(1)}, u32[]{:S(2)}, u32[]{:S(2)}) collective-permute-start(f32[1024]{0:T(1024)S(1)} %multiply_reduce_fusion), channel_id=1, source_target_pairs={{0,16},{16,0},{32,48},{48,32},{64,80},{80,64},{96,112},{112,96},{1... | collective-permute-start | bytes 12296 | tf_op jit(solution)/shard_map/ppermute | solution.py:27
  82.6 3.0 %copy-start.1 = (bf16[4,4,64,1024]{3,2,1,0:T(8,128)(2,1)S(1)}, bf16[4,4,64,1024]{3,2,1,0:T(8,128)(2,1)}, u32[]{:S(2)}) copy-start(bf16[4,4,64,1024]{3,2,1,0:T(8,128)(2,1)} %copy-done) | copy-start | bytes 6291460
  157.5 14.6 %all-to-all-start.7 = ((f32[32,1,1024]{2,1,0:T(1,128)}), f32[32,1,1024]{2,1,0:T(1,128)S(1)}, u32[]{:S(2)}, u32[]{:S(2)}) async-start(f32[32,1,1024]{2,1,0:T(1,128)} %broadcast_in_dim.42), calls=%async_computation.7 | async-start | bytes 262144 | tf_op jit(solution)/shard_map/all_to_all | solution.py:42
  173.4 12.0 %all-to-all-start.8 = ((f32[16,1,512]{2,1,0:T(1,128)}), f32[16,1,512]{2,1,0:T(1,128)S(1)}, u32[]{:S(2)}, u32[]{:S(2)}) async-start(f32[16,1,512]{2,1,0:T(1,128)} %broadcast_in_dim.43), calls=%async_computation.8 | async-start | bytes 65536 | tf_op jit(solution)/shard_map/all_to_all | solution.py:42
  187.3 14.5 %all-to-all-start.9 = ((f32[32,1,1024]{2,1,0:T(1,128)}), f32[32,1,1024]{2,1,0:T(1,128)S(1)}, u32[]{:S(2)}, u32[]{:S(2)}) async-start(f32[32,1,1024]{2,1,0:T(1,128)} %broadcast_in_dim.44), calls=%async_computation.9 | async-start | bytes 262144 | tf_op jit(solution)/shard_map/all_to_all | solution.py:42
  201.9 1.2 copy-start.4
  203.1 3.8 %copy-start.3 = (bf16[1,4,2,64,1024]{4,3,2,1,0:T(8,128)(2,1)S(1)}, bf16[1,4,2,64,1024]{4,3,2,1,0:T(8,128)(2,1)}, u32[]{:S(2)}) copy-start(bf16[1,4,2,64,1024]{4,3,2,1,0:T(8,128)(2,1)} %copy.48) | copy-start | bytes 3145732
  203.9 6.1 %copy-start.2 = (bf16[1,4,2,64,1024]{4,3,1,0,2:T(8,128)(2,1)S(1)}, bf16[1,4,2,64,1024]{4,3,1,0,2:T(8,128)(2,1)}, u32[]{:S(2)}) copy-start(bf16[1,4,2,64,1024]{4,3,1,0,2:T(8,128)(2,1)} %get-tuple-element.41) | copy-start | bytes 3145732
  203.9 17.5 %collective-permute-start.8 = (bf16[512,512]{1,0:T(8,128)(2,1)S(1)}, bf16[512,512]{1,0:T(8,128)(2,1)S(1)}, u32[]{:S(2)}, u32[]{:S(2)}) collective-permute-start(bf16[512,512]{1,0:T(8,128)(2,1)S(1)} %convolution_convert_fusion), channel_id=1, source_target_pairs={{0,7},{1,2},{2,1},{3,4},{4,3},{5,6},{6,5},{7,0},{8,15},{9,10},{10,... | collective-permute-start | bytes 1572872 | tf_op jit(solution)/shard_map/ppermute | solution.py:36
  207.7 15.8 %collective-permute-start.7 = (bf16[512,512]{1,0:T(8,128)(2,1)S(1)}, bf16[512,512]{1,0:T(8,128)(2,1)S(1)}, u32[]{:S(2)}, u32[]{:S(2)}) collective-permute-start(bf16[512,512]{1,0:T(8,128)(2,1)S(1)} %convolution_convert_fusion.1), channel_id=1, source_target_pairs={{0,1},{1,0},{2,3},{3,2},{4,5},{5,4},{6,7},{7,6},{8,9},{9,8},{10,11... | collective-permute-start | bytes 1572872 | tf_op jit(solution)/shard_map/ppermute | solution.py:36

commit v6 on v5

--- a/solution.py
+++ b/solution.py
@@ -43,21 +43,13 @@
 
 
 def gather(noise, data):
-    row, odd = lax.axis_index("row"), lax.axis_index("col") % 2
-    z = row // (X * CORE)
+    z = lax.axis_index("row") // (X * CORE)
     same = share(noise, "col", PARITIES)
     plane = jnp.zeros((Z_HI,) + data.shape, data.dtype)
     pieces = (data, along_z(data, -1), along_z(data, 2), along_z(data, 1))
     for by, piece in enumerate(pieces):
         plane = lax.dynamic_update_slice(plane, piece[None], ((z + by) % Z_HI, 0, 0))
-    plane, same = lax.optimization_barrier((plane, same))
-    whole = share(plane, "row", LINES)
-    n = len(PARITIES[0]) // 2
-    above, below = neighbour(same[:n], 1), neighbour(same[n:], -1)
-    whole, above, below = lax.optimization_barrier((whole, above, below))
-    other = jnp.concatenate([above, below])
-    by_parity = [jnp.where(odd == 0, same, other), jnp.where(odd == 0, other, same)]
-    return by_parity, whole
+    return lax.optimization_barrier((same, plane))
 
 
 def log_total(scores, dim, axis):
@@ -75,10 +67,13 @@
     cols_all = cols * lax.axis_size("col")
     core = lax.axis_index("row") % CORE
 
-    by_parity, here = gather(noise, data)
-    there = other_core(here)
-    sq = jnp.sum(here.astype(jnp.float32) ** 2, axis=(0, 1, 2))
-    data_sq = sq + other_core(sq)
+    odd = lax.axis_index("col") % 2
+
+    same, plane = gather(noise, data)
+    here = share(plane, "row", LINES)
+    n = len(PARITIES[0]) // 2
+    other = jnp.concatenate([neighbour(same[:n], 1), neighbour(same[n:], -1)])
+    by_parity = [jnp.where(odd == 0, same, other), jnp.where(odd == 0, other, same)]
     noise_sq = sum(jnp.sum(part.astype(jnp.float32) ** 2, axis=(0, 2)) for part in by_parity)
 
     def half(which):
@@ -90,6 +85,12 @@
     first, second = half(0), half(1)
     mine = jnp.where(core == 0, first, second)
     others = jnp.where(core == 0, second, first)
+    here, mine, others, noise_sq, kept, away = lax.optimization_barrier(
+        (here, mine, others, noise_sq, odd, 1 - odd)
+    )
+    there = other_core(here)
+    sq = jnp.sum(here.astype(jnp.float32) ** 2, axis=(0, 1, 2))
+    data_sq = sq + other_core(sq)
     cross = jnp.dot(mine, here.reshape(-1, cols), preferred_element_type=jnp.float32)
     cross += jnp.dot(others, there.reshape(-1, cols), preferred_element_type=jnp.float32)
 
@@ -108,9 +109,6 @@
         by_row = (lift / rows_all) / jnp.sum(share(part, "col"), axis=0)
         part = jnp.sum(plan * by_row[:, None], axis=0)
         by_col = (lift / cols_all) / jnp.sum(share(part, "row"), axis=0)
-    row_potential = noise_sq / width + EPS * (row_first + jnp.log(by_row))
-    col_potential = data_sq / width + EPS * (col_first + jnp.log(by_col))
-
     weights = (plan * ((rows_all / lift) * by_row)[:, None] * by_col[None, :]).astype(
         jnp.bfloat16
     )
@@ -126,13 +124,13 @@
         contract = (((1,), (1,)), ((), ()))
         return lax.dot_general(part, weights, contract, preferred_element_type=jnp.float32)
 
-    odd = lax.axis_index("col") % 2
-    away, kept = features(1 - odd), features(odd)
+    sent = [terms(part).astype(jnp.bfloat16) for part in features(away)]
+    got = [neighbour(part, by) for part, by in zip(sent, (1, -1))]
+    sent, kept, by_row, by_col = lax.optimization_barrier((sent[0], kept, by_row, by_col))
+    row_potential = noise_sq / width + EPS * (row_first + jnp.log(by_row))
+    col_potential = data_sq / width + EPS * (col_first + jnp.log(by_col))
     sums = [
-        (terms(kept[z]) + neighbour(terms(away[z]).astype(jnp.bfloat16), by)).astype(
-            jnp.bfloat16
-        )
-        for z, by in ((0, 1), (1, -1))
+        (terms(own) + add).astype(jnp.bfloat16) for own, add in zip(features(kept), got)
     ]
     sums = jnp.stack(sums).reshape(len(PARITIES[0]), -1, rows)
     parts = lax.all_to_all(sums, "col", 0, 0, axis_index_groups=PARITIES)

time: 260 us -> 262 us (level)
  waiting for transfers between devices: 62.9 us -> 82.6 us
  blocking collectives: 96.5 us -> 80 us
  other arithmetic: 17.5 us -> 14.7 us
    all_to_all x1 -> x0, blocking collectives: 30.8 us -> none  [local(): parts = lax.all_to_all(sums, 'col', 0, 0, axis_index_groups=PARITIES)]
    all_to_all x0 -> x1, waiting for transfers between devices: none -> 26.1 us  [local(): parts = lax.all_to_all(sums, 'col', 0, 0, axis_index_groups=PARITIES)]
    all_to_all x5 -> x6, blocking collectives: 65.7 us -> 80 us  [share(): return lax.all_to_all(copies, axis, 0, 0, axis_index_groups=groups)]
    all_to_all x5 -> x4, starting transfers between devices: 28.6 us -> 22.9 us  [share(): return lax.all_to_all(copies, axis, 0, 0, axis_index_groups=groups)]
    all_to_all x5 -> x4, waiting for transfers between devices: 21.7 us -> 18 us  [share(): return lax.all_to_all(copies, axis, 0, 0, axis_index_groups=groups)]
    dot_general x4, matrix products: 3 us -> 6.65 us  [terms(): lax.dot_general(part, weights, contract, preferred_element_type=jnp.float32)]
    all_to_all x0 -> x1, starting transfers between devices: none -> 3.56 us  [local(): parts = lax.all_to_all(sums, 'col', 0, 0, axis_index_groups=PARITIES)]
    ppermute x4, waiting for transfers between devices: 24.7 us -> 22 us  [neighbour(): return lax.ppermute(array, 'col', pairs)]
  transfers between devices with their start and end apart: 14 -> 14, of which waited for: 10 -> 10; matrix products, arithmetic and copies ran while one was open for 6% -> 7% of each run, Pallas kernels for 0% -> 0%
where the time goes in v6:
time: 262 us; the launch traced here: 259 us
  waiting for transfers between devices  82.6 us (32%)
  blocking collectives  80 us (31%)
  starting transfers between devices  58.4 us (22%)
  other arithmetic  14.7 us (6%)
  local copies, waits for them, and re-layouts  12.3 us (5%)
  matrix products  9.31 us (4%)
    all_to_all x6, blocking collectives, share(): return lax.all_to_all(copies, axis, 0, 0, axis_index_groups=groups)  80 us
    all_to_all x1, waiting for transfers between devices, local(): parts = lax.all_to_all(sums, 'col', 0, 0, axis_index_groups=PARITIES)  26.1 us
    all_to_all x4, starting transfers between devices, share(): return lax.all_to_all(copies, axis, 0, 0, axis_index_groups=groups)  22.9 us
    ppermute x4, waiting for transfers between devices, neighbour(): return lax.ppermute(array, 'col', pairs)  22 us
    all_to_all x4, waiting for transfers between devices, share(): return lax.all_to_all(copies, axis, 0, 0, axis_index_groups=groups)  18 us
    ppermute x3, starting transfers between devices, along_z(): return lax.ppermute(array, 'row', pairs)  16.8 us
    ppermute x3, waiting for transfers between devices, along_z(): return lax.ppermute(array, 'row', pairs)  16.5 us
    ppermute x4, starting transfers between devices, neighbour(): return lax.ppermute(array, 'col', pairs)  10.8 us
  transfers between devices with their start and end apart: 14, of which 10 were waited for; matrix products, arithmetic and copies ran while one was open for 7% of the time, Pallas kernels for 0%

profile of v6, /device:TPU:6, one launch (start us, length us, event | category | flops | bytes accessed | tf_op | source)
XLA Modules:
  0.0 258.7 jit_solution(15949017558814695107)
XLA Ops:
  2.8 8.9 %all-to-all-start = ((bf16[8,512,128]{1,2,0:T(8,128)(2,1)}), bf16[8,512,128]{1,2,0:T(8,128)(2,1)S(1)}, u32[]{:S(2)}, u32[]{:S(2)}) async-start(bf16[8,512,128]{1,2,0:T(8,128)(2,1)} %broadcast_in_dim.30), calls=%async_computation | async-start | bytes 2097152 | tf_op jit(solution)/shard_map/all_to_all | solution.py:42
  11.7 10.0 %collective-permute-start = (bf16[64,1024]{1,0:T(8,128)(2,1)S(1)}, bf16[64,1024]{1,0:T(8,128)(2,1)S(1)}, u32[]{:S(2)}, u32[]{:S(2)}) collective-permute-start(bf16[64,1024]{1,0:T(8,128)(2,1)S(1)} %copy-done.7), channel_id=1, source_target_pairs={{0,384},{16,400},{32,416},{48,432},{64,448},{80,464},{96,480},{112... | collective-permute-start | bytes 393224 | tf_op jit(solution)/shard_map/ppermute | solution.py:23
  21.7 1.9 collective-permute-start.2
  23.7 4.8 %collective-permute-start.1 = (bf16[64,1024]{1,0:T(8,128)(2,1)S(1)}, bf16[64,1024]{1,0:T(8,128)(2,1)S(1)}, u32[]{:S(2)}, u32[]{:S(2)}) collective-permute-start(bf16[64,1024]{1,0:T(8,128)(2,1)S(1)} %copy-done.7), channel_id=1, source_target_pairs={{0,256},{16,272},{32,288},{48,304},{64,320},{80,336},{96,352},{112... | collective-permute-start | bytes 393224 | tf_op jit(solution)/shard_map/ppermute | solution.py:23
  28.7 16.0 %collective-permute-done.1 = bf16[64,1024]{1,0:T(8,128)(2,1)S(1)} collective-permute-done((bf16[64,1024]{1,0:T(8,128)(2,1)S(1)}, bf16[64,1024]{1,0:T(8,128)(2,1)S(1)}, u32[]{:S(2)}, u32[]{:S(2)}) %collective-permute-start.1) | collective-permute-done | bytes 131104 | tf_op jit(solution)/shard_map/ppermute | solution.py:23
  46.3 1.9 collective-permute-start.3
  49.9 4.8 %all-to-all-start.1 = ((bf16[4,4,64,1024]{3,2,1,0:T(8,128)(2,1)}), bf16[4,4,64,1024]{3,2,1,0:T(8,128)(2,1)S(1)}, u32[]{:S(2)}, u32[]{:S(2)}) async-start(bf16[4,4,64,1024]{3,2,1,0:T(8,128)(2,1)} %broadcast_in_dim.36), calls=%async_computation.1 | async-start | bytes 4194304 | tf_op jit(solution)/shard_map/all_to_all | solution.py:42
  54.7 3.7 %collective-permute-start.4 = (bf16[4,512,128]{1,2,0:T(8,128)(2,1)}, bf16[4,512,128]{1,2,0:T(8,128)(2,1)}, u32[]{:S(2)}, u32[]{:S(2)}) collective-permute-start(bf16[4,512,128]{1,2,0:T(8,128)(2,1)} %get-tuple-element.45), channel_id=1, source_target_pairs={{0,7},{1,2},{2,1},{3,4},{4,3},{5,6},{6,5},{7,0},{8,15},{9,10},{10,... | collective-permute-start | bytes 1572872 | tf_op jit(solution)/shard_map/ppermute | solution.py:36
  58.4 3.5 %collective-permute-done.3 = bf16[4,512,128]{1,2,0:T(8,128)(2,1)} collective-permute-done((bf16[4,512,128]{1,2,0:T(8,128)(2,1)}, bf16[4,512,128]{1,2,0:T(8,128)(2,1)}, u32[]{:S(2)}, u32[]{:S(2)}) %collective-permute-start.3) | collective-permute-done | bytes 524320 | tf_op jit(solution)/shard_map/ppermute | solution.py:36
  62.9 7.9 %collective-permute-done.4 = bf16[4,512,128]{1,2,0:T(8,128)(2,1)} collective-permute-done((bf16[4,512,128]{1,2,0:T(8,128)(2,1)}, bf16[4,512,128]{1,2,0:T(8,128)(2,1)}, u32[]{:S(2)}, u32[]{:S(2)}) %collective-permute-start.4) | collective-permute-done | bytes 524320 | tf_op jit(solution)/shard_map/ppermute | solution.py:36
  73.9 4.6 %all-to-all-done.1 = bf16[4,4,64,1024]{3,2,1,0:T(8,128)(2,1)S(1)} async-done(((bf16[4,4,64,1024]{3,2,1,0:T(8,128)(2,1)}), bf16[4,4,64,1024]{3,2,1,0:T(8,128)(2,1)S(1)}, u32[]{:S(2)}, u32[]{:S(2)}) %all-to-all-start.1) | async-done | bytes 2097184 | tf_op jit(solution)/shard_map/all_to_all | solution.py:42
  78.5 1.9 collective-permute-start.5
  80.9 2.4 collective-permute-start.6
  86.6 13.7 %all_to_all.69 = f32[16,1,512]{2,1,0:T(1,128)S(1)} all-to-all(f32[16,1,512]{2,1,0:T(1,128)S(1)} %broadcast_in_dim.37), channel_id=1, replica_groups=mesh['row'=32,'col'=16] {'col'}, dimensions={0} | all-to-all | bytes 65536 | tf_op jit(solution)/shard_map/all_to_all | solution.py:42
  101.1 16.3 %all_to_all.70 = f32[32,1,1024]{2,1,0:T(1,128)S(1)} all-to-all(f32[32,1,1024]{2,1,0:T(1,128)S(1)} %broadcast_in_dim.38), channel_id=1, replica_groups=mesh['row'=32,'col'=16] {'row'}, dimensions={0} | all-to-all | bytes 262144 | tf_op jit(solution)/shard_map/all_to_all | solution.py:42
  118.2 11.1 %all_to_all.71 = f32[16,1,512]{2,1,0:T(1,128)S(1)} all-to-all(f32[16,1,512]{2,1,0:T(1,128)S(1)} %broadcast_in_dim.39), channel_id=1, replica_groups=mesh['row'=32,'col'=16] {'col'}, dimensions={0} | all-to-all | bytes 65536 | tf_op jit(solution)/shard_map/all_to_all | solution.py:42
  129.9 13.9 %all_to_all.72 = f32[32,1,1024]{2,1,0:T(1,128)S(1)} all-to-all(f32[32,1,1024]{2,1,0:T(1,128)S(1)} %broadcast_in_dim.40), channel_id=1, replica_groups=mesh['row'=32,'col'=16] {'row'}, dimensions={0} | all-to-all | bytes 262144 | tf_op jit(solution)/shard_map/all_to_all | solution.py:42
  144.6 11.1 %all_to_all.73 = f32[16,1,512]{2,1,0:T(1,128)S(1)} all-to-all(f32[16,1,512]{2,1,0:T(1,128)S(1)} %broadcast_in_dim.41), channel_id=1, replica_groups=mesh['row'=32,'col'=16] {'col'}, dimensions={0} | all-to-all | bytes 65536 | tf_op jit(solution)/shard_map/all_to_all | solution.py:42
  156.4 13.9 %all_to_all.74 = f32[32,1,1024]{2,1,0:T(1,128)S(1)} all-to-all(f32[32,1,1024]{2,1,0:T(1,128)S(1)} %broadcast_in_dim.42), channel_id=1, replica_groups=mesh['row'=32,'col'=16] {'row'}, dimensions={0} | all-to-all | bytes 262144 | tf_op jit(solution)/shard_map/all_to_all | solution.py:42
  171.6 3.7 %all-to-all-start.8 = ((f32[16,1,512]{2,1,0:T(1,128)}), f32[16,1,512]{2,1,0:T(1,128)S(1)}, u32[]{:S(2)}, u32[]{:S(2)}) async-start(f32[16,1,512]{2,1,0:T(1,128)} %broadcast_in_dim.43), calls=%async_computation.8 | async-start | bytes 65536 | tf_op jit(solution)/shard_map/all_to_all | solution.py:42
  175.3 8.5 %all-to-all-done.8 = f32[16,1,512]{2,1,0:T(1,128)S(1)} async-done(((f32[16,1,512]{2,1,0:T(1,128)}), f32[16,1,512]{2,1,0:T(1,128)S(1)}, u32[]{:S(2)}, u32[]{:S(2)}) %all-to-all-start.8) | async-done | bytes 32800 | tf_op jit(solution)/shard_map/all_to_all | solution.py:42
  185.1 5.6 %all-to-all-start.9 = ((f32[32,1,1024]{2,1,0:T(1,128)}), f32[32,1,1024]{2,1,0:T(1,128)S(1)}, u32[]{:S(2)}, u32[]{:S(2)}) async-start(f32[32,1,1024]{2,1,0:T(1,128)} %broadcast_in_dim.44), calls=%async_computation.9 | async-start | bytes 262144 | tf_op jit(solution)/shard_map/all_to_all | solution.py:42
  190.7 1.7 fusion.5
  194.7 4.9 %all-to-all-done.9 = f32[32,1,1024]{2,1,0:T(1,128)S(1)} async-done(((f32[32,1,1024]{2,1,0:T(1,128)}), f32[32,1,1024]{2,1,0:T(1,128)S(1)}, u32[]{:S(2)}, u32[]{:S(2)}) %all-to-all-start.9) | async-done | bytes 131104 | tf_op jit(solution)/shard_map/all_to_all | solution.py:42
  202.4 2.8 %collective-permute-start.7 = (bf16[512,512]{1,0:T(8,128)(2,1)}, bf16[512,512]{1,0:T(8,128)(2,1)}, u32[]{:S(2)}, u32[]{:S(2)}) collective-permute-start(bf16[512,512]{1,0:T(8,128)(2,1)} %convolution_convert_fusion.1), channel_id=1, source_target_pairs={{0,1},{1,0},{2,3},{3,2},{4,5},{5,4},{6,7},{7,6},{8,9},{9,8},{10,11... | collective-permute-start | bytes 1572872 | tf_op jit(solution)/shard_map/ppermute | solution.py:36
  206.8 2.5 collective-permute-start.8
  211.7 7.3 %collective-permute-done.7 = bf16[512,512]{1,0:T(8,128)(2,1)} collective-permute-done((bf16[512,512]{1,0:T(8,128)(2,1)}, bf16[512,512]{1,0:T(8,128)(2,1)}, u32[]{:S(2)}, u32[]{:S(2)}) %collective-permute-start.7) | collective-permute-done | bytes 524320 | tf_op jit(solution)/shard_map/ppermute | solution.py:36
  219.0 1.8 fusion.6
  220.8 3.3 %collective-permute-done.8 = bf16[512,512]{1,0:T(8,128)(2,1)} collective-permute-done((bf16[512,512]{1,0:T(8,128)(2,1)}, bf16[512,512]{1,0:T(8,128)(2,1)}, u32[]{:S(2)}, u32[]{:S(2)}) %collective-permute-start.8) | collective-permute-done | bytes 524320 | tf_op jit(solution)/shard_map/ppermute | solution.py:36
  224.1 1.8 fusion.7
  227.0 3.6 %all-to-all-start.10 = ((bf16[8,128,512]{2,1,0:T(8,128)(2,1)}), bf16[8,128,512]{2,1,0:T(8,128)(2,1)S(1)}, u32[]{:S(2)}, u32[]{:S(2)}) async-start(bf16[8,128,512]{2,1,0:T(8,128)(2,1)} %bitcast.29), calls=%async_computation.10 | async-start | bytes 2097152 | tf_op jit(solution)/shard_map/all_to_all | solution.py:136
  231.7 26.1 %all-to-all-done.10 = bf16[8,128,512]{2,1,0:T(8,128)(2,1)S(1)} async-done(((bf16[8,128,512]{2,1,0:T(8,128)(2,1)}), bf16[8,128,512]{2,1,0:T(8,128)(2,1)S(1)}, u32[]{:S(2)}, u32[]{:S(2)}) %all-to-all-start.10) | async-done | bytes 1048608 | tf_op jit(solution)/shard_map/all_to_all | solution.py:136
  (93 shorter events, 31.6 us)
Async XLA Ops:
  0.6 11.1 %copy-start.7 = (bf16[64,1024]{1,0:T(8,128)(2,1)S(1)}, bf16[64,1024]{1,0:T(8,128)(2,1)}, u32[]{:S(2)}) copy-start(bf16[64,1024]{1,0:T(8,128)(2,1)} %param.3) | copy-start | bytes 393220
  2.8 42.5 %all-to-all-start = ((bf16[8,512,128]{1,2,0:T(8,128)(2,1)}), bf16[8,512,128]{1,2,0:T(8,128)(2,1)S(1)}, u32[]{:S(2)}, u32[]{:S(2)}) async-start(bf16[8,512,128]{1,2,0:T(8,128)(2,1)} %broadcast_in_dim.30), calls=%async_computation | async-start | bytes 2097152 | tf_op jit(solution)/shard_map/all_to_all | solution.py:42
  11.7 17.0 %collective-permute-start = (bf16[64,1024]{1,0:T(8,128)(2,1)S(1)}, bf16[64,1024]{1,0:T(8,128)(2,1)S(1)}, u32[]{:S(2)}, u32[]{:S(2)}) collective-permute-start(bf16[64,1024]{1,0:T(8,128)(2,1)S(1)} %copy-done.7), channel_id=1, source_target_pairs={{0,384},{16,400},{32,416},{48,432},{64,448},{80,464},{96,480},{112... | collective-permute-start | bytes 393224 | tf_op jit(solution)/shard_map/ppermute | solution.py:23
  21.7 23.5 %collective-permute-start.2 = (bf16[64,1024]{1,0:T(8,128)(2,1)S(1)}, bf16[64,1024]{1,0:T(8,128)(2,1)S(1)}, u32[]{:S(2)}, u32[]{:S(2)}) collective-permute-start(bf16[64,1024]{1,0:T(8,128)(2,1)S(1)} %copy-done.7), channel_id=1, source_target_pairs={{0,128},{16,144},{32,160},{48,176},{64,192},{80,208},{96,224},{112... | collective-permute-start | bytes 393224 | tf_op jit(solution)/shard_map/ppermute | solution.py:23
  23.7 21.0 %collective-permute-start.1 = (bf16[64,1024]{1,0:T(8,128)(2,1)S(1)}, bf16[64,1024]{1,0:T(8,128)(2,1)S(1)}, u32[]{:S(2)}, u32[]{:S(2)}) collective-permute-start(bf16[64,1024]{1,0:T(8,128)(2,1)S(1)} %copy-done.7), channel_id=1, source_target_pairs={{0,256},{16,272},{32,288},{48,304},{64,320},{80,336},{96,352},{112... | collective-permute-start | bytes 393224 | tf_op jit(solution)/shard_map/ppermute | solution.py:23
  46.3 15.5 %collective-permute-start.3 = (bf16[4,512,128]{1,2,0:T(8,128)(2,1)}, bf16[4,512,128]{1,2,0:T(8,128)(2,1)}, u32[]{:S(2)}, u32[]{:S(2)}) collective-permute-start(bf16[4,512,128]{1,2,0:T(8,128)(2,1)} %get-tuple-element.46), channel_id=1, source_target_pairs={{0,1},{1,0},{2,3},{3,2},{4,5},{5,4},{6,7},{7,6},{8,9},{9,8},{10,11... | collective-permute-start | bytes 1572872 | tf_op jit(solution)/shard_map/ppermute | solution.py:36
  49.9 28.7 %all-to-all-start.1 = ((bf16[4,4,64,1024]{3,2,1,0:T(8,128)(2,1)}), bf16[4,4,64,1024]{3,2,1,0:T(8,128)(2,1)S(1)}, u32[]{:S(2)}, u32[]{:S(2)}) async-start(bf16[4,4,64,1024]{3,2,1,0:T(8,128)(2,1)} %broadcast_in_dim.36), calls=%async_computation.1 | async-start | bytes 4194304 | tf_op jit(solution)/shard_map/all_to_all | solution.py:42
  54.7 16.1 %collective-permute-start.4 = (bf16[4,512,128]{1,2,0:T(8,128)(2,1)}, bf16[4,512,128]{1,2,0:T(8,128)(2,1)}, u32[]{:S(2)}, u32[]{:S(2)}) collective-permute-start(bf16[4,512,128]{1,2,0:T(8,128)(2,1)} %get-tuple-element.45), channel_id=1, source_target_pairs={{0,7},{1,2},{2,1},{3,4},{4,3},{5,6},{6,5},{7,0},{8,15},{9,10},{10,... | collective-permute-start | bytes 1572872 | tf_op jit(solution)/shard_map/ppermute | solution.py:36
  78.5 6.1 %copy-start = (bf16[4,4,64,1024]{3,2,1,0:T(8,128)(2,1)}, bf16[4,4,64,1024]{3,2,1,0:T(8,128)(2,1)S(1)}, u32[]{:S(2)}) copy-start(bf16[4,4,64,1024]{3,2,1,0:T(8,128)(2,1)S(1)} %all-to-all-done.1) | copy-start | bytes 6291460
  78.5 6.1 %collective-permute-start.5 = (bf16[4,4,64,1024]{3,2,1,0:T(8,128)(2,1)S(1)}, bf16[4,4,64,1024]{3,2,1,0:T(8,128)(2,1)S(1)}, u32[]{:S(2)}, u32[]{:S(2)}) collective-permute-start(bf16[4,4,64,1024]{3,2,1,0:T(8,128)(2,1)S(1)} %all-to-all-done.1), channel_id=1, source_target_pairs={{0,16},{16,0},{32,48},{48,32},{64,80},{80,64},{96,112},{112,96},{1... | collective-permute-start | bytes 6291464 | tf_op jit(solution)/shard_map/ppermute | solution.py:27
  80.9 3.7 %collective-permute-start.6 = (f32[1024]{0:T(1024)S(1)}, f32[1024]{0:T(1024)S(1)}, u32[]{:S(2)}, u32[]{:S(2)}) collective-permute-start(f32[1024]{0:T(1024)S(1)} %multiply_reduce_fusion), channel_id=1, source_target_pairs={{0,16},{16,0},{32,48},{48,32},{64,80},{80,64},{96,112},{112,96},{1... | collective-permute-start | bytes 12296 | tf_op jit(solution)/shard_map/ppermute | solution.py:27
  83.3 1.3 copy-start.4
  84.7 1.4 copy-start.2
  171.6 12.2 %all-to-all-start.8 = ((f32[16,1,512]{2,1,0:T(1,128)}), f32[16,1,512]{2,1,0:T(1,128)S(1)}, u32[]{:S(2)}, u32[]{:S(2)}) async-start(f32[16,1,512]{2,1,0:T(1,128)} %broadcast_in_dim.43), calls=%async_computation.8 | async-start | bytes 65536 | tf_op jit(solution)/shard_map/all_to_all | solution.py:42
  185.1 14.5 %all-to-all-start.9 = ((f32[32,1,1024]{2,1,0:T(1,128)}), f32[32,1,1024]{2,1,0:T(1,128)S(1)}, u32[]{:S(2)}, u32[]{:S(2)}) async-start(f32[32,1,1024]{2,1,0:T(1,128)} %broadcast_in_dim.44), calls=%async_computation.9 | async-start | bytes 262144 | tf_op jit(solution)/shard_map/all_to_all | solution.py:42
  199.7 1.2 copy-start.6
  200.2 5.0 %copy-start.5 = (bf16[1,4,2,64,1024]{4,3,2,1,0:T(8,128)(2,1)S(1)}, bf16[1,4,2,64,1024]{4,3,2,1,0:T(8,128)(2,1)}, u32[]{:S(2)}) copy-start(bf16[1,4,2,64,1024]{4,3,2,1,0:T(8,128)(2,1)} %copy.50) | copy-start | bytes 3145732
  202.4 6.9 %copy-start.1 = (bf16[4,4,64,1024]{3,2,1,0:T(8,128)(2,1)S(1)}, bf16[4,4,64,1024]{3,2,1,0:T(8,128)(2,1)}, u32[]{:S(2)}) copy-start(bf16[4,4,64,1024]{3,2,1,0:T(8,128)(2,1)} %copy-done) | copy-start | bytes 6291460
  202.4 16.6 %collective-permute-start.7 = (bf16[512,512]{1,0:T(8,128)(2,1)}, bf16[512,512]{1,0:T(8,128)(2,1)}, u32[]{:S(2)}, u32[]{:S(2)}) collective-permute-start(bf16[512,512]{1,0:T(8,128)(2,1)} %convolution_convert_fusion.1), channel_id=1, source_target_pairs={{0,1},{1,0},{2,3},{3,2},{4,5},{5,4},{6,7},{7,6},{8,9},{9,8},{10,11... | collective-permute-start | bytes 1572872 | tf_op jit(solution)/shard_map/ppermute | solution.py:36
  206.8 17.3 %collective-permute-start.8 = (bf16[512,512]{1,0:T(8,128)(2,1)}, bf16[512,512]{1,0:T(8,128)(2,1)}, u32[]{:S(2)}, u32[]{:S(2)}) collective-permute-start(bf16[512,512]{1,0:T(8,128)(2,1)} %convolution_convert_fusion), channel_id=1, source_target_pairs={{0,7},{1,2},{2,1},{3,4},{4,3},{5,6},{6,5},{7,0},{8,15},{9,10},{10,... | collective-permute-start | bytes 1572872 | tf_op jit(solution)/shard_map/ppermute | solution.py:36
  209.3 1.9 copy-start.3
  227.0 30.9 %all-to-all-start.10 = ((bf16[8,128,512]{2,1,0:T(8,128)(2,1)}), bf16[8,128,512]{2,1,0:T(8,128)(2,1)S(1)}, u32[]{:S(2)}, u32[]{:S(2)}) async-start(bf16[8,128,512]{2,1,0:T(8,128)(2,1)} %bitcast.29), calls=%async_computation.10 | async-start | bytes 2097152 | tf_op jit(solution)/shard_map/all_to_all | solution.py:136

commit v7 on v6

--- a/solution.py
+++ b/solution.py
@@ -19,7 +19,7 @@
 
 def along_z(array, by):
     step = X * CORE
-    pairs = [(i, (i + by * step) % (Z_HI * step)) for i in range(Z_HI * step)]
+    pairs = [(i, (i + by[i % CORE] * step) % (Z_HI * step)) for i in range(Z_HI * step)]
     return lax.ppermute(array, "row", pairs)
 
 
@@ -43,11 +43,13 @@
 
 
 def gather(noise, data):
-    z = lax.axis_index("row") // (X * CORE)
+    row = lax.axis_index("row")
+    z, core = row // (X * CORE), row % CORE
     same = share(noise, "col", PARITIES)
     plane = jnp.zeros((Z_HI,) + data.shape, data.dtype)
-    pieces = (data, along_z(data, -1), along_z(data, 2), along_z(data, 1))
-    for by, piece in enumerate(pieces):
+    up, down = along_z(data, (1, 1)), along_z(data, (-1, -1))
+    far = along_z(jnp.where(core == 0, up, down), (1, -1))
+    for by, piece in enumerate((data, down, far, up)):
         plane = lax.dynamic_update_slice(plane, piece[None], ((z + by) % Z_HI, 0, 0))
     return lax.optimization_barrier((same, plane))
 
@@ -109,6 +111,9 @@
         by_row = (lift / rows_all) / jnp.sum(share(part, "col"), axis=0)
         part = jnp.sum(plan * by_row[:, None], axis=0)
         by_col = (lift / cols_all) / jnp.sum(share(part, "row"), axis=0)
+    row_potential = noise_sq / width + EPS * (row_first + jnp.log(by_row))
+    col_potential = data_sq / width + EPS * (col_first + jnp.log(by_col))
+
     weights = (plan * ((rows_all / lift) * by_row)[:, None] * by_col[None, :]).astype(
         jnp.bfloat16
     )
@@ -126,9 +131,6 @@
 
     sent = [terms(part).astype(jnp.bfloat16) for part in features(away)]
     got = [neighbour(part, by) for part, by in zip(sent, (1, -1))]
-    sent, kept, by_row, by_col = lax.optimization_barrier((sent[0], kept, by_row, by_col))
-    row_potential = noise_sq / width + EPS * (row_first + jnp.log(by_row))
-    col_potential = data_sq / width + EPS * (col_first + jnp.log(by_col))
     sums = [
         (terms(own) + add).astype(jnp.bfloat16) for own, add in zip(features(kept), got)
     ]

time: 262 us -> 261 us (level)
  waiting for transfers between devices: 82.6 us -> 49.6 us
  blocking collectives: 80 us -> 103 us
  starting transfers between devices: 58.4 us -> 70.4 us
  matrix products: 9.31 us -> 5.75 us
    all_to_all x0 -> x1, blocking collectives: none -> 30.6 us  [local(): parts = lax.all_to_all(sums, 'col', 0, 0, axis_index_groups=PARITIES)]
    all_to_all x1 -> x0, waiting for transfers between devices: 26.1 us -> none  [local(): parts = lax.all_to_all(sums, 'col', 0, 0, axis_index_groups=PARITIES)]
    ppermute x4, starting transfers between devices: 10.8 us -> 21.3 us  [neighbour(): return lax.ppermute(array, 'col', pairs)]
    all_to_all x6 -> x5, blocking collectives: 80 us -> 72.5 us  [share(): return lax.all_to_all(copies, axis, 0, 0, axis_index_groups=groups)]
    all_to_all x4 -> x5, starting transfers between devices: 22.9 us -> 28.6 us  [share(): return lax.all_to_all(copies, axis, 0, 0, axis_index_groups=groups)]
    ppermute x3, waiting for transfers between devices: 16.5 us -> 11.6 us  [along_z(): return lax.ppermute(array, 'row', pairs)]
    dot_general x4, matrix products: 6.65 us -> 3.1 us  [terms(): lax.dot_general(part, weights, contract, preferred_element_type=jnp.float32)]
    all_to_all x1 -> x0, starting transfers between devices: 3.56 us -> none  [local(): parts = lax.all_to_all(sums, 'col', 0, 0, axis_index_groups=PARITIES)]
  transfers between devices with their start and end apart: 14 -> 14, of which waited for: 10 -> 8; matrix products, arithmetic and copies ran while one was open for 7% -> 7% of each run, Pallas kernels for 0% -> 0%
where the time goes in v7:
time: 261 us; the launch traced here: 258 us
  blocking collectives  103 us (39%)
  starting transfers between devices  70.4 us (27%)
  waiting for transfers between devices  49.6 us (19%)
  other arithmetic  15.9 us (6%)
  local copies, waits for them, and re-layouts  12.1 us (5%)
  matrix products  5.75 us (2%)
    all_to_all x5, blocking collectives, share(): return lax.all_to_all(copies, axis, 0, 0, axis_index_groups=groups)  72.5 us
    all_to_all x1, blocking collectives, local(): parts = lax.all_to_all(sums, 'col', 0, 0, axis_index_groups=PARITIES)  30.6 us
    all_to_all x5, starting transfers between devices, share(): return lax.all_to_all(copies, axis, 0, 0, axis_index_groups=groups)  28.6 us
    ppermute x4, starting transfers between devices, neighbour(): return lax.ppermute(array, 'col', pairs)  21.3 us
    ppermute x4, waiting for transfers between devices, neighbour(): return lax.ppermute(array, 'col', pairs)  19.7 us
    all_to_all x5, waiting for transfers between devices, share(): return lax.all_to_all(copies, axis, 0, 0, axis_index_groups=groups)  18.3 us
    ppermute x3, starting transfers between devices, along_z(): return lax.ppermute(array, 'row', pairs)  16.2 us
    ppermute x3, waiting for transfers between devices, along_z(): return lax.ppermute(array, 'row', pairs)  11.6 us
  transfers between devices with their start and end apart: 14, of which 8 were waited for; matrix products, arithmetic and copies ran while one was open for 7% of the time, Pallas kernels for 0%

profile of v7, /device:TPU:6, one launch (start us, length us, event | category | flops | bytes accessed | tf_op | source)
XLA Modules:
  0.0 258.2 jit_solution(3814429554792687703)
XLA Ops:
  2.8 8.9 %all-to-all-start = ((bf16[8,512,128]{1,2,0:T(8,128)(2,1)}), bf16[8,512,128]{1,2,0:T(8,128)(2,1)S(1)}, u32[]{:S(2)}, u32[]{:S(2)}) async-start(bf16[8,512,128]{1,2,0:T(8,128)(2,1)} %broadcast_in_dim.30), calls=%async_computation | async-start | bytes 2097152 | tf_op jit(solution)/shard_map/all_to_all | solution.py:42
  11.7 6.1 %collective-permute-start.1 = (bf16[64,1024]{1,0:T(8,128)(2,1)S(1)}, bf16[64,1024]{1,0:T(8,128)(2,1)S(1)}, u32[]{:S(2)}, u32[]{:S(2)}) collective-permute-start(bf16[64,1024]{1,0:T(8,128)(2,1)S(1)} %copy-done.7), channel_id=1, source_target_pairs={{0,128},{16,144},{32,160},{48,176},{64,192},{80,208},{96,224},{112... | collective-permute-start | bytes 393224 | tf_op jit(solution)/shard_map/ppermute | solution.py:23
  17.8 5.9 %collective-permute-start = (bf16[64,1024]{1,0:T(8,128)(2,1)S(1)}, bf16[64,1024]{1,0:T(8,128)(2,1)S(1)}, u32[]{:S(2)}, u32[]{:S(2)}) collective-permute-start(bf16[64,1024]{1,0:T(8,128)(2,1)S(1)} %copy-done.7), channel_id=1, source_target_pairs={{0,384},{16,400},{32,416},{48,432},{64,448},{80,464},{96,480},{112... | collective-permute-start | bytes 393224 | tf_op jit(solution)/shard_map/ppermute | solution.py:23
  23.8 5.5 %collective-permute-done.1 = bf16[64,1024]{1,0:T(8,128)(2,1)S(1)} collective-permute-done((bf16[64,1024]{1,0:T(8,128)(2,1)S(1)}, bf16[64,1024]{1,0:T(8,128)(2,1)S(1)}, u32[]{:S(2)}, u32[]{:S(2)}) %collective-permute-start.1) | collective-permute-done | bytes 131104 | tf_op jit(solution)/shard_map/ppermute | solution.py:23
  29.4 4.2 %collective-permute-start.2 = (bf16[64,1024]{1,0:T(8,128)(2,1)S(1)}, bf16[64,1024]{1,0:T(8,128)(2,1)S(1)}, u32[]{:S(2)}, u32[]{:S(2)}) collective-permute-start(bf16[64,1024]{1,0:T(8,128)(2,1)S(1)} %broadcast_select_fusion.4), channel_id=1, source_target_pairs={{0,128},{16,400},{32,160},{48,432},{64,192},{80,464},{96,224},{112... | collective-permute-start | bytes 393224 | tf_op jit(solution)/shard_map/ppermute | solution.py:23
  33.6 6.1 %collective-permute-done.2 = bf16[64,1024]{1,0:T(8,128)(2,1)S(1)} collective-permute-done((bf16[64,1024]{1,0:T(8,128)(2,1)S(1)}, bf16[64,1024]{1,0:T(8,128)(2,1)S(1)}, u32[]{:S(2)}, u32[]{:S(2)}) %collective-permute-start.2) | collective-permute-done | bytes 131104 | tf_op jit(solution)/shard_map/ppermute | solution.py:23
  40.9 3.8 %collective-permute-start.3 = (bf16[4,512,128]{1,2,0:T(8,128)(2,1)}, bf16[4,512,128]{1,2,0:T(8,128)(2,1)}, u32[]{:S(2)}, u32[]{:S(2)}) collective-permute-start(bf16[4,512,128]{1,2,0:T(8,128)(2,1)} %get-tuple-element.39), channel_id=1, source_target_pairs={{0,1},{1,0},{2,3},{3,2},{4,5},{5,4},{6,7},{7,6},{8,9},{9,8},{10,11... | collective-permute-start | bytes 1572872 | tf_op jit(solution)/shard_map/ppermute | solution.py:36
  44.6 1.6 broadcast_in_dim.36
  46.3 4.8 %all-to-all-start.1 = ((bf16[4,4,64,1024]{3,2,1,0:T(8,128)(2,1)}), bf16[4,4,64,1024]{3,2,1,0:T(8,128)(2,1)S(1)}, u32[]{:S(2)}, u32[]{:S(2)}) async-start(bf16[4,4,64,1024]{3,2,1,0:T(8,128)(2,1)} %broadcast_in_dim.36), calls=%async_computation.1 | async-start | bytes 4194304 | tf_op jit(solution)/shard_map/all_to_all | solution.py:42
  51.0 12.2 %collective-permute-start.4 = (bf16[4,512,128]{1,2,0:T(8,128)(2,1)}, bf16[4,512,128]{1,2,0:T(8,128)(2,1)}, u32[]{:S(2)}, u32[]{:S(2)}) collective-permute-start(bf16[4,512,128]{1,2,0:T(8,128)(2,1)} %get-tuple-element.38), channel_id=1, source_target_pairs={{0,7},{1,2},{2,1},{3,4},{4,3},{5,6},{6,5},{7,0},{8,15},{9,10},{10,... | collective-permute-start | bytes 1572872 | tf_op jit(solution)/shard_map/ppermute | solution.py:36
  64.3 6.4 %collective-permute-done.4 = bf16[4,512,128]{1,2,0:T(8,128)(2,1)} collective-permute-done((bf16[4,512,128]{1,2,0:T(8,128)(2,1)}, bf16[4,512,128]{1,2,0:T(8,128)(2,1)}, u32[]{:S(2)}, u32[]{:S(2)}) %collective-permute-start.4) | collective-permute-done | bytes 524320 | tf_op jit(solution)/shard_map/ppermute | solution.py:36
  73.8 1.9 collective-permute-start.5
  76.2 2.4 collective-permute-start.6
  80.0 1.4 subtract_reduce_fusion
  81.9 20.5 %all_to_all.69 = f32[16,1,512]{2,1,0:T(1,128)S(1)} all-to-all(f32[16,1,512]{2,1,0:T(1,128)S(1)} %broadcast_in_dim.37), channel_id=1, replica_groups=mesh['row'=32,'col'=16] {'col'}, dimensions={0} | all-to-all | bytes 65536 | tf_op jit(solution)/shard_map/all_to_all | solution.py:42
  103.2 15.9 %all_to_all.70 = f32[32,1,1024]{2,1,0:T(1,128)S(1)} all-to-all(f32[32,1,1024]{2,1,0:T(1,128)S(1)} %broadcast_in_dim.38), channel_id=1, replica_groups=mesh['row'=32,'col'=16] {'row'}, dimensions={0} | all-to-all | bytes 262144 | tf_op jit(solution)/shard_map/all_to_all | solution.py:42
  119.9 11.1 %all_to_all.71 = f32[16,1,512]{2,1,0:T(1,128)S(1)} all-to-all(f32[16,1,512]{2,1,0:T(1,128)S(1)} %broadcast_in_dim.39), channel_id=1, replica_groups=mesh['row'=32,'col'=16] {'col'}, dimensions={0} | all-to-all | bytes 65536 | tf_op jit(solution)/shard_map/all_to_all | solution.py:42
  131.6 13.9 %all_to_all.72 = f32[32,1,1024]{2,1,0:T(1,128)S(1)} all-to-all(f32[32,1,1024]{2,1,0:T(1,128)S(1)} %broadcast_in_dim.40), channel_id=1, replica_groups=mesh['row'=32,'col'=16] {'row'}, dimensions={0} | all-to-all | bytes 262144 | tf_op jit(solution)/shard_map/all_to_all | solution.py:42
  146.3 11.1 %all_to_all.73 = f32[16,1,512]{2,1,0:T(1,128)S(1)} all-to-all(f32[16,1,512]{2,1,0:T(1,128)S(1)} %broadcast_in_dim.41), channel_id=1, replica_groups=mesh['row'=32,'col'=16] {'col'}, dimensions={0} | all-to-all | bytes 65536 | tf_op jit(solution)/shard_map/all_to_all | solution.py:42
  158.7 5.7 %all-to-all-start.7 = ((f32[32,1,1024]{2,1,0:T(1,128)}), f32[32,1,1024]{2,1,0:T(1,128)S(1)}, u32[]{:S(2)}, u32[]{:S(2)}) async-start(f32[32,1,1024]{2,1,0:T(1,128)} %broadcast_in_dim.42), calls=%async_computation.7 | async-start | bytes 262144 | tf_op jit(solution)/shard_map/all_to_all | solution.py:42
  164.4 8.9 %all-to-all-done.7 = f32[32,1,1024]{2,1,0:T(1,128)S(1)} async-done(((f32[32,1,1024]{2,1,0:T(1,128)}), f32[32,1,1024]{2,1,0:T(1,128)S(1)}, u32[]{:S(2)}, u32[]{:S(2)}) %all-to-all-start.7) | async-done | bytes 131104 | tf_op jit(solution)/shard_map/all_to_all | solution.py:42
  174.6 3.7 %all-to-all-start.8 = ((f32[16,1,512]{2,1,0:T(1,128)}), f32[16,1,512]{2,1,0:T(1,128)S(1)}, u32[]{:S(2)}, u32[]{:S(2)}) async-start(f32[16,1,512]{2,1,0:T(1,128)} %broadcast_in_dim.43), calls=%async_computation.8 | async-start | bytes 65536 | tf_op jit(solution)/shard_map/all_to_all | solution.py:42
  178.3 3.8 %fusion.3 = (bf16[2,4,1,64,1024]{4,3,1,0,2:T(8,128)(2,1)}, bf16[2,4,1,64,1024]{4,3,1,0,2:T(8,128)(2,1)S(1)}, bf16[2,4,1,64,1024]{4,3,1,0,2:T(8,128)(2,1)}) fusion(pred[]{:T(512)S(6)} %eq.21, bf16[2,2,4,64,1024]{4,3,2,1,0:T(8,128)(2,1)} %bitcast.89, s32[]{:T(128)S(6)} %select_n.187, bf16[2,2,4,64,1024]{4,3,2,1,0:T(8,128)(2,1)} %bitcast.86, s32[]{:T(128)S(6)} %select_n.182), kind=kLoop, calls=%fused_computation.32 | loop fusion | flops 1572864 | bytes 7340041 | tf_op jit(solution)/shard_map/jit(_where)/select_n | solution.py:125
  182.1 4.7 %all-to-all-done.8 = f32[16,1,512]{2,1,0:T(1,128)S(1)} async-done(((f32[16,1,512]{2,1,0:T(1,128)}), f32[16,1,512]{2,1,0:T(1,128)S(1)}, u32[]{:S(2)}, u32[]{:S(2)}) %all-to-all-start.8) | async-done | bytes 32800 | tf_op jit(solution)/shard_map/all_to_all | solution.py:42
  188.7 5.6 %all-to-all-start.9 = ((f32[32,1,1024]{2,1,0:T(1,128)}), f32[32,1,1024]{2,1,0:T(1,128)S(1)}, u32[]{:S(2)}, u32[]{:S(2)}) async-start(f32[32,1,1024]{2,1,0:T(1,128)} %broadcast_in_dim.44), calls=%async_computation.9 | async-start | bytes 262144 | tf_op jit(solution)/shard_map/all_to_all | solution.py:42
  194.3 1.7 fusion
  198.5 4.7 %all-to-all-done.9 = f32[32,1,1024]{2,1,0:T(1,128)S(1)} async-done(((f32[32,1,1024]{2,1,0:T(1,128)}), f32[32,1,1024]{2,1,0:T(1,128)S(1)}, u32[]{:S(2)}, u32[]{:S(2)}) %all-to-all-start.9) | async-done | bytes 131104 | tf_op jit(solution)/shard_map/all_to_all | solution.py:42
  205.3 2.8 %collective-permute-start.7 = (bf16[512,512]{1,0:T(8,128)(2,1)S(1)}, bf16[512,512]{1,0:T(8,128)(2,1)S(1)}, u32[]{:S(2)}, u32[]{:S(2)}) collective-permute-start(bf16[512,512]{1,0:T(8,128)(2,1)S(1)} %convolution_convert_fusion.1), channel_id=1, source_target_pairs={{0,1},{1,0},{2,3},{3,2},{4,5},{5,4},{6,7},{7,6},{8,9},{9,8},{10,11... | collective-permute-start | bytes 1572872 | tf_op jit(solution)/shard_map/ppermute | solution.py:36
  208.8 2.5 collective-permute-start.8
  211.7 9.8 %collective-permute-done.7 = bf16[512,512]{1,0:T(8,128)(2,1)S(1)} collective-permute-done((bf16[512,512]{1,0:T(8,128)(2,1)S(1)}, bf16[512,512]{1,0:T(8,128)(2,1)S(1)}, u32[]{:S(2)}, u32[]{:S(2)}) %collective-permute-start.7) | collective-permute-done | bytes 524320 | tf_op jit(solution)/shard_map/ppermute | solution.py:36
  222.3 3.6 %collective-permute-done.8 = bf16[512,512]{1,0:T(8,128)(2,1)S(1)} collective-permute-done((bf16[512,512]{1,0:T(8,128)(2,1)S(1)}, bf16[512,512]{1,0:T(8,128)(2,1)S(1)}, u32[]{:S(2)}, u32[]{:S(2)}) %collective-permute-start.8) | collective-permute-done | bytes 524320 | tf_op jit(solution)/shard_map/ppermute | solution.py:36
  226.8 30.6 %all_to_all.74 = bf16[8,128,512]{2,1,0:T(8,128)(2,1)S(1)} all-to-all(bf16[8,128,512]{2,1,0:T(8,128)(2,1)S(1)} %bitcast.92), channel_id=1, replica_groups={{0,4,8,12,2,6,10,14},{1,5,9,13,3,7,11,15},{16,20,24,28,18,22,26,30},{17..., dimensions={0} | all-to-all | bytes 2097152 | tf_op jit(solution)/shard_map/all_to_all | solution.py:138
  (90 shorter events, 25.3 us)
Async XLA Ops:
  0.6 11.1 %copy-start.7 = (bf16[64,1024]{1,0:T(8,128)(2,1)S(1)}, bf16[64,1024]{1,0:T(8,128)(2,1)}, u32[]{:S(2)}) copy-start(bf16[64,1024]{1,0:T(8,128)(2,1)} %param.3) | copy-start | bytes 393220
  2.8 37.0 %all-to-all-start = ((bf16[8,512,128]{1,2,0:T(8,128)(2,1)}), bf16[8,512,128]{1,2,0:T(8,128)(2,1)S(1)}, u32[]{:S(2)}, u32[]{:S(2)}) async-start(bf16[8,512,128]{1,2,0:T(8,128)(2,1)} %broadcast_in_dim.30), calls=%async_computation | async-start | bytes 2097152 | tf_op jit(solution)/shard_map/all_to_all | solution.py:42
  11.7 17.6 %collective-permute-start.1 = (bf16[64,1024]{1,0:T(8,128)(2,1)S(1)}, bf16[64,1024]{1,0:T(8,128)(2,1)S(1)}, u32[]{:S(2)}, u32[]{:S(2)}) collective-permute-start(bf16[64,1024]{1,0:T(8,128)(2,1)S(1)} %copy-done.7), channel_id=1, source_target_pairs={{0,128},{16,144},{32,160},{48,176},{64,192},{80,208},{96,224},{112... | collective-permute-start | bytes 393224 | tf_op jit(solution)/shard_map/ppermute | solution.py:23
  17.8 11.6 %collective-permute-start = (bf16[64,1024]{1,0:T(8,128)(2,1)S(1)}, bf16[64,1024]{1,0:T(8,128)(2,1)S(1)}, u32[]{:S(2)}, u32[]{:S(2)}) collective-permute-start(bf16[64,1024]{1,0:T(8,128)(2,1)S(1)} %copy-done.7), channel_id=1, source_target_pairs={{0,384},{16,400},{32,416},{48,432},{64,448},{80,464},{96,480},{112... | collective-permute-start | bytes 393224 | tf_op jit(solution)/shard_map/ppermute | solution.py:23
  29.4 10.4 %collective-permute-start.2 = (bf16[64,1024]{1,0:T(8,128)(2,1)S(1)}, bf16[64,1024]{1,0:T(8,128)(2,1)S(1)}, u32[]{:S(2)}, u32[]{:S(2)}) collective-permute-start(bf16[64,1024]{1,0:T(8,128)(2,1)S(1)} %broadcast_select_fusion.4), channel_id=1, source_target_pairs={{0,128},{16,400},{32,160},{48,432},{64,192},{80,464},{96,224},{112... | collective-permute-start | bytes 393224 | tf_op jit(solution)/shard_map/ppermute | solution.py:23
  40.9 22.4 %collective-permute-start.3 = (bf16[4,512,128]{1,2,0:T(8,128)(2,1)}, bf16[4,512,128]{1,2,0:T(8,128)(2,1)}, u32[]{:S(2)}, u32[]{:S(2)}) collective-permute-start(bf16[4,512,128]{1,2,0:T(8,128)(2,1)} %get-tuple-element.39), channel_id=1, source_target_pairs={{0,1},{1,0},{2,3},{3,2},{4,5},{5,4},{6,7},{7,6},{8,9},{9,8},{10,11... | collective-permute-start | bytes 1572872 | tf_op jit(solution)/shard_map/ppermute | solution.py:36
  46.3 27.6 %all-to-all-start.1 = ((bf16[4,4,64,1024]{3,2,1,0:T(8,128)(2,1)}), bf16[4,4,64,1024]{3,2,1,0:T(8,128)(2,1)S(1)}, u32[]{:S(2)}, u32[]{:S(2)}) async-start(bf16[4,4,64,1024]{3,2,1,0:T(8,128)(2,1)} %broadcast_in_dim.36), calls=%async_computation.1 | async-start | bytes 4194304 | tf_op jit(solution)/shard_map/all_to_all | solution.py:42
  51.0 19.7 %collective-permute-start.4 = (bf16[4,512,128]{1,2,0:T(8,128)(2,1)}, bf16[4,512,128]{1,2,0:T(8,128)(2,1)}, u32[]{:S(2)}, u32[]{:S(2)}) collective-permute-start(bf16[4,512,128]{1,2,0:T(8,128)(2,1)} %get-tuple-element.38), channel_id=1, source_target_pairs={{0,7},{1,2},{2,1},{3,4},{4,3},{5,6},{6,5},{7,0},{8,15},{9,10},{10,... | collective-permute-start | bytes 1572872 | tf_op jit(solution)/shard_map/ppermute | solution.py:36
  73.8 6.1 %copy-start = (bf16[4,4,64,1024]{3,2,1,0:T(8,128)(2,1)}, bf16[4,4,64,1024]{3,2,1,0:T(8,128)(2,1)S(1)}, u32[]{:S(2)}) copy-start(bf16[4,4,64,1024]{3,2,1,0:T(8,128)(2,1)S(1)} %all-to-all-done.1) | copy-start | bytes 6291460
  73.8 6.1 %collective-permute-start.5 = (bf16[4,4,64,1024]{3,2,1,0:T(8,128)(2,1)S(1)}, bf16[4,4,64,1024]{3,2,1,0:T(8,128)(2,1)S(1)}, u32[]{:S(2)}, u32[]{:S(2)}) collective-permute-start(bf16[4,4,64,1024]{3,2,1,0:T(8,128)(2,1)S(1)} %all-to-all-done.1), channel_id=1, source_target_pairs={{0,16},{16,0},{32,48},{48,32},{64,80},{80,64},{96,112},{112,96},{1... | collective-permute-start | bytes 6291464 | tf_op jit(solution)/shard_map/ppermute | solution.py:27
  76.2 3.7 %collective-permute-start.6 = (f32[1024]{0:T(1024)S(1)}, f32[1024]{0:T(1024)S(1)}, u32[]{:S(2)}, u32[]{:S(2)}) collective-permute-start(f32[1024]{0:T(1024)S(1)} %multiply_reduce_fusion), channel_id=1, source_target_pairs={{0,16},{16,0},{32,48},{48,32},{64,80},{80,64},{96,112},{112,96},{1... | collective-permute-start | bytes 12296 | tf_op jit(solution)/shard_map/ppermute | solution.py:27
  78.6 1.3 copy-start.4
  80.0 1.4 copy-start.1
  158.7 14.6 %all-to-all-start.7 = ((f32[32,1,1024]{2,1,0:T(1,128)}), f32[32,1,1024]{2,1,0:T(1,128)S(1)}, u32[]{:S(2)}, u32[]{:S(2)}) async-start(f32[32,1,1024]{2,1,0:T(1,128)} %broadcast_in_dim.42), calls=%async_computation.7 | async-start | bytes 262144 | tf_op jit(solution)/shard_map/all_to_all | solution.py:42
  174.6 12.2 %all-to-all-start.8 = ((f32[16,1,512]{2,1,0:T(1,128)}), f32[16,1,512]{2,1,0:T(1,128)S(1)}, u32[]{:S(2)}, u32[]{:S(2)}) async-start(f32[16,1,512]{2,1,0:T(1,128)} %broadcast_in_dim.43), calls=%async_computation.8 | async-start | bytes 65536 | tf_op jit(solution)/shard_map/all_to_all | solution.py:42
  188.7 14.5 %all-to-all-start.9 = ((f32[32,1,1024]{2,1,0:T(1,128)}), f32[32,1,1024]{2,1,0:T(1,128)S(1)}, u32[]{:S(2)}, u32[]{:S(2)}) async-start(f32[32,1,1024]{2,1,0:T(1,128)} %broadcast_in_dim.44), calls=%async_computation.9 | async-start | bytes 262144 | tf_op jit(solution)/shard_map/all_to_all | solution.py:42
  194.3 1.9 copy-start.3
  203.3 1.2 copy-start.6
  204.4 3.7 %copy-start.5 = (bf16[1,4,2,64,1024]{4,3,2,1,0:T(8,128)(2,1)S(1)}, bf16[1,4,2,64,1024]{4,3,2,1,0:T(8,128)(2,1)}, u32[]{:S(2)}) copy-start(bf16[1,4,2,64,1024]{4,3,2,1,0:T(8,128)(2,1)} %copy.50) | copy-start | bytes 3145732
  205.3 6.1 %copy-start.2 = (bf16[2,4,1,64,1024]{4,3,1,0,2:T(8,128)(2,1)S(1)}, bf16[2,4,1,64,1024]{4,3,1,0,2:T(8,128)(2,1)}, u32[]{:S(2)}) copy-start(bf16[2,4,1,64,1024]{4,3,1,0,2:T(8,128)(2,1)} %get-tuple-element.25) | copy-start | bytes 3145732
  205.3 16.2 %collective-permute-start.7 = (bf16[512,512]{1,0:T(8,128)(2,1)S(1)}, bf16[512,512]{1,0:T(8,128)(2,1)S(1)}, u32[]{:S(2)}, u32[]{:S(2)}) collective-permute-start(bf16[512,512]{1,0:T(8,128)(2,1)S(1)} %convolution_convert_fusion.1), channel_id=1, source_target_pairs={{0,1},{1,0},{2,3},{3,2},{4,5},{5,4},{6,7},{7,6},{8,9},{9,8},{10,11... | collective-permute-start | bytes 1572872 | tf_op jit(solution)/shard_map/ppermute | solution.py:36
  208.8 17.0 %collective-permute-start.8 = (bf16[512,512]{1,0:T(8,128)(2,1)S(1)}, bf16[512,512]{1,0:T(8,128)(2,1)S(1)}, u32[]{:S(2)}, u32[]{:S(2)}) collective-permute-start(bf16[512,512]{1,0:T(8,128)(2,1)S(1)} %convolution_convert_fusion), channel_id=1, source_target_pairs={{0,7},{1,2},{2,1},{3,4},{4,3},{5,6},{6,5},{7,0},{8,15},{9,10},{10,... | collective-permute-start | bytes 1572872 | tf_op jit(solution)/shard_map/ppermute | solution.py:36

commit v8 on v6

--- a/solution.py
+++ b/solution.py
@@ -72,7 +72,8 @@
     same, plane = gather(noise, data)
     here = share(plane, "row", LINES)
     n = len(PARITIES[0]) // 2
-    other = jnp.concatenate([neighbour(same[:n], 1), neighbour(same[n:], -1)])
+    halves = [neighbour(same[:n], 1), neighbour(same[n:], -1)]
+    other = jnp.concatenate(halves)
     by_parity = [jnp.where(odd == 0, same, other), jnp.where(odd == 0, other, same)]
     noise_sq = sum(jnp.sum(part.astype(jnp.float32) ** 2, axis=(0, 2)) for part in by_parity)
 
@@ -85,12 +86,10 @@
     first, second = half(0), half(1)
     mine = jnp.where(core == 0, first, second)
     others = jnp.where(core == 0, second, first)
-    here, mine, others, noise_sq, kept, away = lax.optimization_barrier(
-        (here, mine, others, noise_sq, odd, 1 - odd)
-    )
+    here, _, kept, away = lax.optimization_barrier((here, halves, odd, 1 - odd))
     there = other_core(here)
-    sq = jnp.sum(here.astype(jnp.float32) ** 2, axis=(0, 1, 2))
-    data_sq = sq + other_core(sq)
+    squares = [jnp.sum(part.astype(jnp.float32) ** 2, axis=(0, 1, 2)) for part in (here, there)]
+    data_sq = sum(lax.optimization_barrier(squares))
     cross = jnp.dot(mine, here.reshape(-1, cols), preferred_element_type=jnp.float32)
     cross += jnp.dot(others, there.reshape(-1, cols), preferred_element_type=jnp.float32)
 
@@ -109,6 +108,9 @@
         by_row = (lift / rows_all) / jnp.sum(share(part, "col"), axis=0)
         part = jnp.sum(plan * by_row[:, None], axis=0)
         by_col = (lift / cols_all) / jnp.sum(share(part, "row"), axis=0)
+    row_potential = noise_sq / width + EPS * (row_first + jnp.log(by_row))
+    col_potential = data_sq / width + EPS * (col_first + jnp.log(by_col))
+
     weights = (plan * ((rows_all / lift) * by_row)[:, None] * by_col[None, :]).astype(
         jnp.bfloat16
     )
@@ -126,9 +128,6 @@
 
     sent = [terms(part).astype(jnp.bfloat16) for part in features(away)]
     got = [neighbour(part, by) for part, by in zip(sent, (1, -1))]
-    sent, kept, by_row, by_col = lax.optimization_barrier((sent[0], kept, by_row, by_col))
-    row_potential = noise_sq / width + EPS * (row_first + jnp.log(by_row))
-    col_potential = data_sq / width + EPS * (col_first + jnp.log(by_col))
     sums = [
         (terms(own) + add).astype(jnp.bfloat16) for own, add in zip(features(kept), got)
     ]

time: 262 us -> 261 us (level)
  waiting for transfers between devices: 82.6 us -> 63.4 us
  blocking collectives: 80 us -> 96.9 us
  other arithmetic: 14.7 us -> 19.6 us
    all_to_all x0 -> x1, blocking collectives: none -> 31.3 us  [local(): parts = lax.all_to_all(sums, 'col', 0, 0, axis_index_groups=PARITIES)]
    all_to_all x1 -> x0, waiting for transfers between devices: 26.1 us -> none  [local(): parts = lax.all_to_all(sums, 'col', 0, 0, axis_index_groups=PARITIES)]
    all_to_all x6 -> x5, blocking collectives: 80 us -> 65.7 us  [share(): return lax.all_to_all(copies, axis, 0, 0, axis_index_groups=groups)]
    all_to_all x4 -> x5, starting transfers between devices: 22.9 us -> 28.5 us  [share(): return lax.all_to_all(copies, axis, 0, 0, axis_index_groups=groups)]
    ppermute x4, waiting for transfers between devices: 22 us -> 25.7 us  [neighbour(): return lax.ppermute(array, 'col', pairs)]
    dot_general x4, matrix products: 6.65 us -> 3 us  [terms(): lax.dot_general(part, weights, contract, preferred_element_type=jnp.float32)]
    all_to_all x1 -> x0, starting transfers between devices: 3.56 us -> none  [local(): parts = lax.all_to_all(sums, 'col', 0, 0, axis_index_groups=PARITIES)]
    all_to_all x4 -> x5, waiting for transfers between devices: 18 us -> 20.6 us  [share(): return lax.all_to_all(copies, axis, 0, 0, axis_index_groups=groups)]
  transfers between devices with their start and end apart: 14 -> 13, of which waited for: 10 -> 11; matrix products, arithmetic and copies ran while one was open for 7% -> 7% of each run, Pallas kernels for 0% -> 0%
where the time goes in v8:
time: 261 us; the launch traced here: 258 us
  blocking collectives  96.9 us (37%)
  waiting for transfers between devices  63.4 us (24%)
  starting transfers between devices  56.9 us (22%)
  other arithmetic  19.6 us (8%)
  local copies, waits for them, and re-layouts  12.1 us (5%)
  matrix products  7.39 us (3%)
    all_to_all x5, blocking collectives, share(): return lax.all_to_all(copies, axis, 0, 0, axis_index_groups=groups)  65.7 us
    all_to_all x1, blocking collectives, local(): parts = lax.all_to_all(sums, 'col', 0, 0, axis_index_groups=PARITIES)  31.3 us
    all_to_all x5, starting transfers between devices, share(): return lax.all_to_all(copies, axis, 0, 0, axis_index_groups=groups)  28.5 us
    ppermute x4, waiting for transfers between devices, neighbour(): return lax.ppermute(array, 'col', pairs)  25.7 us
    all_to_all x5, waiting for transfers between devices, share(): return lax.all_to_all(copies, axis, 0, 0, axis_index_groups=groups)  20.6 us
    ppermute x3, starting transfers between devices, along_z(): return lax.ppermute(array, 'row', pairs)  16.8 us
    ppermute x3, waiting for transfers between devices, along_z(): return lax.ppermute(array, 'row', pairs)  16.5 us
    ppermute x4, starting transfers between devices, neighbour(): return lax.ppermute(array, 'col', pairs)  9.76 us
  transfers between devices with their start and end apart: 13, of which 11 were waited for; matrix products, arithmetic and copies ran while one was open for 7% of the time, Pallas kernels for 0%

profile of v8, /device:TPU:6, one launch (start us, length us, event | category | flops | bytes accessed | tf_op | source)
XLA Modules:
  0.0 257.5 jit_solution(2007133959503102423)
XLA Ops:
  2.8 8.9 %all-to-all-start = ((bf16[8,512,128]{1,2,0:T(8,128)(2,1)}), bf16[8,512,128]{1,2,0:T(8,128)(2,1)S(1)}, u32[]{:S(2)}, u32[]{:S(2)}) async-start(bf16[8,512,128]{1,2,0:T(8,128)(2,1)} %broadcast_in_dim.30), calls=%async_computation | async-start | bytes 2097152 | tf_op jit(solution)/shard_map/all_to_all | solution.py:42
  11.7 10.0 %collective-permute-start = (bf16[64,1024]{1,0:T(8,128)(2,1)S(1)}, bf16[64,1024]{1,0:T(8,128)(2,1)S(1)}, u32[]{:S(2)}, u32[]{:S(2)}) collective-permute-start(bf16[64,1024]{1,0:T(8,128)(2,1)S(1)} %copy-done.5), channel_id=1, source_target_pairs={{0,384},{16,400},{32,416},{48,432},{64,448},{80,464},{96,480},{112... | collective-permute-start | bytes 393224 | tf_op jit(solution)/shard_map/ppermute | solution.py:23
  21.7 1.9 collective-permute-start.2
  23.7 4.8 %collective-permute-start.1 = (bf16[64,1024]{1,0:T(8,128)(2,1)S(1)}, bf16[64,1024]{1,0:T(8,128)(2,1)S(1)}, u32[]{:S(2)}, u32[]{:S(2)}) collective-permute-start(bf16[64,1024]{1,0:T(8,128)(2,1)S(1)} %copy-done.5), channel_id=1, source_target_pairs={{0,256},{16,272},{32,288},{48,304},{64,320},{80,336},{96,352},{112... | collective-permute-start | bytes 393224 | tf_op jit(solution)/shard_map/ppermute | solution.py:23
  28.7 16.0 %collective-permute-done.1 = bf16[64,1024]{1,0:T(8,128)(2,1)S(1)} collective-permute-done((bf16[64,1024]{1,0:T(8,128)(2,1)S(1)}, bf16[64,1024]{1,0:T(8,128)(2,1)S(1)}, u32[]{:S(2)}, u32[]{:S(2)}) %collective-permute-start.1) | collective-permute-done | bytes 131104 | tf_op jit(solution)/shard_map/ppermute | solution.py:23
  45.2 1.6 broadcast_in_dim.36
  46.9 4.8 %all-to-all-start.1 = ((bf16[4,4,64,1024]{3,2,1,0:T(8,128)(2,1)}), bf16[4,4,64,1024]{3,2,1,0:T(8,128)(2,1)S(1)}, u32[]{:S(2)}, u32[]{:S(2)}) async-start(bf16[4,4,64,1024]{3,2,1,0:T(8,128)(2,1)} %broadcast_in_dim.36), calls=%async_computation.1 | async-start | bytes 4194304 | tf_op jit(solution)/shard_map/all_to_all | solution.py:42
  52.7 2.5 collective-permute-start.4
  55.3 1.9 collective-permute-start.3
  57.2 11.7 %collective-permute-done.4 = bf16[4,512,128]{1,2,0:T(8,128)(2,1)} collective-permute-done((bf16[4,512,128]{1,2,0:T(8,128)(2,1)}, bf16[4,512,128]{1,2,0:T(8,128)(2,1)}, u32[]{:S(2)}, u32[]{:S(2)}) %collective-permute-start.4) | collective-permute-done | bytes 524320 | tf_op jit(solution)/shard_map/ppermute | solution.py:36
  70.4 5.1 %all-to-all-done.1 = bf16[4,4,64,1024]{3,2,1,0:T(8,128)(2,1)S(1)} async-done(((bf16[4,4,64,1024]{3,2,1,0:T(8,128)(2,1)}), bf16[4,4,64,1024]{3,2,1,0:T(8,128)(2,1)S(1)}, u32[]{:S(2)}, u32[]{:S(2)}) %all-to-all-start.1) | async-done | bytes 2097184 | tf_op jit(solution)/shard_map/all_to_all | solution.py:42
  75.5 1.9 collective-permute-start.5
  81.7 2.1 multiply_reduce_fusion
  83.8 3.0 %fusion.15 = f32[512,1024]{1,0:T(8,128)S(1)} fusion(bf16[512,1024]{0,1:T(8,128)(2,1)S(1)} %bitcast.88, bf16[1024,1024]{1,0:T(8,128)(2,1)} %bitcast.18), kind=kOutput, calls=%fused_computation.76 | convolution fusion | flops 1073741824 | bytes 5242880 | tf_op jit(solution)/shard_map/dot_general | solution.py:94
  88.7 13.4 %all_to_all.69 = f32[16,1,512]{2,1,0:T(1,128)S(1)} all-to-all(f32[16,1,512]{2,1,0:T(1,128)S(1)} %broadcast_in_dim.37), channel_id=1, replica_groups=mesh['row'=32,'col'=16] {'col'}, dimensions={0} | all-to-all | bytes 65536 | tf_op jit(solution)/shard_map/all_to_all | solution.py:42
  103.0 16.2 %all_to_all.70 = f32[32,1,1024]{2,1,0:T(1,128)S(1)} all-to-all(f32[32,1,1024]{2,1,0:T(1,128)S(1)} %broadcast_in_dim.38), channel_id=1, replica_groups=mesh['row'=32,'col'=16] {'row'}, dimensions={0} | all-to-all | bytes 262144 | tf_op jit(solution)/shard_map/all_to_all | solution.py:42
  119.9 11.1 %all_to_all.71 = f32[16,1,512]{2,1,0:T(1,128)S(1)} all-to-all(f32[16,1,512]{2,1,0:T(1,128)S(1)} %broadcast_in_dim.39), channel_id=1, replica_groups=mesh['row'=32,'col'=16] {'col'}, dimensions={0} | all-to-all | bytes 65536 | tf_op jit(solution)/shard_map/all_to_all | solution.py:42
  131.6 13.9 %all_to_all.72 = f32[32,1,1024]{2,1,0:T(1,128)S(1)} all-to-all(f32[32,1,1024]{2,1,0:T(1,128)S(1)} %broadcast_in_dim.40), channel_id=1, replica_groups=mesh['row'=32,'col'=16] {'row'}, dimensions={0} | all-to-all | bytes 262144 | tf_op jit(solution)/shard_map/all_to_all | solution.py:42
  146.3 11.1 %all_to_all.73 = f32[16,1,512]{2,1,0:T(1,128)S(1)} all-to-all(f32[16,1,512]{2,1,0:T(1,128)S(1)} %broadcast_in_dim.41), channel_id=1, replica_groups=mesh['row'=32,'col'=16] {'col'}, dimensions={0} | all-to-all | bytes 65536 | tf_op jit(solution)/shard_map/all_to_all | solution.py:42
  158.7 5.7 %all-to-all-start.7 = ((f32[32,1,1024]{2,1,0:T(1,128)}), f32[32,1,1024]{2,1,0:T(1,128)S(1)}, u32[]{:S(2)}, u32[]{:S(2)}) async-start(f32[32,1,1024]{2,1,0:T(1,128)} %broadcast_in_dim.42), calls=%async_computation.7 | async-start | bytes 262144 | tf_op jit(solution)/shard_map/all_to_all | solution.py:42
  164.4 8.9 %all-to-all-done.7 = f32[32,1,1024]{2,1,0:T(1,128)S(1)} async-done(((f32[32,1,1024]{2,1,0:T(1,128)}), f32[32,1,1024]{2,1,0:T(1,128)S(1)}, u32[]{:S(2)}, u32[]{:S(2)}) %all-to-all-start.7) | async-done | bytes 131104 | tf_op jit(solution)/shard_map/all_to_all | solution.py:42
  174.6 3.5 %all-to-all-start.8 = ((f32[16,1,512]{2,1,0:T(1,128)}), f32[16,1,512]{2,1,0:T(1,128)S(1)}, u32[]{:S(2)}, u32[]{:S(2)}) async-start(f32[16,1,512]{2,1,0:T(1,128)} %broadcast_in_dim.43), calls=%async_computation.8 | async-start | bytes 65536 | tf_op jit(solution)/shard_map/all_to_all | solution.py:42
  178.1 4.0 %fusion.3 = (bf16[2,4,1,64,1024]{4,3,1,0,2:T(8,128)(2,1)}, bf16[2,4,1,64,1024]{4,3,1,0,2:T(8,128)(2,1)}, bf16[2,4,1,64,1024]{4,3,1,0,2:T(8,128)(2,1)}) fusion(pred[]{:T(512)S(6)} %eq.19, bf16[2,2,4,64,1024]{4,3,2,1,0:T(8,128)(2,1)} %bitcast.5, s32[]{:T(128)S(6)} %select_n.175, bf16[2,2,4,64,1024]{4,3,2,1,0:T(8,128)(2,1)} %bitcast.85, s32[]{:T(128)S(6)} %select_n.160), kind=kLoop, calls=%fused_computation.33 | loop fusion | flops 1572864 | bytes 7340041 | tf_op jit(solution)/shard_map/jit(_where)/select_n | solution.py:122
  182.1 4.5 %all-to-all-done.8 = f32[16,1,512]{2,1,0:T(1,128)S(1)} async-done(((f32[16,1,512]{2,1,0:T(1,128)}), f32[16,1,512]{2,1,0:T(1,128)S(1)}, u32[]{:S(2)}, u32[]{:S(2)}) %all-to-all-start.8) | async-done | bytes 32800 | tf_op jit(solution)/shard_map/all_to_all | solution.py:42
  188.5 5.6 %all-to-all-start.9 = ((f32[32,1,1024]{2,1,0:T(1,128)}), f32[32,1,1024]{2,1,0:T(1,128)S(1)}, u32[]{:S(2)}, u32[]{:S(2)}) async-start(f32[32,1,1024]{2,1,0:T(1,128)} %broadcast_in_dim.44), calls=%async_computation.9 | async-start | bytes 262144 | tf_op jit(solution)/shard_map/all_to_all | solution.py:42
  194.1 1.7 fusion
  195.7 2.8 %fusion.1 = (bf16[1,4,2,64,1024]{4,3,1,0,2:T(8,128)(2,1)S(1)}, bf16[1,4,2,64,1024]{4,3,1,0,2:T(8,128)(2,1)S(1)}, bf16[1,4,2,64,1024]{4,3,1,0,2:T(8,128)(2,1)}, bf16[1,4,2,64,1024]{4,3,1,0,2:T(8,128)(2,1)S(1)}) fusion(bf16[2,4,1,64,1024]{4,3,1,0,2:T(8,128)(2,1)} %get-tuple-element.21, bf16[2,4,1,64,1024]{4,3,1,0,2:T(8,128)(2,1)S(1)} %fusion, ...), kind=kLoop, calls=%fused_computation.25 | loop fusion | flops 2097152 | bytes 8388608 | tf_op jit(solution)/shard_map/stack | solution.py:123
  200.8 2.2 all-to-all-done.9
  205.1 2.9 %collective-permute-start.7 = (bf16[512,512]{1,0:T(8,128)(2,1)S(1)}, bf16[512,512]{1,0:T(8,128)(2,1)S(1)}, u32[]{:S(2)}, u32[]{:S(2)}) collective-permute-start(bf16[512,512]{1,0:T(8,128)(2,1)S(1)} %convolution_convert_fusion), channel_id=1, source_target_pairs={{0,7},{1,2},{2,1},{3,4},{4,3},{5,6},{6,5},{7,0},{8,15},{9,10},{10,... | collective-permute-start | bytes 1572872 | tf_op jit(solution)/shard_map/ppermute | solution.py:36
  208.8 2.4 collective-permute-start.6
  211.4 11.1 %collective-permute-done.7 = bf16[512,512]{1,0:T(8,128)(2,1)S(1)} collective-permute-done((bf16[512,512]{1,0:T(8,128)(2,1)S(1)}, bf16[512,512]{1,0:T(8,128)(2,1)S(1)}, u32[]{:S(2)}, u32[]{:S(2)}) %collective-permute-start.7) | collective-permute-done | bytes 524320 | tf_op jit(solution)/shard_map/ppermute | solution.py:36
  225.5 31.3 %all_to_all.74 = bf16[8,128,512]{2,1,0:T(8,128)(2,1)S(1)} all-to-all(bf16[8,128,512]{2,1,0:T(8,128)(2,1)S(1)} %bitcast.89), channel_id=1, replica_groups={{0,4,8,12,2,6,10,14},{1,5,9,13,3,7,11,15},{16,20,24,28,18,22,26,30},{17..., dimensions={0} | all-to-all | bytes 2097152 | tf_op jit(solution)/shard_map/all_to_all | solution.py:135
  (82 shorter events, 27.9 us)
Async XLA Ops:
  0.6 11.1 %copy-start.5 = (bf16[64,1024]{1,0:T(8,128)(2,1)S(1)}, bf16[64,1024]{1,0:T(8,128)(2,1)}, u32[]{:S(2)}) copy-start(bf16[64,1024]{1,0:T(8,128)(2,1)} %param.3) | copy-start | bytes 393220
  2.8 42.5 %all-to-all-start = ((bf16[8,512,128]{1,2,0:T(8,128)(2,1)}), bf16[8,512,128]{1,2,0:T(8,128)(2,1)S(1)}, u32[]{:S(2)}, u32[]{:S(2)}) async-start(bf16[8,512,128]{1,2,0:T(8,128)(2,1)} %broadcast_in_dim.30), calls=%async_computation | async-start | bytes 2097152 | tf_op jit(solution)/shard_map/all_to_all | solution.py:42
  11.7 17.0 %collective-permute-start = (bf16[64,1024]{1,0:T(8,128)(2,1)S(1)}, bf16[64,1024]{1,0:T(8,128)(2,1)S(1)}, u32[]{:S(2)}, u32[]{:S(2)}) collective-permute-start(bf16[64,1024]{1,0:T(8,128)(2,1)S(1)} %copy-done.5), channel_id=1, source_target_pairs={{0,384},{16,400},{32,416},{48,432},{64,448},{80,464},{96,480},{112... | collective-permute-start | bytes 393224 | tf_op jit(solution)/shard_map/ppermute | solution.py:23
  21.7 23.5 %collective-permute-start.2 = (bf16[64,1024]{1,0:T(8,128)(2,1)S(1)}, bf16[64,1024]{1,0:T(8,128)(2,1)S(1)}, u32[]{:S(2)}, u32[]{:S(2)}) collective-permute-start(bf16[64,1024]{1,0:T(8,128)(2,1)S(1)} %copy-done.5), channel_id=1, source_target_pairs={{0,128},{16,144},{32,160},{48,176},{64,192},{80,208},{96,224},{112... | collective-permute-start | bytes 393224 | tf_op jit(solution)/shard_map/ppermute | solution.py:23
  23.7 21.0 %collective-permute-start.1 = (bf16[64,1024]{1,0:T(8,128)(2,1)S(1)}, bf16[64,1024]{1,0:T(8,128)(2,1)S(1)}, u32[]{:S(2)}, u32[]{:S(2)}) collective-permute-start(bf16[64,1024]{1,0:T(8,128)(2,1)S(1)} %copy-done.5), channel_id=1, source_target_pairs={{0,256},{16,272},{32,288},{48,304},{64,320},{80,336},{96,352},{112... | collective-permute-start | bytes 393224 | tf_op jit(solution)/shard_map/ppermute | solution.py:23
  46.9 28.7 %all-to-all-start.1 = ((bf16[4,4,64,1024]{3,2,1,0:T(8,128)(2,1)}), bf16[4,4,64,1024]{3,2,1,0:T(8,128)(2,1)S(1)}, u32[]{:S(2)}, u32[]{:S(2)}) async-start(bf16[4,4,64,1024]{3,2,1,0:T(8,128)(2,1)} %broadcast_in_dim.36), calls=%async_computation.1 | async-start | bytes 4194304 | tf_op jit(solution)/shard_map/all_to_all | solution.py:42
  52.7 16.1 %collective-permute-start.4 = (bf16[4,512,128]{1,2,0:T(8,128)(2,1)}, bf16[4,512,128]{1,2,0:T(8,128)(2,1)}, u32[]{:S(2)}, u32[]{:S(2)}) collective-permute-start(bf16[4,512,128]{1,2,0:T(8,128)(2,1)} %get-tuple-element.36), channel_id=1, source_target_pairs={{0,7},{1,2},{2,1},{3,4},{4,3},{5,6},{6,5},{7,0},{8,15},{9,10},{10,... | collective-permute-start | bytes 1572872 | tf_op jit(solution)/shard_map/ppermute | solution.py:36
  55.3 15.2 %collective-permute-start.3 = (bf16[4,512,128]{1,2,0:T(8,128)(2,1)}, bf16[4,512,128]{1,2,0:T(8,128)(2,1)}, u32[]{:S(2)}, u32[]{:S(2)}) collective-permute-start(bf16[4,512,128]{1,2,0:T(8,128)(2,1)} %get-tuple-element.37), channel_id=1, source_target_pairs={{0,1},{1,0},{2,3},{3,2},{4,5},{5,4},{6,7},{7,6},{8,9},{9,8},{10,11... | collective-permute-start | bytes 1572872 | tf_op jit(solution)/shard_map/ppermute | solution.py:36
  75.5 5.2 %copy-start = (bf16[4,4,64,1024]{3,2,1,0:T(8,128)(2,1)}, bf16[4,4,64,1024]{3,2,1,0:T(8,128)(2,1)S(1)}, u32[]{:S(2)}) copy-start(bf16[4,4,64,1024]{3,2,1,0:T(8,128)(2,1)S(1)} %all-to-all-done.1) | copy-start | bytes 6291460
  75.5 6.2 %collective-permute-start.5 = (bf16[4,4,64,1024]{3,2,1,0:T(8,128)(2,1)S(1)}, bf16[4,4,64,1024]{3,2,1,0:T(8,128)(2,1)}, u32[]{:S(2)}, u32[]{:S(2)}) collective-permute-start(bf16[4,4,64,1024]{3,2,1,0:T(8,128)(2,1)S(1)} %all-to-all-done.1), channel_id=1, source_target_pairs={{0,16},{16,0},{32,48},{48,32},{64,80},{80,64},{96,112},{112,96},{1... | collective-permute-start | bytes 6291464 | tf_op jit(solution)/shard_map/ppermute | solution.py:27
  83.8 3.0 %copy-start.1 = (bf16[4,4,64,1024]{3,2,1,0:T(8,128)(2,1)S(1)}, bf16[4,4,64,1024]{3,2,1,0:T(8,128)(2,1)}, u32[]{:S(2)}) copy-start(bf16[4,4,64,1024]{3,2,1,0:T(8,128)(2,1)} %copy-done) | copy-start | bytes 6291460
  158.7 14.6 %all-to-all-start.7 = ((f32[32,1,1024]{2,1,0:T(1,128)}), f32[32,1,1024]{2,1,0:T(1,128)S(1)}, u32[]{:S(2)}, u32[]{:S(2)}) async-start(f32[32,1,1024]{2,1,0:T(1,128)} %broadcast_in_dim.42), calls=%async_computation.7 | async-start | bytes 262144 | tf_op jit(solution)/shard_map/all_to_all | solution.py:42
  174.6 12.0 %all-to-all-start.8 = ((f32[16,1,512]{2,1,0:T(1,128)}), f32[16,1,512]{2,1,0:T(1,128)S(1)}, u32[]{:S(2)}, u32[]{:S(2)}) async-start(f32[16,1,512]{2,1,0:T(1,128)} %broadcast_in_dim.43), calls=%async_computation.8 | async-start | bytes 65536 | tf_op jit(solution)/shard_map/all_to_all | solution.py:42
  188.5 14.5 %all-to-all-start.9 = ((f32[32,1,1024]{2,1,0:T(1,128)}), f32[32,1,1024]{2,1,0:T(1,128)S(1)}, u32[]{:S(2)}, u32[]{:S(2)}) async-start(f32[32,1,1024]{2,1,0:T(1,128)} %broadcast_in_dim.44), calls=%async_computation.9 | async-start | bytes 262144 | tf_op jit(solution)/shard_map/all_to_all | solution.py:42
  203.1 1.2 copy-start.4
  204.2 3.8 %copy-start.3 = (bf16[1,4,2,64,1024]{4,3,2,1,0:T(8,128)(2,1)S(1)}, bf16[1,4,2,64,1024]{4,3,2,1,0:T(8,128)(2,1)}, u32[]{:S(2)}) copy-start(bf16[1,4,2,64,1024]{4,3,2,1,0:T(8,128)(2,1)} %copy.48) | copy-start | bytes 3145732
  205.0 6.2 %copy-start.2 = (bf16[1,4,2,64,1024]{4,3,1,0,2:T(8,128)(2,1)S(1)}, bf16[1,4,2,64,1024]{4,3,1,0,2:T(8,128)(2,1)}, u32[]{:S(2)}) copy-start(bf16[1,4,2,64,1024]{4,3,1,0,2:T(8,128)(2,1)} %get-tuple-element.45) | copy-start | bytes 3145732
  205.1 17.5 %collective-permute-start.7 = (bf16[512,512]{1,0:T(8,128)(2,1)S(1)}, bf16[512,512]{1,0:T(8,128)(2,1)S(1)}, u32[]{:S(2)}, u32[]{:S(2)}) collective-permute-start(bf16[512,512]{1,0:T(8,128)(2,1)S(1)} %convolution_convert_fusion), channel_id=1, source_target_pairs={{0,7},{1,2},{2,1},{3,4},{4,3},{5,6},{6,5},{7,0},{8,15},{9,10},{10,... | collective-permute-start | bytes 1572872 | tf_op jit(solution)/shard_map/ppermute | solution.py:36
  208.8 15.8 %collective-permute-start.6 = (bf16[512,512]{1,0:T(8,128)(2,1)S(1)}, bf16[512,512]{1,0:T(8,128)(2,1)S(1)}, u32[]{:S(2)}, u32[]{:S(2)}) collective-permute-start(bf16[512,512]{1,0:T(8,128)(2,1)S(1)} %convolution_convert_fusion.1), channel_id=1, source_target_pairs={{0,1},{1,0},{2,3},{3,2},{4,5},{5,4},{6,7},{7,6},{8,9},{9,8},{10,11... | collective-permute-start | bytes 1572872 | tf_op jit(solution)/shard_map/ppermute | solution.py:36

commit v9 on v6

--- a/solution.py
+++ b/solution.py
@@ -85,8 +85,8 @@
     first, second = half(0), half(1)
     mine = jnp.where(core == 0, first, second)
     others = jnp.where(core == 0, second, first)
-    here, mine, others, noise_sq, kept, away = lax.optimization_barrier(
-        (here, mine, others, noise_sq, odd, 1 - odd)
+    here, _, kept, away = lax.optimization_barrier(
+        (here, other, odd.astype(jnp.uint32), (1 - odd).astype(jnp.uint32))
     )
     there = other_core(here)
     sq = jnp.sum(here.astype(jnp.float32) ** 2, axis=(0, 1, 2))
@@ -109,6 +109,9 @@
         by_row = (lift / rows_all) / jnp.sum(share(part, "col"), axis=0)
         part = jnp.sum(plan * by_row[:, None], axis=0)
         by_col = (lift / cols_all) / jnp.sum(share(part, "row"), axis=0)
+    row_potential = noise_sq / width + EPS * (row_first + jnp.log(by_row))
+    col_potential = data_sq / width + EPS * (col_first + jnp.log(by_col))
+
     weights = (plan * ((rows_all / lift) * by_row)[:, None] * by_col[None, :]).astype(
         jnp.bfloat16
     )
@@ -126,9 +129,6 @@
 
     sent = [terms(part).astype(jnp.bfloat16) for part in features(away)]
     got = [neighbour(part, by) for part, by in zip(sent, (1, -1))]
-    sent, kept, by_row, by_col = lax.optimization_barrier((sent[0], kept, by_row, by_col))
-    row_potential = noise_sq / width + EPS * (row_first + jnp.log(by_row))
-    col_potential = data_sq / width + EPS * (col_first + jnp.log(by_col))
     sums = [
         (terms(own) + add).astype(jnp.bfloat16) for own, add in zip(features(kept), got)
     ]

time: 262 us -> 258 us (0.985)
  waiting for transfers between devices: 82.6 us -> 48.9 us
  blocking collectives: 80 us -> 111 us
  other arithmetic: 14.7 us -> 18.8 us
  starting transfers between devices: 58.4 us -> 54.9 us
    all_to_all x0 -> x1, blocking collectives: none -> 31.3 us  [local(): parts = lax.all_to_all(sums, 'col', 0, 0, axis_index_groups=PARITIES)]
    all_to_all x1 -> x0, waiting for transfers between devices: 26.1 us -> none  [local(): parts = lax.all_to_all(sums, 'col', 0, 0, axis_index_groups=PARITIES)]
    all_to_all x4, waiting for transfers between devices: 18 us -> 9.33 us  [share(): return lax.all_to_all(copies, axis, 0, 0, axis_index_groups=groups)]
    dot_general x4, matrix products: 6.65 us -> 3.01 us  [terms(): lax.dot_general(part, weights, contract, preferred_element_type=jnp.float32)]
    all_to_all x1 -> x0, starting transfers between devices: 3.56 us -> none  [local(): parts = lax.all_to_all(sums, 'col', 0, 0, axis_index_groups=PARITIES)]
    select_n x3 -> x2, other arithmetic: 3.32 us -> 5.64 us  [features(): both = [jnp.where(core == 0, a, b), jnp.where(core == 0, b, a)]]
  transfers between devices with their start and end apart: 14 -> 13, of which waited for: 10 -> 9; matrix products, arithmetic and copies ran while one was open for 7% -> 8% of each run, Pallas kernels for 0% -> 0%
where the time goes in v9:
time: 258 us; the launch traced here: 255 us
  blocking collectives  111 us (43%)
  starting transfers between devices  54.9 us (21%)
  waiting for transfers between devices  48.9 us (19%)
  other arithmetic  18.8 us (7%)
  local copies, waits for them, and re-layouts  13.1 us (5%)
  matrix products  7.24 us (3%)
    all_to_all x6, blocking collectives, share(): return lax.all_to_all(copies, axis, 0, 0, axis_index_groups=groups)  79.6 us
    all_to_all x1, blocking collectives, local(): parts = lax.all_to_all(sums, 'col', 0, 0, axis_index_groups=PARITIES)  31.3 us
    ppermute x4, waiting for transfers between devices, neighbour(): return lax.ppermute(array, 'col', pairs)  23 us
    all_to_all x4, starting transfers between devices, share(): return lax.all_to_all(copies, axis, 0, 0, axis_index_groups=groups)  22.9 us
    ppermute x3, starting transfers between devices, along_z(): return lax.ppermute(array, 'row', pairs)  16.8 us
    ppermute x3, waiting for transfers between devices, along_z(): return lax.ppermute(array, 'row', pairs)  16.5 us
    ppermute x4, starting transfers between devices, neighbour(): return lax.ppermute(array, 'col', pairs)  10.9 us
    all_to_all x4, waiting for transfers between devices, share(): return lax.all_to_all(copies, axis, 0, 0, axis_index_groups=groups)  9.33 us
  transfers between devices with their start and end apart: 13, of which 9 were waited for; matrix products, arithmetic and copies ran while one was open for 8% of the time, Pallas kernels for 0%

profile of v9, /device:TPU:6, one launch (start us, length us, event | category | flops | bytes accessed | tf_op | source)
XLA Modules:
  0.0 254.9 jit_solution(6686269292723335570)
XLA Ops:
  2.8 8.9 %all-to-all-start = ((bf16[8,512,128]{1,2,0:T(8,128)(2,1)}), bf16[8,512,128]{1,2,0:T(8,128)(2,1)S(1)}, u32[]{:S(2)}, u32[]{:S(2)}) async-start(bf16[8,512,128]{1,2,0:T(8,128)(2,1)} %broadcast_in_dim.30), calls=%async_computation | async-start | bytes 2097152 | tf_op jit(solution)/shard_map/all_to_all | solution.py:42
  11.7 10.0 %collective-permute-start = (bf16[64,1024]{1,0:T(8,128)(2,1)S(1)}, bf16[64,1024]{1,0:T(8,128)(2,1)S(1)}, u32[]{:S(2)}, u32[]{:S(2)}) collective-permute-start(bf16[64,1024]{1,0:T(8,128)(2,1)S(1)} %copy-done.4), channel_id=1, source_target_pairs={{0,384},{16,400},{32,416},{48,432},{64,448},{80,464},{96,480},{112... | collective-permute-start | bytes 393224 | tf_op jit(solution)/shard_map/ppermute | solution.py:23
  21.7 1.9 collective-permute-start.2
  23.7 4.8 %collective-permute-start.1 = (bf16[64,1024]{1,0:T(8,128)(2,1)S(1)}, bf16[64,1024]{1,0:T(8,128)(2,1)S(1)}, u32[]{:S(2)}, u32[]{:S(2)}) collective-permute-start(bf16[64,1024]{1,0:T(8,128)(2,1)S(1)} %copy-done.4), channel_id=1, source_target_pairs={{0,256},{16,272},{32,288},{48,304},{64,320},{80,336},{96,352},{112... | collective-permute-start | bytes 393224 | tf_op jit(solution)/shard_map/ppermute | solution.py:23
  28.7 16.0 %collective-permute-done.1 = bf16[64,1024]{1,0:T(8,128)(2,1)S(1)} collective-permute-done((bf16[64,1024]{1,0:T(8,128)(2,1)S(1)}, bf16[64,1024]{1,0:T(8,128)(2,1)S(1)}, u32[]{:S(2)}, u32[]{:S(2)}) %collective-permute-start.1) | collective-permute-done | bytes 131104 | tf_op jit(solution)/shard_map/ppermute | solution.py:23
  46.9 4.8 %all-to-all-start.1 = ((bf16[4,4,64,1024]{3,2,1,0:T(8,128)(2,1)}), bf16[4,4,64,1024]{3,2,1,0:T(8,128)(2,1)S(1)}, u32[]{:S(2)}, u32[]{:S(2)}) async-start(bf16[4,4,64,1024]{3,2,1,0:T(8,128)(2,1)} %broadcast_in_dim.36), calls=%async_computation.1 | async-start | bytes 4194304 | tf_op jit(solution)/shard_map/all_to_all | solution.py:42
  52.7 1.9 collective-permute-start.3
  54.6 3.7 %collective-permute-start.4 = (bf16[4,512,128]{1,2,0:T(8,128)(2,1)}, bf16[4,512,128]{1,2,0:T(8,128)(2,1)}, u32[]{:S(2)}, u32[]{:S(2)}) collective-permute-start(bf16[4,512,128]{1,2,0:T(8,128)(2,1)} %get-tuple-element.32), channel_id=1, source_target_pairs={{0,7},{1,2},{2,1},{3,4},{4,3},{5,6},{6,5},{7,0},{8,15},{9,10},{10,... | collective-permute-start | bytes 1572872 | tf_op jit(solution)/shard_map/ppermute | solution.py:36
  58.3 9.3 %collective-permute-done.3 = bf16[4,512,128]{1,2,0:T(8,128)(2,1)} collective-permute-done((bf16[4,512,128]{1,2,0:T(8,128)(2,1)}, bf16[4,512,128]{1,2,0:T(8,128)(2,1)}, u32[]{:S(2)}, u32[]{:S(2)}) %collective-permute-start.3) | collective-permute-done | bytes 524320 | tf_op jit(solution)/shard_map/ppermute | solution.py:36
  67.7 1.9 constant_dynamic-update-slice_fusion.1
  70.8 1.9 constant_dynamic-update-slice_fusion
  72.7 2.8 %all-to-all-done.1 = bf16[4,4,64,1024]{3,2,1,0:T(8,128)(2,1)S(1)} async-done(((bf16[4,4,64,1024]{3,2,1,0:T(8,128)(2,1)}), bf16[4,4,64,1024]{3,2,1,0:T(8,128)(2,1)S(1)}, u32[]{:S(2)}, u32[]{:S(2)}) %all-to-all-start.1) | async-done | bytes 2097184 | tf_op jit(solution)/shard_map/all_to_all | solution.py:42
  75.5 1.9 collective-permute-start.5
  77.5 1.9 multiply_reduce_fusion.2
  80.3 2.4 collective-permute-start.6
  84.0 3.0 %subtract_reduce_fusion = (f32[512]{0:T(512)S(1)}, f32[512,1024]{1,0:T(8,128)S(1)}) fusion(f32[1024]{0:T(1024)S(1)} %broadcast_multiply_fusion, f32[512,1024]{1,0:T(8,128)S(1)} %fusion.15, bf16[512,1024]{0,1:T(8,128)(2,1)S(1)} %bitcast.94, bf16[1024,1024]{1,0:T(8,128)(2,1)} %bitcast.18), kind=kOutput, calls=%fused_computation.19 | convolution fusion | flops 1075838464 | bytes 7346176 | tf_op jit(solution)/shard_map/dot_general | solution.py:95
  87.5 13.4 %all_to_all.69 = f32[16,1,512]{2,1,0:T(1,128)S(1)} all-to-all(f32[16,1,512]{2,1,0:T(1,128)S(1)} %broadcast_in_dim.37), channel_id=1, replica_groups=mesh['row'=32,'col'=16] {'col'}, dimensions={0} | all-to-all | bytes 65536 | tf_op jit(solution)/shard_map/all_to_all | solution.py:42
  101.7 16.2 %all_to_all.70 = f32[32,1,1024]{2,1,0:T(1,128)S(1)} all-to-all(f32[32,1,1024]{2,1,0:T(1,128)S(1)} %broadcast_in_dim.38), channel_id=1, replica_groups=mesh['row'=32,'col'=16] {'row'}, dimensions={0} | all-to-all | bytes 262144 | tf_op jit(solution)/shard_map/all_to_all | solution.py:42
  118.6 11.1 %all_to_all.71 = f32[16,1,512]{2,1,0:T(1,128)S(1)} all-to-all(f32[16,1,512]{2,1,0:T(1,128)S(1)} %broadcast_in_dim.39), channel_id=1, replica_groups=mesh['row'=32,'col'=16] {'col'}, dimensions={0} | all-to-all | bytes 65536 | tf_op jit(solution)/shard_map/all_to_all | solution.py:42
  130.4 13.9 %all_to_all.72 = f32[32,1,1024]{2,1,0:T(1,128)S(1)} all-to-all(f32[32,1,1024]{2,1,0:T(1,128)S(1)} %broadcast_in_dim.40), channel_id=1, replica_groups=mesh['row'=32,'col'=16] {'row'}, dimensions={0} | all-to-all | bytes 262144 | tf_op jit(solution)/shard_map/all_to_all | solution.py:42
  145.0 11.1 %all_to_all.73 = f32[16,1,512]{2,1,0:T(1,128)S(1)} all-to-all(f32[16,1,512]{2,1,0:T(1,128)S(1)} %broadcast_in_dim.41), channel_id=1, replica_groups=mesh['row'=32,'col'=16] {'col'}, dimensions={0} | all-to-all | bytes 65536 | tf_op jit(solution)/shard_map/all_to_all | solution.py:42
  156.8 13.9 %all_to_all.74 = f32[32,1,1024]{2,1,0:T(1,128)S(1)} all-to-all(f32[32,1,1024]{2,1,0:T(1,128)S(1)} %broadcast_in_dim.42), channel_id=1, replica_groups=mesh['row'=32,'col'=16] {'row'}, dimensions={0} | all-to-all | bytes 262144 | tf_op jit(solution)/shard_map/all_to_all | solution.py:42
  172.0 3.7 %all-to-all-start.8 = ((f32[16,1,512]{2,1,0:T(1,128)}), f32[16,1,512]{2,1,0:T(1,128)S(1)}, u32[]{:S(2)}, u32[]{:S(2)}) async-start(f32[16,1,512]{2,1,0:T(1,128)} %broadcast_in_dim.43), calls=%async_computation.8 | async-start | bytes 65536 | tf_op jit(solution)/shard_map/all_to_all | solution.py:42
  175.7 4.0 %fusion.3 = (bf16[2,4,1,64,1024]{4,3,1,0,2:T(8,128)(2,1)}, bf16[2,4,1,64,1024]{4,3,1,0,2:T(8,128)(2,1)}, bf16[2,4,1,64,1024]{4,3,1,0,2:T(8,128)(2,1)}) fusion(pred[]{:T(512)S(6)} %eq.19, bf16[2,2,4,64,1024]{4,3,2,1,0:T(8,128)(2,1)} %bitcast.5, u32[]{:T(128)S(6)} %convert_element_type.39, bf16[2,2,4,64,1024]{4,3,2,1,0:T(8,128)(2,1)} %bitcast.86, ...), kind=kLoop, calls=%fused_computation.32 | loop fusion | flops 1572864 | bytes 7340041 | tf_op jit(solution)/shard_map/jit(_where)/select_n | solution.py:123
  179.7 4.3 %all-to-all-done.8 = f32[16,1,512]{2,1,0:T(1,128)S(1)} async-done(((f32[16,1,512]{2,1,0:T(1,128)}), f32[16,1,512]{2,1,0:T(1,128)S(1)}, u32[]{:S(2)}, u32[]{:S(2)}) %all-to-all-start.8) | async-done | bytes 32800 | tf_op jit(solution)/shard_map/all_to_all | solution.py:42
  185.9 5.6 %all-to-all-start.9 = ((f32[32,1,1024]{2,1,0:T(1,128)}), f32[32,1,1024]{2,1,0:T(1,128)S(1)}, u32[]{:S(2)}, u32[]{:S(2)}) async-start(f32[32,1,1024]{2,1,0:T(1,128)} %broadcast_in_dim.44), calls=%async_computation.9 | async-start | bytes 262144 | tf_op jit(solution)/shard_map/all_to_all | solution.py:42
  193.1 2.8 %fusion.1 = (bf16[1,4,2,64,1024]{4,3,1,0,2:T(8,128)(2,1)S(1)}, bf16[1,4,2,64,1024]{4,3,1,0,2:T(8,128)(2,1)S(1)}, bf16[1,4,2,64,1024]{4,3,1,0,2:T(8,128)(2,1)}, bf16[1,4,2,64,1024]{4,3,1,0,2:T(8,128)(2,1)S(1)}) fusion(bf16[2,4,1,64,1024]{4,3,1,0,2:T(8,128)(2,1)} %get-tuple-element.17, bf16[2,4,1,64,1024]{4,3,1,0,2:T(8,128)(2,1)S(1)} %fusion, ...), kind=kLoop, calls=%fused_computation.24 | loop fusion | flops 2097152 | bytes 8388608 | tf_op jit(solution)/shard_map/stack | solution.py:124
  198.2 2.2 all-to-all-done.9
  202.5 2.9 %collective-permute-start.8 = (bf16[512,512]{1,0:T(8,128)(2,1)S(1)}, bf16[512,512]{1,0:T(8,128)(2,1)S(1)}, u32[]{:S(2)}, u32[]{:S(2)}) collective-permute-start(bf16[512,512]{1,0:T(8,128)(2,1)S(1)} %convolution_convert_fusion), channel_id=1, source_target_pairs={{0,7},{1,2},{2,1},{3,4},{4,3},{5,6},{6,5},{7,0},{8,15},{9,10},{10,... | collective-permute-start | bytes 1572872 | tf_op jit(solution)/shard_map/ppermute | solution.py:36
  206.2 2.4 collective-permute-start.7
  208.8 11.1 %collective-permute-done.8 = bf16[512,512]{1,0:T(8,128)(2,1)S(1)} collective-permute-done((bf16[512,512]{1,0:T(8,128)(2,1)S(1)}, bf16[512,512]{1,0:T(8,128)(2,1)S(1)}, u32[]{:S(2)}, u32[]{:S(2)}) %collective-permute-start.8) | collective-permute-done | bytes 524320 | tf_op jit(solution)/shard_map/ppermute | solution.py:36
  222.9 31.3 %all_to_all.75 = bf16[8,128,512]{2,1,0:T(8,128)(2,1)S(1)} all-to-all(bf16[8,128,512]{2,1,0:T(8,128)(2,1)S(1)} %bitcast.89), channel_id=1, replica_groups={{0,4,8,12,2,6,10,14},{1,5,9,13,3,7,11,15},{16,20,24,28,18,22,26,30},{17..., dimensions={0} | all-to-all | bytes 2097152 | tf_op jit(solution)/shard_map/all_to_all | solution.py:136
  (80 shorter events, 26.8 us)
Async XLA Ops:
  0.6 11.1 %copy-start.4 = (bf16[64,1024]{1,0:T(8,128)(2,1)S(1)}, bf16[64,1024]{1,0:T(8,128)(2,1)}, u32[]{:S(2)}) copy-start(bf16[64,1024]{1,0:T(8,128)(2,1)} %param.3) | copy-start | bytes 393220
  2.8 42.5 %all-to-all-start = ((bf16[8,512,128]{1,2,0:T(8,128)(2,1)}), bf16[8,512,128]{1,2,0:T(8,128)(2,1)S(1)}, u32[]{:S(2)}, u32[]{:S(2)}) async-start(bf16[8,512,128]{1,2,0:T(8,128)(2,1)} %broadcast_in_dim.30), calls=%async_computation | async-start | bytes 2097152 | tf_op jit(solution)/shard_map/all_to_all | solution.py:42
  11.7 17.0 %collective-permute-start = (bf16[64,1024]{1,0:T(8,128)(2,1)S(1)}, bf16[64,1024]{1,0:T(8,128)(2,1)S(1)}, u32[]{:S(2)}, u32[]{:S(2)}) collective-permute-start(bf16[64,1024]{1,0:T(8,128)(2,1)S(1)} %copy-done.4), channel_id=1, source_target_pairs={{0,384},{16,400},{32,416},{48,432},{64,448},{80,464},{96,480},{112... | collective-permute-start | bytes 393224 | tf_op jit(solution)/shard_map/ppermute | solution.py:23
  21.7 23.5 %collective-permute-start.2 = (bf16[64,1024]{1,0:T(8,128)(2,1)S(1)}, bf16[64,1024]{1,0:T(8,128)(2,1)S(1)}, u32[]{:S(2)}, u32[]{:S(2)}) collective-permute-start(bf16[64,1024]{1,0:T(8,128)(2,1)S(1)} %copy-done.4), channel_id=1, source_target_pairs={{0,128},{16,144},{32,160},{48,176},{64,192},{80,208},{96,224},{112... | collective-permute-start | bytes 393224 | tf_op jit(solution)/shard_map/ppermute | solution.py:23
  23.7 21.0 %collective-permute-start.1 = (bf16[64,1024]{1,0:T(8,128)(2,1)S(1)}, bf16[64,1024]{1,0:T(8,128)(2,1)S(1)}, u32[]{:S(2)}, u32[]{:S(2)}) collective-permute-start(bf16[64,1024]{1,0:T(8,128)(2,1)S(1)} %copy-done.4), channel_id=1, source_target_pairs={{0,256},{16,272},{32,288},{48,304},{64,320},{80,336},{96,352},{112... | collective-permute-start | bytes 393224 | tf_op jit(solution)/shard_map/ppermute | solution.py:23
  46.9 28.7 %all-to-all-start.1 = ((bf16[4,4,64,1024]{3,2,1,0:T(8,128)(2,1)}), bf16[4,4,64,1024]{3,2,1,0:T(8,128)(2,1)S(1)}, u32[]{:S(2)}, u32[]{:S(2)}) async-start(bf16[4,4,64,1024]{3,2,1,0:T(8,128)(2,1)} %broadcast_in_dim.36), calls=%async_computation.1 | async-start | bytes 4194304 | tf_op jit(solution)/shard_map/all_to_all | solution.py:42
  52.7 14.9 %collective-permute-start.3 = (bf16[4,512,128]{1,2,0:T(8,128)(2,1)}, bf16[4,512,128]{1,2,0:T(8,128)(2,1)}, u32[]{:S(2)}, u32[]{:S(2)}) collective-permute-start(bf16[4,512,128]{1,2,0:T(8,128)(2,1)} %get-tuple-element.33), channel_id=1, source_target_pairs={{0,1},{1,0},{2,3},{3,2},{4,5},{5,4},{6,7},{7,6},{8,9},{9,8},{10,11... | collective-permute-start | bytes 1572872 | tf_op jit(solution)/shard_map/ppermute | solution.py:36
  54.6 16.1 %collective-permute-start.4 = (bf16[4,512,128]{1,2,0:T(8,128)(2,1)}, bf16[4,512,128]{1,2,0:T(8,128)(2,1)}, u32[]{:S(2)}, u32[]{:S(2)}) collective-permute-start(bf16[4,512,128]{1,2,0:T(8,128)(2,1)} %get-tuple-element.32), channel_id=1, source_target_pairs={{0,7},{1,2},{2,1},{3,4},{4,3},{5,6},{6,5},{7,0},{8,15},{9,10},{10,... | collective-permute-start | bytes 1572872 | tf_op jit(solution)/shard_map/ppermute | solution.py:36
  75.5 7.1 %copy-start = (bf16[4,4,64,1024]{3,2,1,0:T(8,128)(2,1)}, bf16[4,4,64,1024]{3,2,1,0:T(8,128)(2,1)S(1)}, u32[]{:S(2)}) copy-start(bf16[4,4,64,1024]{3,2,1,0:T(8,128)(2,1)S(1)} %all-to-all-done.1) | copy-start | bytes 6291460
  75.5 8.4 %collective-permute-start.5 = (bf16[4,4,64,1024]{3,2,1,0:T(8,128)(2,1)S(1)}, bf16[4,4,64,1024]{3,2,1,0:T(8,128)(2,1)}, u32[]{:S(2)}, u32[]{:S(2)}) collective-permute-start(bf16[4,4,64,1024]{3,2,1,0:T(8,128)(2,1)S(1)} %all-to-all-done.1), channel_id=1, source_target_pairs={{0,16},{16,0},{32,48},{48,32},{64,80},{80,64},{96,112},{112,96},{1... | collective-permute-start | bytes 6291464 | tf_op jit(solution)/shard_map/ppermute | solution.py:27
  80.3 3.7 %collective-permute-start.6 = (f32[1024]{0:T(1024)S(1)}, f32[1024]{0:T(1024)S(1)}, u32[]{:S(2)}, u32[]{:S(2)}) collective-permute-start(f32[1024]{0:T(1024)S(1)} %multiply_reduce_fusion), channel_id=1, source_target_pairs={{0,16},{16,0},{32,48},{48,32},{64,80},{80,64},{96,112},{112,96},{1... | collective-permute-start | bytes 12296 | tf_op jit(solution)/shard_map/ppermute | solution.py:27
  172.0 12.0 %all-to-all-start.8 = ((f32[16,1,512]{2,1,0:T(1,128)}), f32[16,1,512]{2,1,0:T(1,128)S(1)}, u32[]{:S(2)}, u32[]{:S(2)}) async-start(f32[16,1,512]{2,1,0:T(1,128)} %broadcast_in_dim.43), calls=%async_computation.8 | async-start | bytes 65536 | tf_op jit(solution)/shard_map/all_to_all | solution.py:42
  185.9 14.5 %all-to-all-start.9 = ((f32[32,1,1024]{2,1,0:T(1,128)}), f32[32,1,1024]{2,1,0:T(1,128)S(1)}, u32[]{:S(2)}, u32[]{:S(2)}) async-start(f32[32,1,1024]{2,1,0:T(1,128)} %broadcast_in_dim.44), calls=%async_computation.9 | async-start | bytes 262144 | tf_op jit(solution)/shard_map/all_to_all | solution.py:42
  200.5 1.2 copy-start.3
  201.6 3.8 %copy-start.2 = (bf16[1,4,2,64,1024]{4,3,2,1,0:T(8,128)(2,1)S(1)}, bf16[1,4,2,64,1024]{4,3,2,1,0:T(8,128)(2,1)}, u32[]{:S(2)}) copy-start(bf16[1,4,2,64,1024]{4,3,2,1,0:T(8,128)(2,1)} %copy.48) | copy-start | bytes 3145732
  202.5 6.1 %copy-start.1 = (bf16[1,4,2,64,1024]{4,3,1,0,2:T(8,128)(2,1)S(1)}, bf16[1,4,2,64,1024]{4,3,1,0,2:T(8,128)(2,1)}, u32[]{:S(2)}) copy-start(bf16[1,4,2,64,1024]{4,3,1,0,2:T(8,128)(2,1)} %get-tuple-element.41) | copy-start | bytes 3145732
  202.5 17.5 %collective-permute-start.8 = (bf16[512,512]{1,0:T(8,128)(2,1)S(1)}, bf16[512,512]{1,0:T(8,128)(2,1)S(1)}, u32[]{:S(2)}, u32[]{:S(2)}) collective-permute-start(bf16[512,512]{1,0:T(8,128)(2,1)S(1)} %convolution_convert_fusion), channel_id=1, source_target_pairs={{0,7},{1,2},{2,1},{3,4},{4,3},{5,6},{6,5},{7,0},{8,15},{9,10},{10,... | collective-permute-start | bytes 1572872 | tf_op jit(solution)/shard_map/ppermute | solution.py:36
  206.2 15.8 %collective-permute-start.7 = (bf16[512,512]{1,0:T(8,128)(2,1)S(1)}, bf16[512,512]{1,0:T(8,128)(2,1)S(1)}, u32[]{:S(2)}, u32[]{:S(2)}) collective-permute-start(bf16[512,512]{1,0:T(8,128)(2,1)S(1)} %convolution_convert_fusion.1), channel_id=1, source_target_pairs={{0,1},{1,0},{2,3},{3,2},{4,5},{5,4},{6,7},{7,6},{8,9},{9,8},{10,11... | collective-permute-start | bytes 1572872 | tf_op jit(solution)/shard_map/ppermute | solution.py:36

commit v10 on v9

--- a/solution.py
+++ b/solution.py
@@ -86,7 +86,7 @@
     mine = jnp.where(core == 0, first, second)
     others = jnp.where(core == 0, second, first)
     here, _, kept, away = lax.optimization_barrier(
-        (here, other, odd.astype(jnp.uint32), (1 - odd).astype(jnp.uint32))
+        (here, noise_sq, odd.astype(jnp.uint32), (1 - odd).astype(jnp.uint32))
     )
     there = other_core(here)
     sq = jnp.sum(here.astype(jnp.float32) ** 2, axis=(0, 1, 2))

time: 258 us -> 258 us (level)
  no operation moved by 1% of the time
where the time goes in v10:
time: 258 us; the launch traced here: 255 us
  blocking collectives  111 us (43%)
  starting transfers between devices  54.9 us (21%)
  waiting for transfers between devices  48.5 us (19%)
  other arithmetic  18.9 us (7%)
  local copies, waits for them, and re-layouts  13 us (5%)
  matrix products  7.24 us (3%)
    all_to_all x6, blocking collectives, share(): return lax.all_to_all(copies, axis, 0, 0, axis_index_groups=groups)  79.6 us
    all_to_all x1, blocking collectives, local(): parts = lax.all_to_all(sums, 'col', 0, 0, axis_index_groups=PARITIES)  31.2 us
    ppermute x4, waiting for transfers between devices, neighbour(): return lax.ppermute(array, 'col', pairs)  23.8 us
    all_to_all x4, starting transfers between devices, share(): return lax.all_to_all(copies, axis, 0, 0, axis_index_groups=groups)  22.9 us
    ppermute x3, starting transfers between devices, along_z(): return lax.ppermute(array, 'row', pairs)  16.8 us
    ppermute x3, waiting for transfers between devices, along_z(): return lax.ppermute(array, 'row', pairs)  16.5 us
    ppermute x4, starting transfers between devices, neighbour(): return lax.ppermute(array, 'col', pairs)  10.9 us
    all_to_all x4, waiting for transfers between devices, share(): return lax.all_to_all(copies, axis, 0, 0, axis_index_groups=groups)  8.16 us
  transfers between devices with their start and end apart: 13, of which 9 were waited for; matrix products, arithmetic and copies ran while one was open for 8% of the time, Pallas kernels for 0%

profile of v10, /device:TPU:6, one launch (start us, length us, event | category | flops | bytes accessed | tf_op | source)
XLA Modules:
  0.0 254.6 jit_solution(11998564029195360484)
XLA Ops:
  2.8 8.9 %all-to-all-start = ((bf16[8,512,128]{1,2,0:T(8,128)(2,1)}), bf16[8,512,128]{1,2,0:T(8,128)(2,1)S(1)}, u32[]{:S(2)}, u32[]{:S(2)}) async-start(bf16[8,512,128]{1,2,0:T(8,128)(2,1)} %broadcast_in_dim.30), calls=%async_computation | async-start | bytes 2097152 | tf_op jit(solution)/shard_map/all_to_all | solution.py:42
  11.7 10.0 %collective-permute-start = (bf16[64,1024]{1,0:T(8,128)(2,1)S(1)}, bf16[64,1024]{1,0:T(8,128)(2,1)S(1)}, u32[]{:S(2)}, u32[]{:S(2)}) collective-permute-start(bf16[64,1024]{1,0:T(8,128)(2,1)S(1)} %copy-done.4), channel_id=1, source_target_pairs={{0,384},{16,400},{32,416},{48,432},{64,448},{80,464},{96,480},{112... | collective-permute-start | bytes 393224 | tf_op jit(solution)/shard_map/ppermute | solution.py:23
  21.7 1.9 collective-permute-start.2
  23.7 4.8 %collective-permute-start.1 = (bf16[64,1024]{1,0:T(8,128)(2,1)S(1)}, bf16[64,1024]{1,0:T(8,128)(2,1)S(1)}, u32[]{:S(2)}, u32[]{:S(2)}) collective-permute-start(bf16[64,1024]{1,0:T(8,128)(2,1)S(1)} %copy-done.4), channel_id=1, source_target_pairs={{0,256},{16,272},{32,288},{48,304},{64,320},{80,336},{96,352},{112... | collective-permute-start | bytes 393224 | tf_op jit(solution)/shard_map/ppermute | solution.py:23
  28.7 16.0 %collective-permute-done.1 = bf16[64,1024]{1,0:T(8,128)(2,1)S(1)} collective-permute-done((bf16[64,1024]{1,0:T(8,128)(2,1)S(1)}, bf16[64,1024]{1,0:T(8,128)(2,1)S(1)}, u32[]{:S(2)}, u32[]{:S(2)}) %collective-permute-start.1) | collective-permute-done | bytes 131104 | tf_op jit(solution)/shard_map/ppermute | solution.py:23
  46.9 4.8 %all-to-all-start.1 = ((bf16[4,4,64,1024]{3,2,1,0:T(8,128)(2,1)}), bf16[4,4,64,1024]{3,2,1,0:T(8,128)(2,1)S(1)}, u32[]{:S(2)}, u32[]{:S(2)}) async-start(bf16[4,4,64,1024]{3,2,1,0:T(8,128)(2,1)} %broadcast_in_dim.36), calls=%async_computation.1 | async-start | bytes 4194304 | tf_op jit(solution)/shard_map/all_to_all | solution.py:42
  52.7 1.9 collective-permute-start.3
  54.7 3.7 %collective-permute-start.4 = (bf16[4,512,128]{1,2,0:T(8,128)(2,1)}, bf16[4,512,128]{1,2,0:T(8,128)(2,1)}, u32[]{:S(2)}, u32[]{:S(2)}) collective-permute-start(bf16[4,512,128]{1,2,0:T(8,128)(2,1)} %get-tuple-element.32), channel_id=1, source_target_pairs={{0,7},{1,2},{2,1},{3,4},{4,3},{5,6},{6,5},{7,0},{8,15},{9,10},{10,... | collective-permute-start | bytes 1572872 | tf_op jit(solution)/shard_map/ppermute | solution.py:36
  58.3 9.3 %collective-permute-done.3 = bf16[4,512,128]{1,2,0:T(8,128)(2,1)} collective-permute-done((bf16[4,512,128]{1,2,0:T(8,128)(2,1)}, bf16[4,512,128]{1,2,0:T(8,128)(2,1)}, u32[]{:S(2)}, u32[]{:S(2)}) %collective-permute-start.3) | collective-permute-done | bytes 524320 | tf_op jit(solution)/shard_map/ppermute | solution.py:36
  68.7 2.1 collective-permute-done.4
  71.9 2.0 multiply_reduce_fusion.7
  73.9 1.7 all-to-all-done.1
  75.5 1.9 collective-permute-start.5
  77.5 1.7 fusion.12
  79.9 2.4 collective-permute-start.6
  83.6 3.0 %subtract_reduce_fusion = (f32[512]{0:T(512)S(1)}, f32[512,1024]{1,0:T(8,128)S(1)}) fusion(f32[1024]{0:T(1024)S(1)} %broadcast_multiply_fusion, f32[512,1024]{1,0:T(8,128)S(1)} %fusion.15, bf16[512,1024]{0,1:T(8,128)(2,1)S(1)} %bitcast.94, bf16[1024,1024]{1,0:T(8,128)(2,1)} %bitcast.18), kind=kOutput, calls=%fused_computation.19 | convolution fusion | flops 1075838464 | bytes 7346176 | tf_op jit(solution)/shard_map/dot_general | solution.py:95
  87.1 13.4 %all_to_all.69 = f32[16,1,512]{2,1,0:T(1,128)S(1)} all-to-all(f32[16,1,512]{2,1,0:T(1,128)S(1)} %broadcast_in_dim.37), channel_id=1, replica_groups=mesh['row'=32,'col'=16] {'col'}, dimensions={0} | all-to-all | bytes 65536 | tf_op jit(solution)/shard_map/all_to_all | solution.py:42
  101.4 16.2 %all_to_all.70 = f32[32,1,1024]{2,1,0:T(1,128)S(1)} all-to-all(f32[32,1,1024]{2,1,0:T(1,128)S(1)} %broadcast_in_dim.38), channel_id=1, replica_groups=mesh['row'=32,'col'=16] {'row'}, dimensions={0} | all-to-all | bytes 262144 | tf_op jit(solution)/shard_map/all_to_all | solution.py:42
  118.3 11.1 %all_to_all.71 = f32[16,1,512]{2,1,0:T(1,128)S(1)} all-to-all(f32[16,1,512]{2,1,0:T(1,128)S(1)} %broadcast_in_dim.39), channel_id=1, replica_groups=mesh['row'=32,'col'=16] {'col'}, dimensions={0} | all-to-all | bytes 65536 | tf_op jit(solution)/shard_map/all_to_all | solution.py:42
  130.0 13.9 %all_to_all.72 = f32[32,1,1024]{2,1,0:T(1,128)S(1)} all-to-all(f32[32,1,1024]{2,1,0:T(1,128)S(1)} %broadcast_in_dim.40), channel_id=1, replica_groups=mesh['row'=32,'col'=16] {'row'}, dimensions={0} | all-to-all | bytes 262144 | tf_op jit(solution)/shard_map/all_to_all | solution.py:42
  144.7 11.1 %all_to_all.73 = f32[16,1,512]{2,1,0:T(1,128)S(1)} all-to-all(f32[16,1,512]{2,1,0:T(1,128)S(1)} %broadcast_in_dim.41), channel_id=1, replica_groups=mesh['row'=32,'col'=16] {'col'}, dimensions={0} | all-to-all | bytes 65536 | tf_op jit(solution)/shard_map/all_to_all | solution.py:42
  156.4 13.9 %all_to_all.74 = f32[32,1,1024]{2,1,0:T(1,128)S(1)} all-to-all(f32[32,1,1024]{2,1,0:T(1,128)S(1)} %broadcast_in_dim.42), channel_id=1, replica_groups=mesh['row'=32,'col'=16] {'row'}, dimensions={0} | all-to-all | bytes 262144 | tf_op jit(solution)/shard_map/all_to_all | solution.py:42
  171.6 3.7 %all-to-all-start.8 = ((f32[16,1,512]{2,1,0:T(1,128)}), f32[16,1,512]{2,1,0:T(1,128)S(1)}, u32[]{:S(2)}, u32[]{:S(2)}) async-start(f32[16,1,512]{2,1,0:T(1,128)} %broadcast_in_dim.43), calls=%async_computation.8 | async-start | bytes 65536 | tf_op jit(solution)/shard_map/all_to_all | solution.py:42
  175.3 4.0 %fusion.3 = (bf16[2,4,1,64,1024]{4,3,1,0,2:T(8,128)(2,1)}, bf16[2,4,1,64,1024]{4,3,1,0,2:T(8,128)(2,1)}, bf16[2,4,1,64,1024]{4,3,1,0,2:T(8,128)(2,1)}) fusion(pred[]{:T(512)S(6)} %eq.19, bf16[2,2,4,64,1024]{4,3,2,1,0:T(8,128)(2,1)} %bitcast.5, u32[]{:T(128)S(6)} %convert_element_type.41, bf16[2,2,4,64,1024]{4,3,2,1,0:T(8,128)(2,1)} %bitcast.86, ...), kind=kLoop, calls=%fused_computation.32 | loop fusion | flops 1572864 | bytes 7340041 | tf_op jit(solution)/shard_map/jit(_where)/select_n | solution.py:123
  179.3 4.3 %all-to-all-done.8 = f32[16,1,512]{2,1,0:T(1,128)S(1)} async-done(((f32[16,1,512]{2,1,0:T(1,128)}), f32[16,1,512]{2,1,0:T(1,128)S(1)}, u32[]{:S(2)}, u32[]{:S(2)}) %all-to-all-start.8) | async-done | bytes 32800 | tf_op jit(solution)/shard_map/all_to_all | solution.py:42
  185.5 5.6 %all-to-all-start.9 = ((f32[32,1,1024]{2,1,0:T(1,128)}), f32[32,1,1024]{2,1,0:T(1,128)S(1)}, u32[]{:S(2)}, u32[]{:S(2)}) async-start(f32[32,1,1024]{2,1,0:T(1,128)} %broadcast_in_dim.44), calls=%async_computation.9 | async-start | bytes 262144 | tf_op jit(solution)/shard_map/all_to_all | solution.py:42
  192.8 2.8 %fusion.1 = (bf16[1,4,2,64,1024]{4,3,1,0,2:T(8,128)(2,1)S(1)}, bf16[1,4,2,64,1024]{4,3,1,0,2:T(8,128)(2,1)S(1)}, bf16[1,4,2,64,1024]{4,3,1,0,2:T(8,128)(2,1)}, bf16[1,4,2,64,1024]{4,3,1,0,2:T(8,128)(2,1)S(1)}) fusion(bf16[2,4,1,64,1024]{4,3,1,0,2:T(8,128)(2,1)} %get-tuple-element.17, bf16[2,4,1,64,1024]{4,3,1,0,2:T(8,128)(2,1)S(1)} %fusion, ...), kind=kLoop, calls=%fused_computation.24 | loop fusion | flops 2097152 | bytes 8388608 | tf_op jit(solution)/shard_map/stack | solution.py:124
  197.9 2.2 all-to-all-done.9
  202.1 3.0 %collective-permute-start.8 = (bf16[512,512]{1,0:T(8,128)(2,1)S(1)}, bf16[512,512]{1,0:T(8,128)(2,1)S(1)}, u32[]{:S(2)}, u32[]{:S(2)}) collective-permute-start(bf16[512,512]{1,0:T(8,128)(2,1)S(1)} %convolution_convert_fusion), channel_id=1, source_target_pairs={{0,7},{1,2},{2,1},{3,4},{4,3},{5,6},{6,5},{7,0},{8,15},{9,10},{10,... | collective-permute-start | bytes 1572872 | tf_op jit(solution)/shard_map/ppermute | solution.py:36
  205.9 2.4 collective-permute-start.7
  208.4 11.1 %collective-permute-done.8 = bf16[512,512]{1,0:T(8,128)(2,1)S(1)} collective-permute-done((bf16[512,512]{1,0:T(8,128)(2,1)S(1)}, bf16[512,512]{1,0:T(8,128)(2,1)S(1)}, u32[]{:S(2)}, u32[]{:S(2)}) %collective-permute-start.8) | collective-permute-done | bytes 524320 | tf_op jit(solution)/shard_map/ppermute | solution.py:36
  222.5 31.2 %all_to_all.75 = bf16[8,128,512]{2,1,0:T(8,128)(2,1)S(1)} all-to-all(bf16[8,128,512]{2,1,0:T(8,128)(2,1)S(1)} %bitcast.89), channel_id=1, replica_groups={{0,4,8,12,2,6,10,14},{1,5,9,13,3,7,11,15},{16,20,24,28,18,22,26,30},{17..., dimensions={0} | all-to-all | bytes 2097152 | tf_op jit(solution)/shard_map/all_to_all | solution.py:136
  (81 shorter events, 27.5 us)
Async XLA Ops:
  0.6 11.1 %copy-start.4 = (bf16[64,1024]{1,0:T(8,128)(2,1)S(1)}, bf16[64,1024]{1,0:T(8,128)(2,1)}, u32[]{:S(2)}) copy-start(bf16[64,1024]{1,0:T(8,128)(2,1)} %param.3) | copy-start | bytes 393220
  2.8 42.5 %all-to-all-start = ((bf16[8,512,128]{1,2,0:T(8,128)(2,1)}), bf16[8,512,128]{1,2,0:T(8,128)(2,1)S(1)}, u32[]{:S(2)}, u32[]{:S(2)}) async-start(bf16[8,512,128]{1,2,0:T(8,128)(2,1)} %broadcast_in_dim.30), calls=%async_computation | async-start | bytes 2097152 | tf_op jit(solution)/shard_map/all_to_all | solution.py:42
  11.7 17.0 %collective-permute-start = (bf16[64,1024]{1,0:T(8,128)(2,1)S(1)}, bf16[64,1024]{1,0:T(8,128)(2,1)S(1)}, u32[]{:S(2)}, u32[]{:S(2)}) collective-permute-start(bf16[64,1024]{1,0:T(8,128)(2,1)S(1)} %copy-done.4), channel_id=1, source_target_pairs={{0,384},{16,400},{32,416},{48,432},{64,448},{80,464},{96,480},{112... | collective-permute-start | bytes 393224 | tf_op jit(solution)/shard_map/ppermute | solution.py:23
  21.7 23.5 %collective-permute-start.2 = (bf16[64,1024]{1,0:T(8,128)(2,1)S(1)}, bf16[64,1024]{1,0:T(8,128)(2,1)S(1)}, u32[]{:S(2)}, u32[]{:S(2)}) collective-permute-start(bf16[64,1024]{1,0:T(8,128)(2,1)S(1)} %copy-done.4), channel_id=1, source_target_pairs={{0,128},{16,144},{32,160},{48,176},{64,192},{80,208},{96,224},{112... | collective-permute-start | bytes 393224 | tf_op jit(solution)/shard_map/ppermute | solution.py:23
  23.7 21.0 %collective-permute-start.1 = (bf16[64,1024]{1,0:T(8,128)(2,1)S(1)}, bf16[64,1024]{1,0:T(8,128)(2,1)S(1)}, u32[]{:S(2)}, u32[]{:S(2)}) collective-permute-start(bf16[64,1024]{1,0:T(8,128)(2,1)S(1)} %copy-done.4), channel_id=1, source_target_pairs={{0,256},{16,272},{32,288},{48,304},{64,320},{80,336},{96,352},{112... | collective-permute-start | bytes 393224 | tf_op jit(solution)/shard_map/ppermute | solution.py:23
  46.9 28.7 %all-to-all-start.1 = ((bf16[4,4,64,1024]{3,2,1,0:T(8,128)(2,1)}), bf16[4,4,64,1024]{3,2,1,0:T(8,128)(2,1)S(1)}, u32[]{:S(2)}, u32[]{:S(2)}) async-start(bf16[4,4,64,1024]{3,2,1,0:T(8,128)(2,1)} %broadcast_in_dim.36), calls=%async_computation.1 | async-start | bytes 4194304 | tf_op jit(solution)/shard_map/all_to_all | solution.py:42
  52.7 14.9 %collective-permute-start.3 = (bf16[4,512,128]{1,2,0:T(8,128)(2,1)}, bf16[4,512,128]{1,2,0:T(8,128)(2,1)}, u32[]{:S(2)}, u32[]{:S(2)}) collective-permute-start(bf16[4,512,128]{1,2,0:T(8,128)(2,1)} %get-tuple-element.33), channel_id=1, source_target_pairs={{0,1},{1,0},{2,3},{3,2},{4,5},{5,4},{6,7},{7,6},{8,9},{9,8},{10,11... | collective-permute-start | bytes 1572872 | tf_op jit(solution)/shard_map/ppermute | solution.py:36
  54.7 16.1 %collective-permute-start.4 = (bf16[4,512,128]{1,2,0:T(8,128)(2,1)}, bf16[4,512,128]{1,2,0:T(8,128)(2,1)}, u32[]{:S(2)}, u32[]{:S(2)}) collective-permute-start(bf16[4,512,128]{1,2,0:T(8,128)(2,1)} %get-tuple-element.32), channel_id=1, source_target_pairs={{0,7},{1,2},{2,1},{3,4},{4,3},{5,6},{6,5},{7,0},{8,15},{9,10},{10,... | collective-permute-start | bytes 1572872 | tf_op jit(solution)/shard_map/ppermute | solution.py:36
  75.5 6.8 %copy-start = (bf16[4,4,64,1024]{3,2,1,0:T(8,128)(2,1)}, bf16[4,4,64,1024]{3,2,1,0:T(8,128)(2,1)S(1)}, u32[]{:S(2)}) copy-start(bf16[4,4,64,1024]{3,2,1,0:T(8,128)(2,1)S(1)} %all-to-all-done.1) | copy-start | bytes 6291460
  75.5 8.1 %collective-permute-start.5 = (bf16[4,4,64,1024]{3,2,1,0:T(8,128)(2,1)S(1)}, bf16[4,4,64,1024]{3,2,1,0:T(8,128)(2,1)}, u32[]{:S(2)}, u32[]{:S(2)}) collective-permute-start(bf16[4,4,64,1024]{3,2,1,0:T(8,128)(2,1)S(1)} %all-to-all-done.1), channel_id=1, source_target_pairs={{0,16},{16,0},{32,48},{48,32},{64,80},{80,64},{96,112},{112,96},{1... | collective-permute-start | bytes 6291464 | tf_op jit(solution)/shard_map/ppermute | solution.py:27
  79.9 3.7 %collective-permute-start.6 = (f32[1024]{0:T(1024)S(1)}, f32[1024]{0:T(1024)S(1)}, u32[]{:S(2)}, u32[]{:S(2)}) collective-permute-start(f32[1024]{0:T(1024)S(1)} %multiply_reduce_fusion), channel_id=1, source_target_pairs={{0,16},{16,0},{32,48},{48,32},{64,80},{80,64},{96,112},{112,96},{1... | collective-permute-start | bytes 12296 | tf_op jit(solution)/shard_map/ppermute | solution.py:27
  171.6 12.0 %all-to-all-start.8 = ((f32[16,1,512]{2,1,0:T(1,128)}), f32[16,1,512]{2,1,0:T(1,128)S(1)}, u32[]{:S(2)}, u32[]{:S(2)}) async-start(f32[16,1,512]{2,1,0:T(1,128)} %broadcast_in_dim.43), calls=%async_computation.8 | async-start | bytes 65536 | tf_op jit(solution)/shard_map/all_to_all | solution.py:42
  185.5 14.5 %all-to-all-start.9 = ((f32[32,1,1024]{2,1,0:T(1,128)}), f32[32,1,1024]{2,1,0:T(1,128)S(1)}, u32[]{:S(2)}, u32[]{:S(2)}) async-start(f32[32,1,1024]{2,1,0:T(1,128)} %broadcast_in_dim.44), calls=%async_computation.9 | async-start | bytes 262144 | tf_op jit(solution)/shard_map/all_to_all | solution.py:42
  200.1 1.2 copy-start.3
  201.3 3.8 %copy-start.2 = (bf16[1,4,2,64,1024]{4,3,2,1,0:T(8,128)(2,1)S(1)}, bf16[1,4,2,64,1024]{4,3,2,1,0:T(8,128)(2,1)}, u32[]{:S(2)}) copy-start(bf16[1,4,2,64,1024]{4,3,2,1,0:T(8,128)(2,1)} %copy.48) | copy-start | bytes 3145732
  202.1 6.1 %copy-start.1 = (bf16[1,4,2,64,1024]{4,3,1,0,2:T(8,128)(2,1)S(1)}, bf16[1,4,2,64,1024]{4,3,1,0,2:T(8,128)(2,1)}, u32[]{:S(2)}) copy-start(bf16[1,4,2,64,1024]{4,3,1,0,2:T(8,128)(2,1)} %get-tuple-element.43) | copy-start | bytes 3145732
  202.1 17.5 %collective-permute-start.8 = (bf16[512,512]{1,0:T(8,128)(2,1)S(1)}, bf16[512,512]{1,0:T(8,128)(2,1)S(1)}, u32[]{:S(2)}, u32[]{:S(2)}) collective-permute-start(bf16[512,512]{1,0:T(8,128)(2,1)S(1)} %convolution_convert_fusion), channel_id=1, source_target_pairs={{0,7},{1,2},{2,1},{3,4},{4,3},{5,6},{6,5},{7,0},{8,15},{9,10},{10,... | collective-permute-start | bytes 1572872 | tf_op jit(solution)/shard_map/ppermute | solution.py:36
  205.9 15.8 %collective-permute-start.7 = (bf16[512,512]{1,0:T(8,128)(2,1)S(1)}, bf16[512,512]{1,0:T(8,128)(2,1)S(1)}, u32[]{:S(2)}, u32[]{:S(2)}) collective-permute-start(bf16[512,512]{1,0:T(8,128)(2,1)S(1)} %convolution_convert_fusion.1), channel_id=1, source_target_pairs={{0,1},{1,0},{2,3},{3,2},{4,5},{5,4},{6,7},{7,6},{8,9},{9,8},{10,11... | collective-permute-start | bytes 1572872 | tf_op jit(solution)/shard_map/ppermute | solution.py:36

commit v11 on v10

--- a/solution.py
+++ b/solution.py
@@ -46,8 +46,8 @@
     z = lax.axis_index("row") // (X * CORE)
     same = share(noise, "col", PARITIES)
     plane = jnp.zeros((Z_HI,) + data.shape, data.dtype)
-    pieces = (data, along_z(data, -1), along_z(data, 2), along_z(data, 1))
-    for by, piece in enumerate(pieces):
+    for by in (2, 3, 1, 0):
+        piece = along_z(data, -by) if by else data
         plane = lax.dynamic_update_slice(plane, piece[None], ((z + by) % Z_HI, 0, 0))
     return lax.optimization_barrier((same, plane))
 

time: 258 us -> 258 us (level)
  waiting for transfers between devices: 48.5 us -> 39 us
  starting transfers between devices: 54.9 us -> 61 us
  blocking collectives: 111 us -> 114 us
    ppermute x3, waiting for transfers between devices: 16.5 us -> 10.6 us  [along_z(): return lax.ppermute(array, 'row', pairs)]
    ppermute x4, starting transfers between devices: 10.9 us -> 15.8 us  [neighbour(): return lax.ppermute(array, 'col', pairs)]
    all_to_all x6, blocking collectives: 79.6 us -> 83.4 us  [share(): return lax.all_to_all(copies, axis, 0, 0, axis_index_groups=groups)]
  transfers between devices with their start and end apart: 13 -> 13, of which waited for: 9 -> 7; matrix products, arithmetic and copies ran while one was open for 8% -> 8% of each run, Pallas kernels for 0% -> 0%
where the time goes in v11:
time: 258 us; the launch traced here: 254 us
  blocking collectives  114 us (44%)
  starting transfers between devices  61 us (24%)
  waiting for transfers between devices  39 us (15%)
  other arithmetic  18.9 us (7%)
  local copies, waits for them, and re-layouts  13 us (5%)
  matrix products  7.25 us (3%)
    all_to_all x6, blocking collectives, share(): return lax.all_to_all(copies, axis, 0, 0, axis_index_groups=groups)  83.4 us
    all_to_all x1, blocking collectives, local(): parts = lax.all_to_all(sums, 'col', 0, 0, axis_index_groups=PARITIES)  30.7 us
    all_to_all x4, starting transfers between devices, share(): return lax.all_to_all(copies, axis, 0, 0, axis_index_groups=groups)  22.9 us
    ppermute x4, waiting for transfers between devices, neighbour(): return lax.ppermute(array, 'col', pairs)  21.9 us
    ppermute x3, starting transfers between devices, along_z(): return lax.ppermute(array, 'row', pairs)  18 us
    ppermute x4, starting transfers between devices, neighbour(): return lax.ppermute(array, 'col', pairs)  15.8 us
    ppermute x3, waiting for transfers between devices, along_z(): return lax.ppermute(array, 'row', pairs)  10.6 us
    all_to_all x4, waiting for transfers between devices, share(): return lax.all_to_all(copies, axis, 0, 0, axis_index_groups=groups)  6.5 us
  transfers between devices with their start and end apart: 13, of which 7 were waited for; matrix products, arithmetic and copies ran while one was open for 8% of the time, Pallas kernels for 0%

profile of v11, /device:TPU:6, one launch (start us, length us, event | category | flops | bytes accessed | tf_op | source)
XLA Modules:
  0.0 254.5 jit_solution(3306569824879002695)
XLA Ops:
  2.8 8.9 %all-to-all-start = ((bf16[8,512,128]{1,2,0:T(8,128)(2,1)}), bf16[8,512,128]{1,2,0:T(8,128)(2,1)S(1)}, u32[]{:S(2)}, u32[]{:S(2)}) async-start(bf16[8,512,128]{1,2,0:T(8,128)(2,1)} %broadcast_in_dim.30), calls=%async_computation | async-start | bytes 2097152 | tf_op jit(solution)/shard_map/all_to_all | solution.py:42
  11.7 10.0 %collective-permute-start = (bf16[64,1024]{1,0:T(8,128)(2,1)S(1)}, bf16[64,1024]{1,0:T(8,128)(2,1)S(1)}, u32[]{:S(2)}, u32[]{:S(2)}) collective-permute-start(bf16[64,1024]{1,0:T(8,128)(2,1)S(1)} %copy-done.4), channel_id=1, source_target_pairs={{0,256},{16,272},{32,288},{48,304},{64,320},{80,336},{96,352},{112... | collective-permute-start | bytes 393224 | tf_op jit(solution)/shard_map/ppermute | solution.py:23
  21.7 4.3 %collective-permute-start.1 = (bf16[64,1024]{1,0:T(8,128)(2,1)S(1)}, bf16[64,1024]{1,0:T(8,128)(2,1)S(1)}, u32[]{:S(2)}, u32[]{:S(2)}) collective-permute-start(bf16[64,1024]{1,0:T(8,128)(2,1)S(1)} %copy-done.4), channel_id=1, source_target_pairs={{0,128},{16,144},{32,160},{48,176},{64,192},{80,208},{96,224},{112... | collective-permute-start | bytes 393224 | tf_op jit(solution)/shard_map/ppermute | solution.py:23
  26.0 3.7 %collective-permute-start.2 = (bf16[64,1024]{1,0:T(8,128)(2,1)S(1)}, bf16[64,1024]{1,0:T(8,128)(2,1)S(1)}, u32[]{:S(2)}, u32[]{:S(2)}) collective-permute-start(bf16[64,1024]{1,0:T(8,128)(2,1)S(1)} %copy-done.4), channel_id=1, source_target_pairs={{0,384},{16,400},{32,416},{48,432},{64,448},{80,464},{96,480},{112... | collective-permute-start | bytes 393224 | tf_op jit(solution)/shard_map/ppermute | solution.py:23
  29.9 10.6 %collective-permute-done.1 = bf16[64,1024]{1,0:T(8,128)(2,1)S(1)} collective-permute-done((bf16[64,1024]{1,0:T(8,128)(2,1)S(1)}, bf16[64,1024]{1,0:T(8,128)(2,1)S(1)}, u32[]{:S(2)}, u32[]{:S(2)}) %collective-permute-start.1) | collective-permute-done | bytes 131104 | tf_op jit(solution)/shard_map/ppermute | solution.py:23
  42.2 4.8 %all-to-all-start.1 = ((bf16[4,4,64,1024]{3,2,1,0:T(8,128)(2,1)}), bf16[4,4,64,1024]{3,2,1,0:T(8,128)(2,1)S(1)}, u32[]{:S(2)}, u32[]{:S(2)}) async-start(bf16[4,4,64,1024]{3,2,1,0:T(8,128)(2,1)} %broadcast_in_dim.36), calls=%async_computation.1 | async-start | bytes 4194304 | tf_op jit(solution)/shard_map/all_to_all | solution.py:42
  48.0 2.2 collective-permute-start.3
  50.2 8.3 %collective-permute-start.4 = (bf16[4,512,128]{1,2,0:T(8,128)(2,1)}, bf16[4,512,128]{1,2,0:T(8,128)(2,1)}, u32[]{:S(2)}, u32[]{:S(2)}) collective-permute-start(bf16[4,512,128]{1,2,0:T(8,128)(2,1)} %get-tuple-element.32), channel_id=1, source_target_pairs={{0,7},{1,2},{2,1},{3,4},{4,3},{5,6},{6,5},{7,0},{8,15},{9,10},{10,... | collective-permute-start | bytes 1572872 | tf_op jit(solution)/shard_map/ppermute | solution.py:36
  58.5 4.5 %collective-permute-done.3 = bf16[4,512,128]{1,2,0:T(8,128)(2,1)} collective-permute-done((bf16[4,512,128]{1,2,0:T(8,128)(2,1)}, bf16[4,512,128]{1,2,0:T(8,128)(2,1)}, u32[]{:S(2)}, u32[]{:S(2)}) %collective-permute-start.3) | collective-permute-done | bytes 524320 | tf_op jit(solution)/shard_map/ppermute | solution.py:36
  64.1 5.0 %collective-permute-done.4 = bf16[4,512,128]{1,2,0:T(8,128)(2,1)} collective-permute-done((bf16[4,512,128]{1,2,0:T(8,128)(2,1)}, bf16[4,512,128]{1,2,0:T(8,128)(2,1)}, u32[]{:S(2)}, u32[]{:S(2)}) %collective-permute-start.4) | collective-permute-done | bytes 524320 | tf_op jit(solution)/shard_map/ppermute | solution.py:36
  70.1 2.0 multiply_reduce_fusion.7
  72.1 1.9 collective-permute-start.5
  74.0 1.7 fusion.12
  76.5 2.4 collective-permute-start.6
  80.2 3.0 %subtract_reduce_fusion = (f32[512]{0:T(512)S(1)}, f32[512,1024]{1,0:T(8,128)S(1)}) fusion(f32[1024]{0:T(1024)S(1)} %broadcast_multiply_fusion, f32[512,1024]{1,0:T(8,128)S(1)} %fusion.15, bf16[512,1024]{0,1:T(8,128)(2,1)S(1)} %bitcast.94, bf16[1024,1024]{1,0:T(8,128)(2,1)} %bitcast.18), kind=kOutput, calls=%fused_computation.19 | convolution fusion | flops 1075838464 | bytes 7346176 | tf_op jit(solution)/shard_map/dot_general | solution.py:95
  83.7 16.9 %all_to_all.69 = f32[16,1,512]{2,1,0:T(1,128)S(1)} all-to-all(f32[16,1,512]{2,1,0:T(1,128)S(1)} %broadcast_in_dim.37), channel_id=1, replica_groups=mesh['row'=32,'col'=16] {'col'}, dimensions={0} | all-to-all | bytes 65536 | tf_op jit(solution)/shard_map/all_to_all | solution.py:42
  101.4 16.5 %all_to_all.70 = f32[32,1,1024]{2,1,0:T(1,128)S(1)} all-to-all(f32[32,1,1024]{2,1,0:T(1,128)S(1)} %broadcast_in_dim.38), channel_id=1, replica_groups=mesh['row'=32,'col'=16] {'row'}, dimensions={0} | all-to-all | bytes 262144 | tf_op jit(solution)/shard_map/all_to_all | solution.py:42
  118.7 11.1 %all_to_all.71 = f32[16,1,512]{2,1,0:T(1,128)S(1)} all-to-all(f32[16,1,512]{2,1,0:T(1,128)S(1)} %broadcast_in_dim.39), channel_id=1, replica_groups=mesh['row'=32,'col'=16] {'col'}, dimensions={0} | all-to-all | bytes 65536 | tf_op jit(solution)/shard_map/all_to_all | solution.py:42
  130.4 13.9 %all_to_all.72 = f32[32,1,1024]{2,1,0:T(1,128)S(1)} all-to-all(f32[32,1,1024]{2,1,0:T(1,128)S(1)} %broadcast_in_dim.40), channel_id=1, replica_groups=mesh['row'=32,'col'=16] {'row'}, dimensions={0} | all-to-all | bytes 262144 | tf_op jit(solution)/shard_map/all_to_all | solution.py:42
  145.0 11.1 %all_to_all.73 = f32[16,1,512]{2,1,0:T(1,128)S(1)} all-to-all(f32[16,1,512]{2,1,0:T(1,128)S(1)} %broadcast_in_dim.41), channel_id=1, replica_groups=mesh['row'=32,'col'=16] {'col'}, dimensions={0} | all-to-all | bytes 65536 | tf_op jit(solution)/shard_map/all_to_all | solution.py:42
  156.8 13.9 %all_to_all.74 = f32[32,1,1024]{2,1,0:T(1,128)S(1)} all-to-all(f32[32,1,1024]{2,1,0:T(1,128)S(1)} %broadcast_in_dim.42), channel_id=1, replica_groups=mesh['row'=32,'col'=16] {'row'}, dimensions={0} | all-to-all | bytes 262144 | tf_op jit(solution)/shard_map/all_to_all | solution.py:42
  172.0 3.7 %all-to-all-start.8 = ((f32[16,1,512]{2,1,0:T(1,128)}), f32[16,1,512]{2,1,0:T(1,128)S(1)}, u32[]{:S(2)}, u32[]{:S(2)}) async-start(f32[16,1,512]{2,1,0:T(1,128)} %broadcast_in_dim.43), calls=%async_computation.8 | async-start | bytes 65536 | tf_op jit(solution)/shard_map/all_to_all | solution.py:42
  175.7 4.0 %fusion.3 = (bf16[2,4,1,64,1024]{4,3,1,0,2:T(8,128)(2,1)}, bf16[2,4,1,64,1024]{4,3,1,0,2:T(8,128)(2,1)}, bf16[2,4,1,64,1024]{4,3,1,0,2:T(8,128)(2,1)}) fusion(pred[]{:T(512)S(6)} %eq.19, bf16[2,2,4,64,1024]{4,3,2,1,0:T(8,128)(2,1)} %bitcast.5, u32[]{:T(128)S(6)} %convert_element_type.41, bf16[2,2,4,64,1024]{4,3,2,1,0:T(8,128)(2,1)} %bitcast.86, ...), kind=kLoop, calls=%fused_computation.32 | loop fusion | flops 1572864 | bytes 7340041 | tf_op jit(solution)/shard_map/jit(_where)/select_n | solution.py:123
  179.7 4.3 %all-to-all-done.8 = f32[16,1,512]{2,1,0:T(1,128)S(1)} async-done(((f32[16,1,512]{2,1,0:T(1,128)}), f32[16,1,512]{2,1,0:T(1,128)S(1)}, u32[]{:S(2)}, u32[]{:S(2)}) %all-to-all-start.8) | async-done | bytes 32800 | tf_op jit(solution)/shard_map/all_to_all | solution.py:42
  185.9 5.6 %all-to-all-start.9 = ((f32[32,1,1024]{2,1,0:T(1,128)}), f32[32,1,1024]{2,1,0:T(1,128)S(1)}, u32[]{:S(2)}, u32[]{:S(2)}) async-start(f32[32,1,1024]{2,1,0:T(1,128)} %broadcast_in_dim.44), calls=%async_computation.9 | async-start | bytes 262144 | tf_op jit(solution)/shard_map/all_to_all | solution.py:42
  191.5 1.7 fusion
  193.2 2.8 %fusion.1 = (bf16[1,4,2,64,1024]{4,3,1,0,2:T(8,128)(2,1)S(1)}, bf16[1,4,2,64,1024]{4,3,1,0,2:T(8,128)(2,1)S(1)}, bf16[1,4,2,64,1024]{4,3,1,0,2:T(8,128)(2,1)}, bf16[1,4,2,64,1024]{4,3,1,0,2:T(8,128)(2,1)S(1)}) fusion(bf16[2,4,1,64,1024]{4,3,1,0,2:T(8,128)(2,1)} %get-tuple-element.17, bf16[2,4,1,64,1024]{4,3,1,0,2:T(8,128)(2,1)S(1)} %fusion, ...), kind=kLoop, calls=%fused_computation.24 | loop fusion | flops 2097152 | bytes 8388608 | tf_op jit(solution)/shard_map/stack | solution.py:124
  198.3 2.2 all-to-all-done.9
  202.5 2.9 %collective-permute-start.8 = (bf16[512,512]{1,0:T(8,128)(2,1)S(1)}, bf16[512,512]{1,0:T(8,128)(2,1)S(1)}, u32[]{:S(2)}, u32[]{:S(2)}) collective-permute-start(bf16[512,512]{1,0:T(8,128)(2,1)S(1)} %convolution_convert_fusion), channel_id=1, source_target_pairs={{0,7},{1,2},{2,1},{3,4},{4,3},{5,6},{6,5},{7,0},{8,15},{9,10},{10,... | collective-permute-start | bytes 1572872 | tf_op jit(solution)/shard_map/ppermute | solution.py:36
  206.2 2.4 collective-permute-start.7
  208.8 11.1 %collective-permute-done.8 = bf16[512,512]{1,0:T(8,128)(2,1)S(1)} collective-permute-done((bf16[512,512]{1,0:T(8,128)(2,1)S(1)}, bf16[512,512]{1,0:T(8,128)(2,1)S(1)}, u32[]{:S(2)}, u32[]{:S(2)}) %collective-permute-start.8) | collective-permute-done | bytes 524320 | tf_op jit(solution)/shard_map/ppermute | solution.py:36
  222.9 30.7 %all_to_all.75 = bf16[8,128,512]{2,1,0:T(8,128)(2,1)S(1)} all-to-all(bf16[8,128,512]{2,1,0:T(8,128)(2,1)S(1)} %bitcast.89), channel_id=1, replica_groups={{0,4,8,12,2,6,10,14},{1,5,9,13,3,7,11,15},{16,20,24,28,18,22,26,30},{17..., dimensions={0} | all-to-all | bytes 2097152 | tf_op jit(solution)/shard_map/all_to_all | solution.py:136
  (81 shorter events, 25.3 us)
Async XLA Ops:
  0.6 11.1 %copy-start.4 = (bf16[64,1024]{1,0:T(8,128)(2,1)S(1)}, bf16[64,1024]{1,0:T(8,128)(2,1)}, u32[]{:S(2)}) copy-start(bf16[64,1024]{1,0:T(8,128)(2,1)} %param.3) | copy-start | bytes 393220
  2.8 37.8 %all-to-all-start = ((bf16[8,512,128]{1,2,0:T(8,128)(2,1)}), bf16[8,512,128]{1,2,0:T(8,128)(2,1)S(1)}, u32[]{:S(2)}, u32[]{:S(2)}) async-start(bf16[8,512,128]{1,2,0:T(8,128)(2,1)} %broadcast_in_dim.30), calls=%async_computation | async-start | bytes 2097152 | tf_op jit(solution)/shard_map/all_to_all | solution.py:42
  11.7 18.1 %collective-permute-start = (bf16[64,1024]{1,0:T(8,128)(2,1)S(1)}, bf16[64,1024]{1,0:T(8,128)(2,1)S(1)}, u32[]{:S(2)}, u32[]{:S(2)}) collective-permute-start(bf16[64,1024]{1,0:T(8,128)(2,1)S(1)} %copy-done.4), channel_id=1, source_target_pairs={{0,256},{16,272},{32,288},{48,304},{64,320},{80,336},{96,352},{112... | collective-permute-start | bytes 393224 | tf_op jit(solution)/shard_map/ppermute | solution.py:23
  21.7 18.8 %collective-permute-start.1 = (bf16[64,1024]{1,0:T(8,128)(2,1)S(1)}, bf16[64,1024]{1,0:T(8,128)(2,1)S(1)}, u32[]{:S(2)}, u32[]{:S(2)}) collective-permute-start(bf16[64,1024]{1,0:T(8,128)(2,1)S(1)} %copy-done.4), channel_id=1, source_target_pairs={{0,128},{16,144},{32,160},{48,176},{64,192},{80,208},{96,224},{112... | collective-permute-start | bytes 393224 | tf_op jit(solution)/shard_map/ppermute | solution.py:23
  26.0 14.5 %collective-permute-start.2 = (bf16[64,1024]{1,0:T(8,128)(2,1)S(1)}, bf16[64,1024]{1,0:T(8,128)(2,1)S(1)}, u32[]{:S(2)}, u32[]{:S(2)}) collective-permute-start(bf16[64,1024]{1,0:T(8,128)(2,1)S(1)} %copy-done.4), channel_id=1, source_target_pairs={{0,384},{16,400},{32,416},{48,432},{64,448},{80,464},{96,480},{112... | collective-permute-start | bytes 393224 | tf_op jit(solution)/shard_map/ppermute | solution.py:23
  42.2 29.9 %all-to-all-start.1 = ((bf16[4,4,64,1024]{3,2,1,0:T(8,128)(2,1)}), bf16[4,4,64,1024]{3,2,1,0:T(8,128)(2,1)S(1)}, u32[]{:S(2)}, u32[]{:S(2)}) async-start(bf16[4,4,64,1024]{3,2,1,0:T(8,128)(2,1)} %broadcast_in_dim.36), calls=%async_computation.1 | async-start | bytes 4194304 | tf_op jit(solution)/shard_map/all_to_all | solution.py:42
  48.0 15.0 %collective-permute-start.3 = (bf16[4,512,128]{1,2,0:T(8,128)(2,1)}, bf16[4,512,128]{1,2,0:T(8,128)(2,1)}, u32[]{:S(2)}, u32[]{:S(2)}) collective-permute-start(bf16[4,512,128]{1,2,0:T(8,128)(2,1)} %get-tuple-element.33), channel_id=1, source_target_pairs={{0,1},{1,0},{2,3},{3,2},{4,5},{5,4},{6,7},{7,6},{8,9},{9,8},{10,11... | collective-permute-start | bytes 1572872 | tf_op jit(solution)/shard_map/ppermute | solution.py:36
  50.2 18.8 %collective-permute-start.4 = (bf16[4,512,128]{1,2,0:T(8,128)(2,1)}, bf16[4,512,128]{1,2,0:T(8,128)(2,1)}, u32[]{:S(2)}, u32[]{:S(2)}) collective-permute-start(bf16[4,512,128]{1,2,0:T(8,128)(2,1)} %get-tuple-element.32), channel_id=1, source_target_pairs={{0,7},{1,2},{2,1},{3,4},{4,3},{5,6},{6,5},{7,0},{8,15},{9,10},{10,... | collective-permute-start | bytes 1572872 | tf_op jit(solution)/shard_map/ppermute | solution.py:36
  72.1 6.8 %copy-start = (bf16[4,4,64,1024]{3,2,1,0:T(8,128)(2,1)}, bf16[4,4,64,1024]{3,2,1,0:T(8,128)(2,1)S(1)}, u32[]{:S(2)}) copy-start(bf16[4,4,64,1024]{3,2,1,0:T(8,128)(2,1)S(1)} %all-to-all-done.1) | copy-start | bytes 6291460
  72.1 8.1 %collective-permute-start.5 = (bf16[4,4,64,1024]{3,2,1,0:T(8,128)(2,1)S(1)}, bf16[4,4,64,1024]{3,2,1,0:T(8,128)(2,1)}, u32[]{:S(2)}, u32[]{:S(2)}) collective-permute-start(bf16[4,4,64,1024]{3,2,1,0:T(8,128)(2,1)S(1)} %all-to-all-done.1), channel_id=1, source_target_pairs={{0,16},{16,0},{32,48},{48,32},{64,80},{80,64},{96,112},{112,96},{1... | collective-permute-start | bytes 6291464 | tf_op jit(solution)/shard_map/ppermute | solution.py:27
  76.5 3.7 %collective-permute-start.6 = (f32[1024]{0:T(1024)S(1)}, f32[1024]{0:T(1024)S(1)}, u32[]{:S(2)}, u32[]{:S(2)}) collective-permute-start(f32[1024]{0:T(1024)S(1)} %multiply_reduce_fusion), channel_id=1, source_target_pairs={{0,16},{16,0},{32,48},{48,32},{64,80},{80,64},{96,112},{112,96},{1... | collective-permute-start | bytes 12296 | tf_op jit(solution)/shard_map/ppermute | solution.py:27
  172.0 12.0 %all-to-all-start.8 = ((f32[16,1,512]{2,1,0:T(1,128)}), f32[16,1,512]{2,1,0:T(1,128)S(1)}, u32[]{:S(2)}, u32[]{:S(2)}) async-start(f32[16,1,512]{2,1,0:T(1,128)} %broadcast_in_dim.43), calls=%async_computation.8 | async-start | bytes 65536 | tf_op jit(solution)/shard_map/all_to_all | solution.py:42
  185.9 14.5 %all-to-all-start.9 = ((f32[32,1,1024]{2,1,0:T(1,128)}), f32[32,1,1024]{2,1,0:T(1,128)S(1)}, u32[]{:S(2)}, u32[]{:S(2)}) async-start(f32[32,1,1024]{2,1,0:T(1,128)} %broadcast_in_dim.44), calls=%async_computation.9 | async-start | bytes 262144 | tf_op jit(solution)/shard_map/all_to_all | solution.py:42
  200.5 1.2 copy-start.3
  201.6 3.8 %copy-start.2 = (bf16[1,4,2,64,1024]{4,3,2,1,0:T(8,128)(2,1)S(1)}, bf16[1,4,2,64,1024]{4,3,2,1,0:T(8,128)(2,1)}, u32[]{:S(2)}) copy-start(bf16[1,4,2,64,1024]{4,3,2,1,0:T(8,128)(2,1)} %copy.48) | copy-start | bytes 3145732
  202.5 6.1 %copy-start.1 = (bf16[1,4,2,64,1024]{4,3,1,0,2:T(8,128)(2,1)S(1)}, bf16[1,4,2,64,1024]{4,3,1,0,2:T(8,128)(2,1)}, u32[]{:S(2)}) copy-start(bf16[1,4,2,64,1024]{4,3,1,0,2:T(8,128)(2,1)} %get-tuple-element.43) | copy-start | bytes 3145732
  202.5 17.5 %collective-permute-start.8 = (bf16[512,512]{1,0:T(8,128)(2,1)S(1)}, bf16[512,512]{1,0:T(8,128)(2,1)S(1)}, u32[]{:S(2)}, u32[]{:S(2)}) collective-permute-start(bf16[512,512]{1,0:T(8,128)(2,1)S(1)} %convolution_convert_fusion), channel_id=1, source_target_pairs={{0,7},{1,2},{2,1},{3,4},{4,3},{5,6},{6,5},{7,0},{8,15},{9,10},{10,... | collective-permute-start | bytes 1572872 | tf_op jit(solution)/shard_map/ppermute | solution.py:36
  206.2 15.8 %collective-permute-start.7 = (bf16[512,512]{1,0:T(8,128)(2,1)S(1)}, bf16[512,512]{1,0:T(8,128)(2,1)S(1)}, u32[]{:S(2)}, u32[]{:S(2)}) collective-permute-start(bf16[512,512]{1,0:T(8,128)(2,1)S(1)} %convolution_convert_fusion.1), channel_id=1, source_target_pairs={{0,1},{1,0},{2,3},{3,2},{4,5},{5,4},{6,7},{7,6},{8,9},{9,8},{10,11... | collective-permute-start | bytes 1572872 | tf_op jit(solution)/shard_map/ppermute | solution.py:36

commit v12 on v11

--- a/solution.py
+++ b/solution.py
@@ -109,12 +109,13 @@
         by_row = (lift / rows_all) / jnp.sum(share(part, "col"), axis=0)
         part = jnp.sum(plan * by_row[:, None], axis=0)
         by_col = (lift / cols_all) / jnp.sum(share(part, "row"), axis=0)
-    row_potential = noise_sq / width + EPS * (row_first + jnp.log(by_row))
-    col_potential = data_sq / width + EPS * (col_first + jnp.log(by_col))
-
     weights = (plan * ((rows_all / lift) * by_row)[:, None] * by_col[None, :]).astype(
         jnp.bfloat16
     )
+
+    weights, by_row, by_col = lax.optimization_barrier((weights, by_row, by_col))
+    row_potential = noise_sq / width + EPS * (row_first + jnp.log(by_row))
+    col_potential = data_sq / width + EPS * (col_first + jnp.log(by_col))
 
     def features(parity):
         shape = (X // 2, 2, Z_HI, -1, cols)
@@ -129,6 +130,9 @@
 
     sent = [terms(part).astype(jnp.bfloat16) for part in features(away)]
     got = [neighbour(part, by) for part, by in zip(sent, (1, -1))]
+    got, row_potential, col_potential = lax.optimization_barrier(
+        (got, row_potential, col_potential)
+    )
     sums = [
         (terms(own) + add).astype(jnp.bfloat16) for own, add in zip(features(kept), got)
     ]

time: 258 us -> 257 us (level)
  no operation moved by 1% of the time
where the time goes in v12:
time: 257 us; the launch traced here: 255 us
  blocking collectives  114 us (44%)
  starting transfers between devices  60.8 us (24%)
  waiting for transfers between devices  40 us (16%)
  other arithmetic  16.8 us (7%)
  local copies, waits for them, and re-layouts  14.9 us (6%)
  matrix products  7.32 us (3%)
    all_to_all x6, blocking collectives, share(): return lax.all_to_all(copies, axis, 0, 0, axis_index_groups=groups)  83.4 us
    all_to_all x1, blocking collectives, local(): parts = lax.all_to_all(sums, 'col', 0, 0, axis_index_groups=PARITIES)  30.6 us
    all_to_all x4, starting transfers between devices, share(): return lax.all_to_all(copies, axis, 0, 0, axis_index_groups=groups)  22.9 us
    ppermute x4, waiting for transfers between devices, neighbour(): return lax.ppermute(array, 'col', pairs)  22 us
    ppermute x3, starting transfers between devices, along_z(): return lax.ppermute(array, 'row', pairs)  18 us
    ppermute x4, starting transfers between devices, neighbour(): return lax.ppermute(array, 'col', pairs)  15.6 us
    ppermute x3, waiting for transfers between devices, along_z(): return lax.ppermute(array, 'row', pairs)  10.6 us
    all_to_all x4, waiting for transfers between devices, share(): return lax.all_to_all(copies, axis, 0, 0, axis_index_groups=groups)  7.43 us
  transfers between devices with their start and end apart: 13, of which 7 were waited for; matrix products, arithmetic and copies ran while one was open for 8% of the time, Pallas kernels for 0%

profile of v12, /device:TPU:6, one launch (start us, length us, event | category | flops | bytes accessed | tf_op | source)
XLA Modules:
  0.0 255.1 jit_solution(132932411492081800)
XLA Ops:
  2.8 8.9 %all-to-all-start = ((bf16[8,512,128]{1,2,0:T(8,128)(2,1)}), bf16[8,512,128]{1,2,0:T(8,128)(2,1)S(1)}, u32[]{:S(2)}, u32[]{:S(2)}) async-start(bf16[8,512,128]{1,2,0:T(8,128)(2,1)} %broadcast_in_dim.30), calls=%async_computation | async-start | bytes 2097152 | tf_op jit(solution)/shard_map/all_to_all | solution.py:42
  11.7 10.0 %collective-permute-start = (bf16[64,1024]{1,0:T(8,128)(2,1)S(1)}, bf16[64,1024]{1,0:T(8,128)(2,1)S(1)}, u32[]{:S(2)}, u32[]{:S(2)}) collective-permute-start(bf16[64,1024]{1,0:T(8,128)(2,1)S(1)} %copy-done.6), channel_id=1, source_target_pairs={{0,256},{16,272},{32,288},{48,304},{64,320},{80,336},{96,352},{112... | collective-permute-start | bytes 393224 | tf_op jit(solution)/shard_map/ppermute | solution.py:23
  21.7 4.3 %collective-permute-start.1 = (bf16[64,1024]{1,0:T(8,128)(2,1)S(1)}, bf16[64,1024]{1,0:T(8,128)(2,1)S(1)}, u32[]{:S(2)}, u32[]{:S(2)}) collective-permute-start(bf16[64,1024]{1,0:T(8,128)(2,1)S(1)} %copy-done.6), channel_id=1, source_target_pairs={{0,128},{16,144},{32,160},{48,176},{64,192},{80,208},{96,224},{112... | collective-permute-start | bytes 393224 | tf_op jit(solution)/shard_map/ppermute | solution.py:23
  26.0 3.7 %collective-permute-start.2 = (bf16[64,1024]{1,0:T(8,128)(2,1)S(1)}, bf16[64,1024]{1,0:T(8,128)(2,1)S(1)}, u32[]{:S(2)}, u32[]{:S(2)}) collective-permute-start(bf16[64,1024]{1,0:T(8,128)(2,1)S(1)} %copy-done.6), channel_id=1, source_target_pairs={{0,384},{16,400},{32,416},{48,432},{64,448},{80,464},{96,480},{112... | collective-permute-start | bytes 393224 | tf_op jit(solution)/shard_map/ppermute | solution.py:23
  29.9 10.6 %collective-permute-done.1 = bf16[64,1024]{1,0:T(8,128)(2,1)S(1)} collective-permute-done((bf16[64,1024]{1,0:T(8,128)(2,1)S(1)}, bf16[64,1024]{1,0:T(8,128)(2,1)S(1)}, u32[]{:S(2)}, u32[]{:S(2)}) %collective-permute-start.1) | collective-permute-done | bytes 131104 | tf_op jit(solution)/shard_map/ppermute | solution.py:23
  42.2 4.8 %all-to-all-start.1 = ((bf16[4,4,64,1024]{3,2,1,0:T(8,128)(2,1)}), bf16[4,4,64,1024]{3,2,1,0:T(8,128)(2,1)S(1)}, u32[]{:S(2)}, u32[]{:S(2)}) async-start(bf16[4,4,64,1024]{3,2,1,0:T(8,128)(2,1)} %broadcast_in_dim.36), calls=%async_computation.1 | async-start | bytes 4194304 | tf_op jit(solution)/shard_map/all_to_all | solution.py:42
  48.0 2.2 collective-permute-start.3
  50.2 8.3 %collective-permute-start.4 = (bf16[4,512,128]{1,2,0:T(8,128)(2,1)}, bf16[4,512,128]{1,2,0:T(8,128)(2,1)}, u32[]{:S(2)}, u32[]{:S(2)}) collective-permute-start(bf16[4,512,128]{1,2,0:T(8,128)(2,1)} %get-tuple-element.48), channel_id=1, source_target_pairs={{0,7},{1,2},{2,1},{3,4},{4,3},{5,6},{6,5},{7,0},{8,15},{9,10},{10,... | collective-permute-start | bytes 1572872 | tf_op jit(solution)/shard_map/ppermute | solution.py:36
  58.5 4.5 %collective-permute-done.3 = bf16[4,512,128]{1,2,0:T(8,128)(2,1)} collective-permute-done((bf16[4,512,128]{1,2,0:T(8,128)(2,1)}, bf16[4,512,128]{1,2,0:T(8,128)(2,1)}, u32[]{:S(2)}, u32[]{:S(2)}) %collective-permute-start.3) | collective-permute-done | bytes 524320 | tf_op jit(solution)/shard_map/ppermute | solution.py:36
  64.1 5.0 %collective-permute-done.4 = bf16[4,512,128]{1,2,0:T(8,128)(2,1)} collective-permute-done((bf16[4,512,128]{1,2,0:T(8,128)(2,1)}, bf16[4,512,128]{1,2,0:T(8,128)(2,1)}, u32[]{:S(2)}, u32[]{:S(2)}) %collective-permute-start.4) | collective-permute-done | bytes 524320 | tf_op jit(solution)/shard_map/ppermute | solution.py:36
  70.1 2.0 multiply_reduce_fusion.7
  72.1 1.9 collective-permute-start.5
  74.0 1.7 fusion.12
  76.5 2.4 collective-permute-start.6
  80.2 3.0 %subtract_reduce_fusion = (f32[512]{0:T(512)S(1)}, f32[512,1024]{1,0:T(8,128)S(1)}) fusion(f32[1024]{0:T(1024)S(1)} %broadcast_multiply_fusion, f32[512,1024]{1,0:T(8,128)S(1)} %fusion.15, bf16[512,1024]{0,1:T(8,128)(2,1)S(1)} %bitcast.94, bf16[1024,1024]{1,0:T(8,128)(2,1)} %bitcast.18), kind=kOutput, calls=%fused_computation.19 | convolution fusion | flops 1075838464 | bytes 7346176 | tf_op jit(solution)/shard_map/dot_general | solution.py:95
  83.7 16.9 %all_to_all.69 = f32[16,1,512]{2,1,0:T(1,128)S(1)} all-to-all(f32[16,1,512]{2,1,0:T(1,128)S(1)} %broadcast_in_dim.37), channel_id=1, replica_groups=mesh['row'=32,'col'=16] {'col'}, dimensions={0} | all-to-all | bytes 65536 | tf_op jit(solution)/shard_map/all_to_all | solution.py:42
  101.4 16.5 %all_to_all.70 = f32[32,1,1024]{2,1,0:T(1,128)S(1)} all-to-all(f32[32,1,1024]{2,1,0:T(1,128)S(1)} %broadcast_in_dim.38), channel_id=1, replica_groups=mesh['row'=32,'col'=16] {'row'}, dimensions={0} | all-to-all | bytes 262144 | tf_op jit(solution)/shard_map/all_to_all | solution.py:42
  118.7 11.1 %all_to_all.71 = f32[16,1,512]{2,1,0:T(1,128)S(1)} all-to-all(f32[16,1,512]{2,1,0:T(1,128)S(1)} %broadcast_in_dim.39), channel_id=1, replica_groups=mesh['row'=32,'col'=16] {'col'}, dimensions={0} | all-to-all | bytes 65536 | tf_op jit(solution)/shard_map/all_to_all | solution.py:42
  130.4 13.9 %all_to_all.72 = f32[32,1,1024]{2,1,0:T(1,128)S(1)} all-to-all(f32[32,1,1024]{2,1,0:T(1,128)S(1)} %broadcast_in_dim.40), channel_id=1, replica_groups=mesh['row'=32,'col'=16] {'row'}, dimensions={0} | all-to-all | bytes 262144 | tf_op jit(solution)/shard_map/all_to_all | solution.py:42
  145.0 11.1 %all_to_all.73 = f32[16,1,512]{2,1,0:T(1,128)S(1)} all-to-all(f32[16,1,512]{2,1,0:T(1,128)S(1)} %broadcast_in_dim.41), channel_id=1, replica_groups=mesh['row'=32,'col'=16] {'col'}, dimensions={0} | all-to-all | bytes 65536 | tf_op jit(solution)/shard_map/all_to_all | solution.py:42
  156.8 13.9 %all_to_all.74 = f32[32,1,1024]{2,1,0:T(1,128)S(1)} all-to-all(f32[32,1,1024]{2,1,0:T(1,128)S(1)} %broadcast_in_dim.42), channel_id=1, replica_groups=mesh['row'=32,'col'=16] {'row'}, dimensions={0} | all-to-all | bytes 262144 | tf_op jit(solution)/shard_map/all_to_all | solution.py:42
  172.0 3.7 %all-to-all-start.8 = ((f32[16,1,512]{2,1,0:T(1,128)}), f32[16,1,512]{2,1,0:T(1,128)S(1)}, u32[]{:S(2)}, u32[]{:S(2)}) async-start(f32[16,1,512]{2,1,0:T(1,128)} %broadcast_in_dim.43), calls=%async_computation.8 | async-start | bytes 65536 | tf_op jit(solution)/shard_map/all_to_all | solution.py:42
  175.7 3.8 %fusion.3 = (bf16[2,4,1,64,1024]{4,3,1,0,2:T(8,128)(2,1)S(1)}, bf16[2,4,1,64,1024]{4,3,1,0,2:T(8,128)(2,1)}, bf16[2,4,1,64,1024]{4,3,1,0,2:T(8,128)(2,1)}) fusion(pred[]{:T(512)S(6)} %eq.19, bf16[2,2,4,64,1024]{4,3,2,1,0:T(8,128)(2,1)} %bitcast.5, u32[]{:T(128)S(6)} %convert_element_type.41, bf16[2,2,4,64,1024]{4,3,2,1,0:T(8,128)(2,1)} %bitcast.86, ...), kind=kLoop, calls=%fused_computation.32 | loop fusion | flops 1572864 | bytes 7340041 | tf_op jit(solution)/shard_map/jit(_where)/select_n | solution.py:124
  179.5 4.6 %all-to-all-done.8 = f32[16,1,512]{2,1,0:T(1,128)S(1)} async-done(((f32[16,1,512]{2,1,0:T(1,128)}), f32[16,1,512]{2,1,0:T(1,128)S(1)}, u32[]{:S(2)}, u32[]{:S(2)}) %all-to-all-start.8) | async-done | bytes 32800 | tf_op jit(solution)/shard_map/all_to_all | solution.py:42
  185.3 5.6 %all-to-all-start.9 = ((f32[32,1,1024]{2,1,0:T(1,128)}), f32[32,1,1024]{2,1,0:T(1,128)S(1)}, u32[]{:S(2)}, u32[]{:S(2)}) async-start(f32[32,1,1024]{2,1,0:T(1,128)} %broadcast_in_dim.44), calls=%async_computation.9 | async-start | bytes 262144 | tf_op jit(solution)/shard_map/all_to_all | solution.py:42
  191.0 1.8 fusion
  197.0 2.9 %all-to-all-done.9 = f32[32,1,1024]{2,1,0:T(1,128)S(1)} async-done(((f32[32,1,1024]{2,1,0:T(1,128)}), f32[32,1,1024]{2,1,0:T(1,128)S(1)}, u32[]{:S(2)}, u32[]{:S(2)}) %all-to-all-start.9) | async-done | bytes 131104 | tf_op jit(solution)/shard_map/all_to_all | solution.py:42
  202.7 2.7 %collective-permute-start.7 = (bf16[512,512]{1,0:T(8,128)(2,1)S(1)}, bf16[512,512]{1,0:T(8,128)(2,1)S(1)}, u32[]{:S(2)}, u32[]{:S(2)}) collective-permute-start(bf16[512,512]{1,0:T(8,128)(2,1)S(1)} %convolution_convert_fusion.1), channel_id=1, source_target_pairs={{0,1},{1,0},{2,3},{3,2},{4,5},{5,4},{6,7},{7,6},{8,9},{9,8},{10,11... | collective-permute-start | bytes 1572872 | tf_op jit(solution)/shard_map/ppermute | solution.py:36
  206.2 2.5 collective-permute-start.8
  210.7 8.1 %collective-permute-done.7 = bf16[512,512]{1,0:T(8,128)(2,1)S(1)} collective-permute-done((bf16[512,512]{1,0:T(8,128)(2,1)S(1)}, bf16[512,512]{1,0:T(8,128)(2,1)S(1)}, u32[]{:S(2)}, u32[]{:S(2)}) %collective-permute-start.7) | collective-permute-done | bytes 524320 | tf_op jit(solution)/shard_map/ppermute | solution.py:36
  218.8 4.4 %collective-permute-done.8 = bf16[512,512]{1,0:T(8,128)(2,1)S(1)} collective-permute-done((bf16[512,512]{1,0:T(8,128)(2,1)S(1)}, bf16[512,512]{1,0:T(8,128)(2,1)S(1)}, u32[]{:S(2)}, u32[]{:S(2)}) %collective-permute-start.8) | collective-permute-done | bytes 524320 | tf_op jit(solution)/shard_map/ppermute | solution.py:36
  223.7 30.6 %all_to_all.75 = bf16[8,128,512]{2,1,0:T(8,128)(2,1)S(1)} all-to-all(bf16[8,128,512]{2,1,0:T(8,128)(2,1)S(1)} %bitcast.89), channel_id=1, replica_groups={{0,4,8,12,2,6,10,14},{1,5,9,13,3,7,11,15},{16,20,24,28,18,22,26,30},{17..., dimensions={0} | all-to-all | bytes 2097152 | tf_op jit(solution)/shard_map/all_to_all | solution.py:140
  (90 shorter events, 26.8 us)
Async XLA Ops:
  0.6 11.1 %copy-start.6 = (bf16[64,1024]{1,0:T(8,128)(2,1)S(1)}, bf16[64,1024]{1,0:T(8,128)(2,1)}, u32[]{:S(2)}) copy-start(bf16[64,1024]{1,0:T(8,128)(2,1)} %param.3) | copy-start | bytes 393220
  2.8 37.8 %all-to-all-start = ((bf16[8,512,128]{1,2,0:T(8,128)(2,1)}), bf16[8,512,128]{1,2,0:T(8,128)(2,1)S(1)}, u32[]{:S(2)}, u32[]{:S(2)}) async-start(bf16[8,512,128]{1,2,0:T(8,128)(2,1)} %broadcast_in_dim.30), calls=%async_computation | async-start | bytes 2097152 | tf_op jit(solution)/shard_map/all_to_all | solution.py:42
  11.7 18.1 %collective-permute-start = (bf16[64,1024]{1,0:T(8,128)(2,1)S(1)}, bf16[64,1024]{1,0:T(8,128)(2,1)S(1)}, u32[]{:S(2)}, u32[]{:S(2)}) collective-permute-start(bf16[64,1024]{1,0:T(8,128)(2,1)S(1)} %copy-done.6), channel_id=1, source_target_pairs={{0,256},{16,272},{32,288},{48,304},{64,320},{80,336},{96,352},{112... | collective-permute-start | bytes 393224 | tf_op jit(solution)/shard_map/ppermute | solution.py:23
  21.7 18.8 %collective-permute-start.1 = (bf16[64,1024]{1,0:T(8,128)(2,1)S(1)}, bf16[64,1024]{1,0:T(8,128)(2,1)S(1)}, u32[]{:S(2)}, u32[]{:S(2)}) collective-permute-start(bf16[64,1024]{1,0:T(8,128)(2,1)S(1)} %copy-done.6), channel_id=1, source_target_pairs={{0,128},{16,144},{32,160},{48,176},{64,192},{80,208},{96,224},{112... | collective-permute-start | bytes 393224 | tf_op jit(solution)/shard_map/ppermute | solution.py:23
  26.0 14.5 %collective-permute-start.2 = (bf16[64,1024]{1,0:T(8,128)(2,1)S(1)}, bf16[64,1024]{1,0:T(8,128)(2,1)S(1)}, u32[]{:S(2)}, u32[]{:S(2)}) collective-permute-start(bf16[64,1024]{1,0:T(8,128)(2,1)S(1)} %copy-done.6), channel_id=1, source_target_pairs={{0,384},{16,400},{32,416},{48,432},{64,448},{80,464},{96,480},{112... | collective-permute-start | bytes 393224 | tf_op jit(solution)/shard_map/ppermute | solution.py:23
  42.2 29.9 %all-to-all-start.1 = ((bf16[4,4,64,1024]{3,2,1,0:T(8,128)(2,1)}), bf16[4,4,64,1024]{3,2,1,0:T(8,128)(2,1)S(1)}, u32[]{:S(2)}, u32[]{:S(2)}) async-start(bf16[4,4,64,1024]{3,2,1,0:T(8,128)(2,1)} %broadcast_in_dim.36), calls=%async_computation.1 | async-start | bytes 4194304 | tf_op jit(solution)/shard_map/all_to_all | solution.py:42
  48.0 15.0 %collective-permute-start.3 = (bf16[4,512,128]{1,2,0:T(8,128)(2,1)}, bf16[4,512,128]{1,2,0:T(8,128)(2,1)}, u32[]{:S(2)}, u32[]{:S(2)}) collective-permute-start(bf16[4,512,128]{1,2,0:T(8,128)(2,1)} %get-tuple-element.49), channel_id=1, source_target_pairs={{0,1},{1,0},{2,3},{3,2},{4,5},{5,4},{6,7},{7,6},{8,9},{9,8},{10,11... | collective-permute-start | bytes 1572872 | tf_op jit(solution)/shard_map/ppermute | solution.py:36
  50.2 18.8 %collective-permute-start.4 = (bf16[4,512,128]{1,2,0:T(8,128)(2,1)}, bf16[4,512,128]{1,2,0:T(8,128)(2,1)}, u32[]{:S(2)}, u32[]{:S(2)}) collective-permute-start(bf16[4,512,128]{1,2,0:T(8,128)(2,1)} %get-tuple-element.48), channel_id=1, source_target_pairs={{0,7},{1,2},{2,1},{3,4},{4,3},{5,6},{6,5},{7,0},{8,15},{9,10},{10,... | collective-permute-start | bytes 1572872 | tf_op jit(solution)/shard_map/ppermute | solution.py:36
  72.1 6.8 %copy-start = (bf16[4,4,64,1024]{3,2,1,0:T(8,128)(2,1)}, bf16[4,4,64,1024]{3,2,1,0:T(8,128)(2,1)S(1)}, u32[]{:S(2)}) copy-start(bf16[4,4,64,1024]{3,2,1,0:T(8,128)(2,1)S(1)} %all-to-all-done.1) | copy-start | bytes 6291460
  72.1 8.1 %collective-permute-start.5 = (bf16[4,4,64,1024]{3,2,1,0:T(8,128)(2,1)S(1)}, bf16[4,4,64,1024]{3,2,1,0:T(8,128)(2,1)}, u32[]{:S(2)}, u32[]{:S(2)}) collective-permute-start(bf16[4,4,64,1024]{3,2,1,0:T(8,128)(2,1)S(1)} %all-to-all-done.1), channel_id=1, source_target_pairs={{0,16},{16,0},{32,48},{48,32},{64,80},{80,64},{96,112},{112,96},{1... | collective-permute-start | bytes 6291464 | tf_op jit(solution)/shard_map/ppermute | solution.py:27
  76.5 3.7 %collective-permute-start.6 = (f32[1024]{0:T(1024)S(1)}, f32[1024]{0:T(1024)S(1)}, u32[]{:S(2)}, u32[]{:S(2)}) collective-permute-start(f32[1024]{0:T(1024)S(1)} %multiply_reduce_fusion), channel_id=1, source_target_pairs={{0,16},{16,0},{32,48},{48,32},{64,80},{80,64},{96,112},{112,96},{1... | collective-permute-start | bytes 12296 | tf_op jit(solution)/shard_map/ppermute | solution.py:27
  172.0 12.0 %all-to-all-start.8 = ((f32[16,1,512]{2,1,0:T(1,128)}), f32[16,1,512]{2,1,0:T(1,128)S(1)}, u32[]{:S(2)}, u32[]{:S(2)}) async-start(f32[16,1,512]{2,1,0:T(1,128)} %broadcast_in_dim.43), calls=%async_computation.8 | async-start | bytes 65536 | tf_op jit(solution)/shard_map/all_to_all | solution.py:42
  185.3 14.5 %all-to-all-start.9 = ((f32[32,1,1024]{2,1,0:T(1,128)}), f32[32,1,1024]{2,1,0:T(1,128)S(1)}, u32[]{:S(2)}, u32[]{:S(2)}) async-start(f32[32,1,1024]{2,1,0:T(1,128)} %broadcast_in_dim.44), calls=%async_computation.9 | async-start | bytes 262144 | tf_op jit(solution)/shard_map/all_to_all | solution.py:42
  190.9 1.9 copy-start.1
  190.9 2.2 copy-start.2
  199.9 1.2 copy-start.4
  200.5 1.4 copy-start.5
  201.9 3.5 %copy-start.3 = (bf16[1,4,2,64,1024]{4,3,2,1,0:T(8,128)(2,1)S(1)}, bf16[1,4,2,64,1024]{4,3,2,1,0:T(8,128)(2,1)}, u32[]{:S(2)}) copy-start(bf16[1,4,2,64,1024]{4,3,2,1,0:T(8,128)(2,1)} %copy.49) | copy-start | bytes 3145732
  202.7 16.1 %collective-permute-start.7 = (bf16[512,512]{1,0:T(8,128)(2,1)S(1)}, bf16[512,512]{1,0:T(8,128)(2,1)S(1)}, u32[]{:S(2)}, u32[]{:S(2)}) collective-permute-start(bf16[512,512]{1,0:T(8,128)(2,1)S(1)} %convolution_convert_fusion.1), channel_id=1, source_target_pairs={{0,1},{1,0},{2,3},{3,2},{4,5},{5,4},{6,7},{7,6},{8,9},{9,8},{10,11... | collective-permute-start | bytes 1572872 | tf_op jit(solution)/shard_map/ppermute | solution.py:36
  206.2 17.0 %collective-permute-start.8 = (bf16[512,512]{1,0:T(8,128)(2,1)S(1)}, bf16[512,512]{1,0:T(8,128)(2,1)S(1)}, u32[]{:S(2)}, u32[]{:S(2)}) collective-permute-start(bf16[512,512]{1,0:T(8,128)(2,1)S(1)} %convolution_convert_fusion), channel_id=1, source_target_pairs={{0,7},{1,2},{2,1},{3,4},{4,3},{5,6},{6,5},{7,0},{8,15},{9,10},{10,... | collective-permute-start | bytes 1572872 | tf_op jit(solution)/shard_map/ppermute | solution.py:36
